TPU v7x, 32 devices: a whole 2x2x4 slice. The times are simulated.
32 devices in a mesh: parts: 2 (over y), blk: 16 (over z, x, core).
Axes of the slice: x: 2, y: 2, z: 4, core: 2. Of those that a mesh axis runs over, the one named last changes fastest.
Arguments:
- student: bfloat16 [6144, 3584], P(('parts', 'blk')), parts along dimension 0, may hold values from -6 to 6, as said below
- teacher: bfloat16 [6144, 3584], P(('parts', 'blk')), parts along dimension 0, may hold values from -6 to 6, as said below
Outputs:
- grad: bfloat16 [6144, 3584], P(('parts', 'blk')), parts along dimension 0
- row_loss: float32 [6144], P(('parts', 'blk')), parts along dimension 0
There are 2 independent parts, one for each index of `parts`. A program takes and returns all parts, laid end to end along the dimension named above; each array names one. Nothing has to cross between parts.
Inputs may be any that keep to these rules, and one draw needn't show every extreme that they name: `student`: hidden states of one token per row. `teacher`: hidden states of one token per row.
All inputs are finite; a program needn't handle non-finite values.
Results may differ from a plain program's by a relative error of at most 0.0047.
Values may be sent and summed in bfloat16 or wider, within the bound.
No kernel may reach another device: no remote copies, remote signals or barrier semaphores. Data moves between devices by JAX's collectives and lax.ppermute only.
A program may use at most 64 MiB of HBM per device.

v0:
```python
import math

import jax
import jax.numpy as jnp
from jax import lax
from jax.sharding import PartitionSpec as P

REACH = 4


def from_behind(block, axis, distance):
    devices = range(lax.axis_size(axis))
    route = [(i - distance, i) for i in devices if i - distance in devices]
    return lax.ppermute(block, axis, route)


def relation_gap(own_student, own_teacher, other_student, other_teacher, scale):
    dims = (((1,), (1,)), ((), ()))
    student_gram = lax.dot_general(
        own_student, other_student, dims, preferred_element_type=jnp.float32
    )
    teacher_gram = lax.dot_general(
        own_teacher, other_teacher, dims, preferred_element_type=jnp.float32
    )
    return (student_gram - teacher_gram) * scale


def body(student, teacher):
    rows, width = student.shape
    window = (2 * REACH + 1) * rows
    scale = 1.0 / math.sqrt(width)

    def absorb(grad_acc, row_acc, other_student, other_teacher):
        gap = relation_gap(student, teacher, other_student, other_teacher, scale)
        gap_b = gap.astype(jnp.bfloat16)
        grad_acc = grad_acc + jnp.dot(gap_b, other_student, preferred_element_type=jnp.float32)
        row_acc = row_acc + jnp.sum(gap * gap, axis=1)
        return (grad_acc, row_acc, gap, gap_b)

    grad_sum, row_sum, unused_gap, unused_gap_b = absorb(
        jnp.zeros((rows, width), jnp.float32), jnp.zeros((rows,), jnp.float32), student, teacher
    )
    for distance in range(1, REACH + 1):
        lower_student, lower_teacher = from_behind((student, teacher), "blk", distance)
        grad_sum, row_sum, unused_gap, unused_gap_b = absorb(
            grad_sum, row_sum, lower_student, lower_teacher
        )
        upper_student, upper_teacher = from_behind((student, teacher), "blk", -distance)
        grad_sum, row_sum, unused_gap, unused_gap_b = absorb(
            grad_sum, row_sum, upper_student, upper_teacher
        )
    grad = (grad_sum / math.sqrt(window)).astype(jnp.bfloat16)
    row_loss = row_sum / window
    return (grad, row_loss)


def solution(mesh):
    return jax.shard_map(
        body,
        mesh=mesh,
        in_specs=(P(("parts", "blk"), None), P(("parts", "blk"), None)),
        out_specs=(P(("parts", "blk"), None), P(("parts", "blk"))),
        check_vma=False,
    )
```

profile of v0, /device:TPU:0, one launch (start us, length us, event | category | flops | bytes accessed | tf_op | source)
XLA Modules:
  0.0 262.5 jit_solution(11109355242896306506)
XLA Ops:
  0.6 2.6 collective-permute-start.1
  3.2 4.5 %collective-permute-start = (bf16[192,3584]{1,0:T(8,128)(2,1)}, bf16[192,3584]{1,0:T(8,128)(2,1)S(1)}, u32[]{:S(2)}, u32[]{:S(2)}) collective-permute-start(bf16[192,3584]{1,0:T(8,128)(2,1)} %param.2), channel_id=1, source_target_pairs={{0,1},{1,2},{2,3},{3,4},{4,5},{5,6},{6,7},{7,8},{8,9},{9,10},{10,1... | collective-permute-start | bytes 4128776 | tf_op jit(solution)/shard_map/ppermute | solution.py:14
  7.7 3.5 %collective-permute-start.12 = (bf16[192,3584]{1,0:T(8,128)(2,1)}, bf16[192,3584]{1,0:T(8,128)(2,1)S(1)}, u32[]{:S(2)}, u32[]{:S(2)}) collective-permute-start(bf16[192,3584]{1,0:T(8,128)(2,1)} %param.2), channel_id=1, source_target_pairs={{0,4},{1,5},{2,6},{3,7},{4,8},{5,9},{6,10},{7,11},{8,12},{9,13},{1... | collective-permute-start | bytes 4128776 | tf_op jit(solution)/shard_map/ppermute | solution.py:14
  11.2 3.5 %collective-permute-start.13 = (bf16[192,3584]{1,0:T(8,128)(2,1)}, bf16[192,3584]{1,0:T(8,128)(2,1)S(1)}, u32[]{:S(2)}, u32[]{:S(2)}) collective-permute-start(bf16[192,3584]{1,0:T(8,128)(2,1)} %param.3), channel_id=1, source_target_pairs={{0,4},{1,5},{2,6},{3,7},{4,8},{5,9},{6,10},{7,11},{8,12},{9,13},{1... | collective-permute-start | bytes 4128776 | tf_op jit(solution)/shard_map/ppermute | solution.py:14
  14.7 1.3 collective-permute-start.11
  16.0 2.4 fusion.33
  19.0 0.8 copy-done.1
  20.3 1.3 collective-permute-start.10
  22.2 40.3 %collective-permute-start.9 = (bf16[192,3584]{1,0:T(8,128)(2,1)S(1)}, bf16[192,3584]{1,0:T(8,128)(2,1)S(1)}, u32[]{:S(2)}, u32[]{:S(2)}) collective-permute-start(bf16[192,3584]{1,0:T(8,128)(2,1)S(1)} %copy-done), channel_id=1, source_target_pairs={{0,3},{1,4},{2,5},{3,6},{4,7},{5,8},{6,9},{7,10},{8,11},{9,12},{10... | collective-permute-start | bytes 4128776 | tf_op jit(solution)/shard_map/ppermute | solution.py:14
  63.1 8.5 %collective-permute-done.13 = bf16[192,3584]{1,0:T(8,128)(2,1)S(1)} collective-permute-done((bf16[192,3584]{1,0:T(8,128)(2,1)}, bf16[192,3584]{1,0:T(8,128)(2,1)S(1)}, u32[]{:S(2)}, u32[]{:S(2)}) %collective-permute-start.13) | collective-permute-done | bytes 1376288 | tf_op jit(solution)/shard_map/ppermute | solution.py:14
  71.5 1.3 collective-permute-start.7
  73.4 4.6 %collective-permute-start.5 = (bf16[192,3584]{1,0:T(8,128)(2,1)S(1)}, bf16[192,3584]{1,0:T(8,128)(2,1)S(1)}, u32[]{:S(2)}, u32[]{:S(2)}) collective-permute-start(bf16[192,3584]{1,0:T(8,128)(2,1)S(1)} %copy-done), channel_id=1, source_target_pairs={{0,2},{1,3},{2,4},{3,5},{4,6},{5,7},{6,8},{7,9},{8,10},{9,11},{10,... | collective-permute-start | bytes 4128776 | tf_op jit(solution)/shard_map/ppermute | solution.py:14
  78.6 1.3 collective-permute-start.15
  80.4 1.3 collective-permute-start.3
  82.3 18.3 %collective-permute-done.9 = bf16[192,3584]{1,0:T(8,128)(2,1)S(1)} collective-permute-done((bf16[192,3584]{1,0:T(8,128)(2,1)S(1)}, bf16[192,3584]{1,0:T(8,128)(2,1)S(1)}, u32[]{:S(2)}, u32[]{:S(2)}) %collective-permute-start.9) | collective-permute-done | bytes 1376288 | tf_op jit(solution)/shard_map/ppermute | solution.py:14
  100.6 46.5 %collective-permute-start.8 = (bf16[192,3584]{1,0:T(8,128)(2,1)S(1)}, bf16[192,3584]{1,0:T(8,128)(2,1)S(1)}, u32[]{:S(2)}, u32[]{:S(2)}) collective-permute-start(bf16[192,3584]{1,0:T(8,128)(2,1)S(1)} %copy-done.1), channel_id=1, source_target_pairs={{0,3},{1,4},{2,5},{3,6},{4,7},{5,8},{6,9},{7,10},{8,11},{9,12},{10... | collective-permute-start | bytes 4128776 | tf_op jit(solution)/shard_map/ppermute | solution.py:14
  147.7 1.3 collective-permute-start.6
  149.6 4.6 %collective-permute-start.4 = (bf16[192,3584]{1,0:T(8,128)(2,1)S(1)}, bf16[192,3584]{1,0:T(8,128)(2,1)S(1)}, u32[]{:S(2)}, u32[]{:S(2)}) collective-permute-start(bf16[192,3584]{1,0:T(8,128)(2,1)S(1)} %copy-done.1), channel_id=1, source_target_pairs={{0,2},{1,3},{2,4},{3,5},{4,6},{5,7},{6,8},{7,9},{8,10},{9,11},{10,... | collective-permute-start | bytes 4128776 | tf_op jit(solution)/shard_map/ppermute | solution.py:14
  154.7 1.3 collective-permute-start.14
  156.6 1.5 collective-permute-start.2
  158.6 37.9 %collective-permute-done.8 = bf16[192,3584]{1,0:T(8,128)(2,1)S(1)} collective-permute-done((bf16[192,3584]{1,0:T(8,128)(2,1)S(1)}, bf16[192,3584]{1,0:T(8,128)(2,1)S(1)}, u32[]{:S(2)}, u32[]{:S(2)}) %collective-permute-start.8) | collective-permute-done | bytes 1376288 | tf_op jit(solution)/shard_map/ppermute | solution.py:14
  197.6 56.4 %collective-permute-done.4 = bf16[192,3584]{1,0:T(8,128)(2,1)S(1)} collective-permute-done((bf16[192,3584]{1,0:T(8,128)(2,1)S(1)}, bf16[192,3584]{1,0:T(8,128)(2,1)S(1)}, u32[]{:S(2)}, u32[]{:S(2)}) %collective-permute-start.4) | collective-permute-done | bytes 1376288 | tf_op jit(solution)/shard_map/ppermute | solution.py:14
  255.7 0.6 add_multiply_fusion
  260.1 2.4 fusion.7
  (40 shorter events, 13.6 us)
Async XLA Ops:
  0.6 17.8 %copy-start = (bf16[192,3584]{1,0:T(8,128)(2,1)S(1)}, bf16[192,3584]{1,0:T(8,128)(2,1)}, u32[]{:S(2)}) copy-start(bf16[192,3584]{1,0:T(8,128)(2,1)} %param.3) | copy-start | bytes 4128772
  0.6 19.7 %collective-permute-start.1 = (bf16[192,3584]{1,0:T(8,128)(2,1)}, bf16[192,3584]{1,0:T(8,128)(2,1)S(1)}, u32[]{:S(2)}, u32[]{:S(2)}) collective-permute-start(bf16[192,3584]{1,0:T(8,128)(2,1)} %param.3), channel_id=1, source_target_pairs={{0,1},{1,2},{2,3},{3,4},{4,5},{5,6},{6,7},{7,8},{8,9},{9,10},{10,1... | collective-permute-start | bytes 4128776 | tf_op jit(solution)/shard_map/ppermute | solution.py:14
  3.2 18.9 %collective-permute-start = (bf16[192,3584]{1,0:T(8,128)(2,1)}, bf16[192,3584]{1,0:T(8,128)(2,1)S(1)}, u32[]{:S(2)}, u32[]{:S(2)}) collective-permute-start(bf16[192,3584]{1,0:T(8,128)(2,1)} %param.2), channel_id=1, source_target_pairs={{0,1},{1,2},{2,3},{3,4},{4,5},{5,6},{6,7},{7,8},{8,9},{9,10},{10,1... | collective-permute-start | bytes 4128776 | tf_op jit(solution)/shard_map/ppermute | solution.py:14
  7.7 65.6 %collective-permute-start.12 = (bf16[192,3584]{1,0:T(8,128)(2,1)}, bf16[192,3584]{1,0:T(8,128)(2,1)S(1)}, u32[]{:S(2)}, u32[]{:S(2)}) collective-permute-start(bf16[192,3584]{1,0:T(8,128)(2,1)} %param.2), channel_id=1, source_target_pairs={{0,4},{1,5},{2,6},{3,7},{4,8},{5,9},{6,10},{7,11},{8,12},{9,13},{1... | collective-permute-start | bytes 4128776 | tf_op jit(solution)/shard_map/ppermute | solution.py:14
  11.2 60.3 %collective-permute-start.13 = (bf16[192,3584]{1,0:T(8,128)(2,1)}, bf16[192,3584]{1,0:T(8,128)(2,1)S(1)}, u32[]{:S(2)}, u32[]{:S(2)}) collective-permute-start(bf16[192,3584]{1,0:T(8,128)(2,1)} %param.3), channel_id=1, source_target_pairs={{0,4},{1,5},{2,6},{3,7},{4,8},{5,9},{6,10},{7,11},{8,12},{9,13},{1... | collective-permute-start | bytes 4128776 | tf_op jit(solution)/shard_map/ppermute | solution.py:14
  14.7 63.8 %collective-permute-start.11 = (bf16[192,3584]{1,0:T(8,128)(2,1)}, bf16[192,3584]{1,0:T(8,128)(2,1)S(1)}, u32[]{:S(2)}, u32[]{:S(2)}) collective-permute-start(bf16[192,3584]{1,0:T(8,128)(2,1)} %param.3), channel_id=1, source_target_pairs={{3,0},{4,1},{5,2},{6,3},{7,4},{8,5},{9,6},{10,7},{11,8},{12,9},{13... | collective-permute-start | bytes 4128776 | tf_op jit(solution)/shard_map/ppermute | solution.py:14
  18.4 1.3 copy-start.1
  20.3 60.1 %collective-permute-start.10 = (bf16[192,3584]{1,0:T(8,128)(2,1)S(1)}, bf16[192,3584]{1,0:T(8,128)(2,1)S(1)}, u32[]{:S(2)}, u32[]{:S(2)}) collective-permute-start(bf16[192,3584]{1,0:T(8,128)(2,1)S(1)} %copy-done.1), channel_id=1, source_target_pairs={{3,0},{4,1},{5,2},{6,3},{7,4},{8,5},{9,6},{10,7},{11,8},{12,9},{13... | collective-permute-start | bytes 4128776 | tf_op jit(solution)/shard_map/ppermute | solution.py:14
  22.2 78.4 %collective-permute-start.9 = (bf16[192,3584]{1,0:T(8,128)(2,1)S(1)}, bf16[192,3584]{1,0:T(8,128)(2,1)S(1)}, u32[]{:S(2)}, u32[]{:S(2)}) collective-permute-start(bf16[192,3584]{1,0:T(8,128)(2,1)S(1)} %copy-done), channel_id=1, source_target_pairs={{0,3},{1,4},{2,5},{3,6},{4,7},{5,8},{6,9},{7,10},{8,11},{9,12},{10... | collective-permute-start | bytes 4128776 | tf_op jit(solution)/shard_map/ppermute | solution.py:14
  71.5 76.2 %collective-permute-start.7 = (bf16[192,3584]{1,0:T(8,128)(2,1)S(1)}, bf16[192,3584]{1,0:T(8,128)(2,1)S(1)}, u32[]{:S(2)}, u32[]{:S(2)}) collective-permute-start(bf16[192,3584]{1,0:T(8,128)(2,1)S(1)} %copy-done), channel_id=1, source_target_pairs={{2,0},{3,1},{4,2},{5,3},{6,4},{7,5},{8,6},{9,7},{10,8},{11,9},{12,... | collective-permute-start | bytes 4128776 | tf_op jit(solution)/shard_map/ppermute | solution.py:14
  73.4 76.2 %collective-permute-start.5 = (bf16[192,3584]{1,0:T(8,128)(2,1)S(1)}, bf16[192,3584]{1,0:T(8,128)(2,1)S(1)}, u32[]{:S(2)}, u32[]{:S(2)}) collective-permute-start(bf16[192,3584]{1,0:T(8,128)(2,1)S(1)} %copy-done), channel_id=1, source_target_pairs={{0,2},{1,3},{2,4},{3,5},{4,6},{5,7},{6,8},{7,9},{8,10},{9,11},{10,... | collective-permute-start | bytes 4128776 | tf_op jit(solution)/shard_map/ppermute | solution.py:14
  78.6 76.2 %collective-permute-start.15 = (bf16[192,3584]{1,0:T(8,128)(2,1)S(1)}, bf16[192,3584]{1,0:T(8,128)(2,1)S(1)}, u32[]{:S(2)}, u32[]{:S(2)}) collective-permute-start(bf16[192,3584]{1,0:T(8,128)(2,1)S(1)} %copy-done), channel_id=1, source_target_pairs={{4,0},{5,1},{6,2},{7,3},{8,4},{9,5},{10,6},{11,7},{12,8},{13,9},{1... | collective-permute-start | bytes 4128776 | tf_op jit(solution)/shard_map/ppermute | solution.py:14
  80.4 76.2 %collective-permute-start.3 = (bf16[192,3584]{1,0:T(8,128)(2,1)S(1)}, bf16[192,3584]{1,0:T(8,128)(2,1)S(1)}, u32[]{:S(2)}, u32[]{:S(2)}) collective-permute-start(bf16[192,3584]{1,0:T(8,128)(2,1)S(1)} %copy-done), channel_id=1, source_target_pairs={{1,0},{2,1},{3,2},{4,3},{5,4},{6,5},{7,6},{8,7},{9,8},{10,9},{11,1... | collective-permute-start | bytes 4128776 | tf_op jit(solution)/shard_map/ppermute | solution.py:14
  100.6 95.9 %collective-permute-start.8 = (bf16[192,3584]{1,0:T(8,128)(2,1)S(1)}, bf16[192,3584]{1,0:T(8,128)(2,1)S(1)}, u32[]{:S(2)}, u32[]{:S(2)}) collective-permute-start(bf16[192,3584]{1,0:T(8,128)(2,1)S(1)} %copy-done.1), channel_id=1, source_target_pairs={{0,3},{1,4},{2,5},{3,6},{4,7},{5,8},{6,9},{7,10},{8,11},{9,12},{10... | collective-permute-start | bytes 4128776 | tf_op jit(solution)/shard_map/ppermute | solution.py:14
  147.7 49.4 %collective-permute-start.6 = (bf16[192,3584]{1,0:T(8,128)(2,1)S(1)}, bf16[192,3584]{1,0:T(8,128)(2,1)S(1)}, u32[]{:S(2)}, u32[]{:S(2)}) collective-permute-start(bf16[192,3584]{1,0:T(8,128)(2,1)S(1)} %copy-done.1), channel_id=1, source_target_pairs={{2,0},{3,1},{4,2},{5,3},{6,4},{7,5},{8,6},{9,7},{10,8},{11,9},{12,... | collective-permute-start | bytes 4128776 | tf_op jit(solution)/shard_map/ppermute | solution.py:14
  149.6 104.5 %collective-permute-start.4 = (bf16[192,3584]{1,0:T(8,128)(2,1)S(1)}, bf16[192,3584]{1,0:T(8,128)(2,1)S(1)}, u32[]{:S(2)}, u32[]{:S(2)}) collective-permute-start(bf16[192,3584]{1,0:T(8,128)(2,1)S(1)} %copy-done.1), channel_id=1, source_target_pairs={{0,2},{1,3},{2,4},{3,5},{4,6},{5,7},{6,8},{7,9},{8,10},{9,11},{10,... | collective-permute-start | bytes 4128776 | tf_op jit(solution)/shard_map/ppermute | solution.py:14
  154.7 99.8 %collective-permute-start.14 = (bf16[192,3584]{1,0:T(8,128)(2,1)S(1)}, bf16[192,3584]{1,0:T(8,128)(2,1)S(1)}, u32[]{:S(2)}, u32[]{:S(2)}) collective-permute-start(bf16[192,3584]{1,0:T(8,128)(2,1)S(1)} %copy-done.1), channel_id=1, source_target_pairs={{4,0},{5,1},{6,2},{7,3},{8,4},{9,5},{10,6},{11,7},{12,8},{13,9},{1... | collective-permute-start | bytes 4128776 | tf_op jit(solution)/shard_map/ppermute | solution.py:14
  156.6 98.5 %collective-permute-start.2 = (bf16[192,3584]{1,0:T(8,128)(2,1)S(1)}, bf16[192,3584]{1,0:T(8,128)(2,1)S(1)}, u32[]{:S(2)}, u32[]{:S(2)}) collective-permute-start(bf16[192,3584]{1,0:T(8,128)(2,1)S(1)} %copy-done.1), channel_id=1, source_target_pairs={{1,0},{2,1},{3,2},{4,3},{5,4},{6,5},{7,6},{8,7},{9,8},{10,9},{11,1... | collective-permute-start | bytes 4128776 | tf_op jit(solution)/shard_map/ppermute | solution.py:14
where the time goes:
time: 267 us; the launch traced here: 262 us
  starting transfers between devices  121 us (45%)
  waiting for transfers between devices  121 us (45%)
  matrix products  18.3 us (7%)
    ppermute x16, waiting for transfers between devices, from_behind(): return lax.ppermute(block, axis, route)  121 us
    ppermute x16, starting transfers between devices, from_behind(): return lax.ppermute(block, axis, route)  121 us
    dot_general x9, matrix products, relation_gap(): lax.dot_general(own_student, other_student, dims, preferred_element_type=...  6.8 us
    dot_general x9, matrix products, absorb(): jnp.dot(gap_b, other_student, preferred_element_type=jnp.float32)  6.69 us
  transfers between devices with their start and end apart: 16, of which 4 were waited for; matrix products, arithmetic and copies ran while one was open for 4% of the time, Pallas kernels for 0%

commit v1 on v0

v1 whole, which is shorter than its diff:
```python
import math

import jax
import jax.numpy as jnp
from jax import lax
from jax.sharding import PartitionSpec as P

REACH = 4
AXIS = "blk"


def move(block, target):
    devices = range(lax.axis_size(AXIS))
    route = [(i, target(i)) for i in devices if target(i) is not None and target(i) in devices]
    return lax.ppermute(block, AXIS, route)


def odd_chip(i):
    return (i // 2) % 2


def partner(i):
    return i ^ 2


def heavy(i):
    return i + 4 if odd_chip(i) else i - 4


def light(i):
    return i - 4 if odd_chip(i) else i + 4


def swap(i):
    return i ^ 1


def outer(i):
    return (i % 2) ^ odd_chip(i)


def swap_to_outer(i):
    return None if outer(i) else i ^ 1


def swap_to_inner(i):
    return i ^ 1 if outer(i) else None


def gram(a, b):
    return lax.dot_general(a, b, (((1,), (1,)), ((), ())), preferred_element_type=jnp.float32)


def body(student, teacher):
    rows, width = student.shape
    window = (2 * REACH + 1) * rows
    scale = 1.0 / math.sqrt(width)
    index = lax.axis_index(AXIS)
    inner = (1 - ((index % 2) ^ ((index // 2) % 2))).astype(jnp.float32)

    def gap(s, t, other_s, other_t, factor=scale):
        return (gram(s, other_s) - gram(t, other_t)) * factor

    t_far = move(teacher, heavy)
    s_side = move(student, partner)
    s_back = move(student, light)
    s_mate = move(student, swap)
    t_mate = move(teacher, swap)
    s_far = move(student, heavy)
    t_side = move(teacher, partner)
    s_diag = move(s_side, light)
    s_side_mate = move(s_side, swap)
    s_back_mate = move(s_back, swap_to_inner)
    t_far_mate = move(t_far, swap_to_outer)
    s_far_mate = move(s_far, swap_to_outer)
    t_side_mate = move(t_side, swap)
    s_diag_mate = move(s_diag, swap)

    out_gap = jnp.concatenate(
        [
            gap(s_far, t_far, student, teacher),
            gap(s_far, t_far, s_mate, t_mate, scale * inner),
            gap(s_far, t_far, s_side, t_side),
            gap(s_far, t_far, s_side_mate, t_side_mate),
        ],
        axis=1,
    ).astype(jnp.bfloat16)
    in_gap = move(out_gap, light)

    pairs = [
        (student, teacher),
        (s_mate, t_mate),
        (s_side, t_side),
        (s_side_mate, t_side_mate),
        (s_far, t_far),
        (s_far_mate, t_far_mate),
    ]
    grad = jnp.zeros((rows, width), jnp.float32)
    row_sum = jnp.zeros((rows,), jnp.float32)
    for other_s, other_t in pairs:
        g = gap(student, teacher, other_s, other_t)
        row_sum = row_sum + jnp.sum(g * g, axis=1)
        grad = grad + jnp.dot(g.astype(jnp.bfloat16), other_s, preferred_element_type=jnp.float32)
    wide = in_gap.astype(jnp.float32)
    row_sum = row_sum + jnp.sum(wide * wide, axis=1)
    for k, other_s in enumerate((s_back, s_back_mate, s_diag, s_diag_mate)):
        g = in_gap[:, k * rows : (k + 1) * rows]
        grad = grad + jnp.dot(g, other_s, preferred_element_type=jnp.float32)
    return ((grad / math.sqrt(window)).astype(jnp.bfloat16), row_sum / window)


def solution(mesh):
    return jax.shard_map(
        body,
        mesh=mesh,
        in_specs=(P(("parts", "blk"), None), P(("parts", "blk"), None)),
        out_specs=(P(("parts", "blk"), None), P(("parts", "blk"))),
        check_vma=False,
    )
```

time: 267 us -> 120 us (0.45); the launches traced: 262 us -> 118 us
  starting transfers between devices: 121 us -> 25 us
  waiting for transfers between devices: 121 us -> 56.7 us
  matrix products: 18.3 us -> 34.8 us
    ppermute x16 -> x15, starting transfers between devices: 121 us -> 25 us  [move(): return lax.ppermute(block, AXIS, route)]
    ppermute x16 -> x15, waiting for transfers between devices: 121 us -> 56.7 us  [move(): return lax.ppermute(block, AXIS, route)]
    dot_general x27 -> x30, matrix products: 18.3 us -> 34.8 us  [the longest x20 25.5 us: gram(): lax.dot_general(a, b, (((1,), (1,)), ((), ())), preferred_element_type=jn...]
  transfers between devices with their start and end apart: 16 -> 15, of which waited for: 4 -> 6; matrix products, arithmetic and copies ran while one was open for 4% -> 29% of each run, Pallas kernels for 0% -> 0%
where the time goes in v1:
time: 120 us; the launch traced here: 118 us
  waiting for transfers between devices  56.7 us (47%)
  matrix products  34.8 us (29%)
  starting transfers between devices  25 us (21%)
    ppermute x15, waiting for transfers between devices, move(): return lax.ppermute(block, AXIS, route)  56.7 us
    dot_general x20, matrix products, gram(): lax.dot_general(a, b, (((1,), (1,)), ((), ())), preferred_element_type=jn...  25.5 us
    ppermute x15, starting transfers between devices, move(): return lax.ppermute(block, AXIS, route)  25 us
    dot_general x6, matrix products, body(): jnp.dot(g.astype(jnp.bfloat16), other_s, preferred_element_type=jnp.float32)  6.11 us
    dot_general x4, matrix products, body(): grad = grad + jnp.dot(g, other_s, preferred_element_type=jnp.float32)  3.26 us
  transfers between devices with their start and end apart: 15, of which 6 were waited for; matrix products, arithmetic and copies ran while one was open for 29% of the time, Pallas kernels for 0%

profile of v1, /device:TPU:0, one launch (start us, length us, event | category | flops | bytes accessed | tf_op | source)
XLA Modules:
  0.0 118.3 jit_solution(3203574168488653396)
XLA Ops:
  0.6 1.4 %collective-permute-start.7 = (bf16[192,3584]{1,0:T(8,128)(2,1)}, bf16[192,3584]{1,0:T(8,128)(2,1)}, u32[]{:S(2)}, u32[]{:S(2)}) collective-permute-start(bf16[192,3584]{1,0:T(8,128)(2,1)} %param.3), channel_id=1, source_target_pairs={{2,6},{3,7},{4,0},{5,1},{6,10},{7,11},{8,4},{9,5},{10,14},{11,15},... | collective-permute-start | bytes 4128776 | tf_op jit(solution)/shard_map/ppermute | solution.py:15
  2.1 6.2 %collective-permute-start.3 = (bf16[192,3584]{1,0:T(8,128)(2,1)}, bf16[192,3584]{1,0:T(8,128)(2,1)}, u32[]{:S(2)}, u32[]{:S(2)}) collective-permute-start(bf16[192,3584]{1,0:T(8,128)(2,1)} %param.3), channel_id=1, source_target_pairs={{0,2},{1,3},{2,0},{3,1},{4,6},{5,7},{6,4},{7,5},{8,10},{9,11},{10,... | collective-permute-start | bytes 4128776 | tf_op jit(solution)/shard_map/ppermute | solution.py:15
  9.6 1.4 %collective-permute-start.2 = (bf16[192,3584]{1,0:T(8,128)(2,1)}, bf16[192,3584]{1,0:T(8,128)(2,1)}, u32[]{:S(2)}, u32[]{:S(2)}) collective-permute-start(bf16[192,3584]{1,0:T(8,128)(2,1)} %param.2), channel_id=1, source_target_pairs={{0,2},{1,3},{2,0},{3,1},{4,6},{5,7},{6,4},{7,5},{8,10},{9,11},{10,... | collective-permute-start | bytes 4128776 | tf_op jit(solution)/shard_map/ppermute | solution.py:15
  11.0 2.3 %fusion.33 = f32[192,192]{0,1:T(8,128)S(1)} fusion(bf16[192,3584]{1,0:T(8,128)(2,1)} %param.2), kind=kOutput, calls=%fused_computation.58 | convolution fusion | flops 264241152 | bytes 1523712 | tf_op jit(solution)/shard_map/dot_general | solution.py:51
  14.0 2.0 %fusion.31 = f32[192,3584]{1,0:T(8,128)S(1)} fusion(bf16[192,3584]{1,0:T(8,128)(2,1)} %param.2, bf16[192,192]{0,1:T(8,128)(2,1)S(1)} %get-tuple-element.11), kind=kOutput, calls=%fused_computation.55 | convolution fusion | flops 264241152 | bytes 4202496 | tf_op jit(solution)/shard_map/dot_general | solution.py:103
  16.0 21.1 %collective-permute-done.7 = bf16[192,3584]{1,0:T(8,128)(2,1)} collective-permute-done((bf16[192,3584]{1,0:T(8,128)(2,1)}, bf16[192,3584]{1,0:T(8,128)(2,1)}, u32[]{:S(2)}, u32[]{:S(2)}) %collective-permute-start.7) | collective-permute-done | bytes 1376288 | tf_op jit(solution)/shard_map/ppermute | solution.py:15
  37.0 1.9 %fusion.39 = f32[192,192]{0,1:T(8,128)S(1)} fusion(bf16[192,3584]{1,0:T(8,128)(2,1)} %collective-permute-done.7, bf16[192,3584]{1,0:T(8,128)(2,1)S(1)} %copy-done), kind=kOutput, calls=%fused_computation.64 | convolution fusion | flops 264241152 | bytes 2899968 | tf_op jit(solution)/shard_map/dot_general | solution.py:51
  39.7 3.3 %collective-permute-start.11 = (bf16[192,3584]{1,0:T(8,128)(2,1)S(1)}, bf16[192,3584]{1,0:T(8,128)(2,1)S(1)}, u32[]{:S(2)}, u32[]{:S(2)}) collective-permute-start(bf16[192,3584]{1,0:T(8,128)(2,1)S(1)} %copy-done.1), channel_id=1, source_target_pairs={{0,4},{1,5},{4,8},{5,9},{6,2},{7,3},{8,12},{9,13},{10,6},{11,7},{1... | collective-permute-start | bytes 4128776 | tf_op jit(solution)/shard_map/ppermute | solution.py:15
  43.0 2.3 %fusion.41 = f32[192,192]{0,1:T(8,128)S(1)} fusion(bf16[192,3584]{1,0:T(8,128)(2,1)} %collective-permute-done.7, bf16[192,3584]{1,0:T(8,128)(2,1)} %collective-permute-done.3), kind=kOutput, calls=%fused_computation.66 | convolution fusion | flops 264241152 | bytes 2899968 | tf_op jit(solution)/shard_map/dot_general | solution.py:51
  45.3 1.9 %fusion.35 = f32[192,192]{0,1:T(8,128)S(1)} fusion(bf16[192,3584]{1,0:T(8,128)(2,1)S(1)} %copy-done, bf16[192,3584]{1,0:T(8,128)(2,1)} %collective-permute-done.3), kind=kOutput, calls=%fused_computation.60 | convolution fusion | flops 264241152 | bytes 2899968 | tf_op jit(solution)/shard_map/dot_general | solution.py:51
  47.4 1.9 %fusion.34 = f32[192,192]{0,1:T(8,128)S(1)} fusion(bf16[192,3584]{1,0:T(8,128)(2,1)S(1)} %copy-done, bf16[192,3584]{1,0:T(8,128)(2,1)} %collective-permute-done.1), kind=kOutput, calls=%fused_computation.59 | convolution fusion | flops 264241152 | bytes 2899968 | tf_op jit(solution)/shard_map/dot_general | solution.py:51
  49.3 16.3 %collective-permute-done.6 = bf16[192,3584]{1,0:T(8,128)(2,1)S(1)} collective-permute-done((bf16[192,3584]{1,0:T(8,128)(2,1)}, bf16[192,3584]{1,0:T(8,128)(2,1)S(1)}, u32[]{:S(2)}, u32[]{:S(2)}) %collective-permute-start.6) | collective-permute-done | bytes 1376288 | tf_op jit(solution)/shard_map/ppermute | solution.py:15
  68.0 1.9 %fusion.17 = bf16[192,192]{0,1:T(8,128)(2,1)S(1)} fusion(f32[192,192]{0,1:T(8,128)S(1)} %fusion.41, bf16[192,3584]{1,0:T(8,128)(2,1)S(1)} %collective-permute-done.6, bf16[192,3584]{1,0:T(8,128)(2,1)} %collective-permute-done.2), kind=kOutput, calls=%fused_computation.33 | convolution fusion | flops 264351744 | bytes 2973696 | tf_op jit(solution)/shard_map/dot_general | solution.py:51
  70.4 1.9 %multiply_reduce_fusion.4 = (f32[192]{0:T(256)S(1)}, bf16[192,192]{0,1:T(8,128)(2,1)S(1)}) fusion(f32[192,192]{0,1:T(8,128)S(1)} %fusion.35, bf16[192,3584]{1,0:T(8,128)(2,1)S(1)} %copy-done.1, bf16[192,3584]{1,0:T(8,128)(2,1)} %collective-permute-done.2), kind=kOutput, calls=%fused_computation.40 | convolution fusion | flops 264425280 | bytes 2974464 | tf_op jit(solution)/shard_map/dot_general | solution.py:51
  72.3 2.8 %collective-permute-start.13 = (bf16[192,3584]{1,0:T(8,128)(2,1)}, bf16[192,3584]{1,0:T(8,128)(2,1)S(1)}, u32[]{:S(2)}, u32[]{:S(2)}) collective-permute-start(bf16[192,3584]{1,0:T(8,128)(2,1)} %collective-permute-done.2), channel_id=1, source_target_pairs={{0,4},{1,5},{4,8},{5,9},{6,2},{7,3},{8,12},{9,13},{10,6},{11,7},{1... | collective-permute-start | bytes 4128776 | tf_op jit(solution)/shard_map/ppermute | solution.py:15
  76.2 1.9 %convolution_add_fusion.4 = f32[192,3584]{1,0:T(8,128)S(1)} fusion(f32[192,3584]{1,0:T(8,128)S(1)} %convolution_add_fusion.5, bf16[192,3584]{1,0:T(8,128)(2,1)} %collective-permute-done.2, bf16[192,192]{0,1:T(8,128)(2,1)S(1)} %get-tuple-element.9), kind=kOutput, calls=%fused_computation.4 | convolution fusion | flops 264929280 | bytes 6955008 | tf_op jit(solution)/shard_map/dot_general | solution.py:103
  78.1 1.9 %fusion.37 = f32[192,192]{0,1:T(8,128)S(1)} fusion(bf16[192,3584]{1,0:T(8,128)(2,1)S(1)} %copy-done, bf16[192,3584]{1,0:T(8,128)(2,1)} %collective-permute-done.7), kind=kOutput, calls=%fused_computation.62 | convolution fusion | flops 264241152 | bytes 2899968 | tf_op jit(solution)/shard_map/dot_general | solution.py:51
  80.5 2.3 %fusion.40 = f32[192,192]{0,1:T(8,128)S(1)} fusion(bf16[192,3584]{1,0:T(8,128)(2,1)} %collective-permute-done.7, bf16[192,3584]{1,0:T(8,128)(2,1)} %collective-permute-done.1), kind=kOutput, calls=%fused_computation.65 | convolution fusion | flops 264241152 | bytes 2899968 | tf_op jit(solution)/shard_map/dot_general | solution.py:51
  83.9 2.2 %collective-permute-start.8 = (bf16[192,3584]{1,0:T(8,128)(2,1)S(1)}, bf16[192,3584]{1,0:T(8,128)(2,1)S(1)}, u32[]{:S(2)}, u32[]{:S(2)}) collective-permute-start(bf16[192,3584]{1,0:T(8,128)(2,1)S(1)} %collective-permute-done.6), channel_id=1, source_target_pairs={{0,1},{3,2},{4,5},{7,6},{8,9},{11,10},{12,13},{15,14},{16,17},{19,... | collective-permute-start | bytes 4128776 | tf_op jit(solution)/shard_map/ppermute | solution.py:15
  87.5 1.9 %fusion.42 = f32[192,192]{0,1:T(8,128)S(1)} fusion(bf16[192,3584]{1,0:T(8,128)(2,1)} %collective-permute-done.7, bf16[192,3584]{1,0:T(8,128)(2,1)S(1)} %collective-permute-done.5), kind=kOutput, calls=%fused_computation.67 | convolution fusion | flops 264241152 | bytes 2899968 | tf_op jit(solution)/shard_map/dot_general | solution.py:51
  90.0 3.4 %collective-permute-start.10 = (bf16[192,768]{0,1:T(8,128)(2,1)S(1)}, bf16[192,768]{0,1:T(8,128)(2,1)S(1)}, u32[]{:S(2)}, u32[]{:S(2)}) collective-permute-start(bf16[192,768]{0,1:T(8,128)(2,1)S(1)} %pad_maximum_fusion), channel_id=1, source_target_pairs={{0,4},{1,5},{4,8},{5,9},{6,2},{7,3},{8,12},{9,13},{10,6},{11,7},{1... | collective-permute-start | bytes 884744 | tf_op jit(solution)/shard_map/ppermute | solution.py:15
  93.4 12.4 %collective-permute-done.13 = bf16[192,3584]{1,0:T(8,128)(2,1)S(1)} collective-permute-done((bf16[192,3584]{1,0:T(8,128)(2,1)}, bf16[192,3584]{1,0:T(8,128)(2,1)S(1)}, u32[]{:S(2)}, u32[]{:S(2)}) %collective-permute-start.13) | collective-permute-done | bytes 1376288 | tf_op jit(solution)/shard_map/ppermute | solution.py:15
  108.6 5.2 %collective-permute-done.10 = bf16[192,768]{0,1:T(8,128)(2,1)S(1)} collective-permute-done((bf16[192,768]{0,1:T(8,128)(2,1)S(1)}, bf16[192,768]{0,1:T(8,128)(2,1)S(1)}, u32[]{:S(2)}, u32[]{:S(2)}) %collective-permute-start.10) | collective-permute-done | bytes 294944 | tf_op jit(solution)/shard_map/ppermute | solution.py:15
  116.7 1.6 %fusion.4 = bf16[192,3584]{1,0:T(8,128)(2,1)} fusion(f32[192,3584]{1,0:T(8,128)S(1)} %fusion.2, bf16[192,3584]{1,0:T(8,128)(2,1)S(1)} %collective-permute-done.14, bf16[192,768]{0,1:T(8,128)(2,1)S(1)} %collective-permute-done.10), kind=kOutput, calls=%fused_computation.10 | convolution fusion | flops 266305536 | bytes 5603328 | tf_op jit(solution)/shard_map/dot_general | solution.py:108
  (43 shorter events, 16.2 us)
Async XLA Ops:
  0.6 12.7 %copy-start = (bf16[192,3584]{1,0:T(8,128)(2,1)S(1)}, bf16[192,3584]{1,0:T(8,128)(2,1)}, u32[]{:S(2)}) copy-start(bf16[192,3584]{1,0:T(8,128)(2,1)} %param.3) | copy-start | bytes 4128772
  0.6 36.4 %collective-permute-start.7 = (bf16[192,3584]{1,0:T(8,128)(2,1)}, bf16[192,3584]{1,0:T(8,128)(2,1)}, u32[]{:S(2)}, u32[]{:S(2)}) collective-permute-start(bf16[192,3584]{1,0:T(8,128)(2,1)} %param.3), channel_id=1, source_target_pairs={{2,6},{3,7},{4,0},{5,1},{6,10},{7,11},{8,4},{9,5},{10,14},{11,15},... | collective-permute-start | bytes 4128776 | tf_op jit(solution)/shard_map/ppermute | solution.py:15
  2.1 37.6 %collective-permute-start.3 = (bf16[192,3584]{1,0:T(8,128)(2,1)}, bf16[192,3584]{1,0:T(8,128)(2,1)}, u32[]{:S(2)}, u32[]{:S(2)}) collective-permute-start(bf16[192,3584]{1,0:T(8,128)(2,1)} %param.3), channel_id=1, source_target_pairs={{0,2},{1,3},{2,0},{3,1},{4,6},{5,7},{6,4},{7,5},{8,10},{9,11},{10,... | collective-permute-start | bytes 4128776 | tf_op jit(solution)/shard_map/ppermute | solution.py:15
  8.3 38.9 %collective-permute-start.1 = (bf16[192,3584]{1,0:T(8,128)(2,1)}, bf16[192,3584]{1,0:T(8,128)(2,1)}, u32[]{:S(2)}, u32[]{:S(2)}) collective-permute-start(bf16[192,3584]{1,0:T(8,128)(2,1)} %param.3), channel_id=1, source_target_pairs={{0,1},{1,0},{2,3},{3,2},{4,5},{5,4},{6,7},{7,6},{8,9},{9,8},{10,11... | collective-permute-start | bytes 4128776 | tf_op jit(solution)/shard_map/ppermute | solution.py:15
  8.3 57.3 %collective-permute-start.6 = (bf16[192,3584]{1,0:T(8,128)(2,1)}, bf16[192,3584]{1,0:T(8,128)(2,1)S(1)}, u32[]{:S(2)}, u32[]{:S(2)}) collective-permute-start(bf16[192,3584]{1,0:T(8,128)(2,1)} %param.2), channel_id=1, source_target_pairs={{2,6},{3,7},{4,0},{5,1},{6,10},{7,11},{8,4},{9,5},{10,14},{11,15},... | collective-permute-start | bytes 4128776 | tf_op jit(solution)/shard_map/ppermute | solution.py:15
  9.6 58.4 %collective-permute-start.2 = (bf16[192,3584]{1,0:T(8,128)(2,1)}, bf16[192,3584]{1,0:T(8,128)(2,1)}, u32[]{:S(2)}, u32[]{:S(2)}) collective-permute-start(bf16[192,3584]{1,0:T(8,128)(2,1)} %param.2), channel_id=1, source_target_pairs={{0,2},{1,3},{2,0},{3,1},{4,6},{5,7},{6,4},{7,5},{8,10},{9,11},{10,... | collective-permute-start | bytes 4128776 | tf_op jit(solution)/shard_map/ppermute | solution.py:15
  14.0 23.1 %copy-start.1 = (bf16[192,3584]{1,0:T(8,128)(2,1)S(1)}, bf16[192,3584]{1,0:T(8,128)(2,1)}, u32[]{:S(2)}) copy-start(bf16[192,3584]{1,0:T(8,128)(2,1)} %param.2) | copy-start | bytes 4128772
  37.0 35.3 %collective-permute-start = (bf16[192,3584]{1,0:T(8,128)(2,1)S(1)}, bf16[192,3584]{1,0:T(8,128)(2,1)S(1)}, u32[]{:S(2)}, u32[]{:S(2)}) collective-permute-start(bf16[192,3584]{1,0:T(8,128)(2,1)S(1)} %copy-done.1), channel_id=1, source_target_pairs={{0,1},{1,0},{2,3},{3,2},{4,5},{5,4},{6,7},{7,6},{8,9},{9,8},{10,11... | collective-permute-start | bytes 4128776 | tf_op jit(solution)/shard_map/ppermute | solution.py:15
  39.7 44.3 %collective-permute-start.11 = (bf16[192,3584]{1,0:T(8,128)(2,1)S(1)}, bf16[192,3584]{1,0:T(8,128)(2,1)S(1)}, u32[]{:S(2)}, u32[]{:S(2)}) collective-permute-start(bf16[192,3584]{1,0:T(8,128)(2,1)S(1)} %copy-done.1), channel_id=1, source_target_pairs={{0,4},{1,5},{4,8},{5,9},{6,2},{7,3},{8,12},{9,13},{10,6},{11,7},{1... | collective-permute-start | bytes 4128776 | tf_op jit(solution)/shard_map/ppermute | solution.py:15
  47.2 39.0 %collective-permute-start.5 = (bf16[192,3584]{1,0:T(8,128)(2,1)}, bf16[192,3584]{1,0:T(8,128)(2,1)S(1)}, u32[]{:S(2)}, u32[]{:S(2)}) collective-permute-start(bf16[192,3584]{1,0:T(8,128)(2,1)} %collective-permute-done.3), channel_id=1, source_target_pairs={{0,1},{1,0},{2,3},{3,2},{4,5},{5,4},{6,7},{7,6},{8,9},{9,8},{10,11... | collective-permute-start | bytes 4128776 | tf_op jit(solution)/shard_map/ppermute | solution.py:15
  65.6 40.8 %collective-permute-start.9 = (bf16[192,3584]{1,0:T(8,128)(2,1)}, bf16[192,3584]{1,0:T(8,128)(2,1)S(1)}, u32[]{:S(2)}, u32[]{:S(2)}) collective-permute-start(bf16[192,3584]{1,0:T(8,128)(2,1)} %collective-permute-done.7), channel_id=1, source_target_pairs={{0,1},{3,2},{4,5},{7,6},{8,9},{11,10},{12,13},{15,14},{16,17},{19,... | collective-permute-start | bytes 4128776 | tf_op jit(solution)/shard_map/ppermute | solution.py:15
  68.0 21.3 %collective-permute-start.4 = (bf16[192,3584]{1,0:T(8,128)(2,1)}, bf16[192,3584]{1,0:T(8,128)(2,1)S(1)}, u32[]{:S(2)}, u32[]{:S(2)}) collective-permute-start(bf16[192,3584]{1,0:T(8,128)(2,1)} %collective-permute-done.2), channel_id=1, source_target_pairs={{0,1},{1,0},{2,3},{3,2},{4,5},{5,4},{6,7},{7,6},{8,9},{9,8},{10,11... | collective-permute-start | bytes 4128776 | tf_op jit(solution)/shard_map/ppermute | solution.py:15
  72.3 33.5 %collective-permute-start.13 = (bf16[192,3584]{1,0:T(8,128)(2,1)}, bf16[192,3584]{1,0:T(8,128)(2,1)S(1)}, u32[]{:S(2)}, u32[]{:S(2)}) collective-permute-start(bf16[192,3584]{1,0:T(8,128)(2,1)} %collective-permute-done.2), channel_id=1, source_target_pairs={{0,4},{1,5},{4,8},{5,9},{6,2},{7,3},{8,12},{9,13},{10,6},{11,7},{1... | collective-permute-start | bytes 4128776 | tf_op jit(solution)/shard_map/ppermute | solution.py:15
  83.9 24.1 %collective-permute-start.8 = (bf16[192,3584]{1,0:T(8,128)(2,1)S(1)}, bf16[192,3584]{1,0:T(8,128)(2,1)S(1)}, u32[]{:S(2)}, u32[]{:S(2)}) collective-permute-start(bf16[192,3584]{1,0:T(8,128)(2,1)S(1)} %collective-permute-done.6), channel_id=1, source_target_pairs={{0,1},{3,2},{4,5},{7,6},{8,9},{11,10},{12,13},{15,14},{16,17},{19,... | collective-permute-start | bytes 4128776 | tf_op jit(solution)/shard_map/ppermute | solution.py:15
  86.2 30.0 %collective-permute-start.12 = (bf16[192,3584]{1,0:T(8,128)(2,1)S(1)}, bf16[192,3584]{1,0:T(8,128)(2,1)S(1)}, u32[]{:S(2)}, u32[]{:S(2)}) collective-permute-start(bf16[192,3584]{1,0:T(8,128)(2,1)S(1)} %collective-permute-done.11), channel_id=1, source_target_pairs={{1,0},{2,3},{5,4},{6,7},{9,8},{10,11},{13,12},{14,15},{17,16},{18,... | collective-permute-start | bytes 4128776 | tf_op jit(solution)/shard_map/ppermute | solution.py:15
  90.0 23.8 %collective-permute-start.10 = (bf16[192,768]{0,1:T(8,128)(2,1)S(1)}, bf16[192,768]{0,1:T(8,128)(2,1)S(1)}, u32[]{:S(2)}, u32[]{:S(2)}) collective-permute-start(bf16[192,768]{0,1:T(8,128)(2,1)S(1)} %pad_maximum_fusion), channel_id=1, source_target_pairs={{0,4},{1,5},{4,8},{5,9},{6,2},{7,3},{8,12},{9,13},{10,6},{11,7},{1... | collective-permute-start | bytes 884744 | tf_op jit(solution)/shard_map/ppermute | solution.py:15
  105.8 10.9 %collective-permute-start.14 = (bf16[192,3584]{1,0:T(8,128)(2,1)S(1)}, bf16[192,3584]{1,0:T(8,128)(2,1)S(1)}, u32[]{:S(2)}, u32[]{:S(2)}) collective-permute-start(bf16[192,3584]{1,0:T(8,128)(2,1)S(1)} %collective-permute-done.13), channel_id=1, source_target_pairs={{0,1},{1,0},{2,3},{3,2},{4,5},{5,4},{6,7},{7,6},{8,9},{9,8},{10,11... | collective-permute-start | bytes 4128776 | tf_op jit(solution)/shard_map/ppermute | solution.py:15

commit v2 on v1

v2 whole, which is shorter than its diff:
```python
import functools
import math

import jax
import jax.numpy as jnp
from jax import lax
from jax.experimental import pallas as pl
from jax.experimental.pallas import tpu as pltpu
from jax.sharding import PartitionSpec as P

REACH = 4
AXIS = "blk"
LANES = 128
VMEM_BYTES = 9 * 1024 * 1024


def move(block, target):
    devices = range(lax.axis_size(AXIS))
    route = [(i, target(i)) for i in devices if target(i) is not None and target(i) in devices]
    return lax.ppermute(block, AXIS, route)


def odd_chip(i):
    return (i // 2) % 2


def partner(i):
    return i ^ 2


def heavy(i):
    return i + 4 if odd_chip(i) else i - 4


def light(i):
    return i - 4 if odd_chip(i) else i + 4


def swap(i):
    return i ^ 1


def outer(i):
    return (i % 2) ^ odd_chip(i)


def swap_to_outer(i):
    return None if outer(i) else i ^ 1


def swap_to_inner(i):
    return i ^ 1 if outer(i) else None


def after(block, *others):
    return lax.optimization_barrier((block, *others))[0]


def gram(a, b):
    return lax.dot_general(a, b, (((1,), (1,)), ((), ())), preferred_element_type=jnp.float32)


def lane_sums(x):
    total = x[:, :LANES]
    for k in range(1, x.shape[1] // LANES):
        total = total + x[:, k * LANES : (k + 1) * LANES]
    return total


def columns(width):
    for tile in (512, 384, 256, 128):
        if width % tile == 0:
            return tile
    return width


def call(kernel, ins, outs, scratch, flops, name):
    nbytes = sum(x.size * x.dtype.itemsize for x in ins) + sum(math.prod(o.shape) * o.dtype.itemsize for o in outs)
    spec = pl.BlockSpec(memory_space=pltpu.VMEM)
    return pl.pallas_call(
        kernel,
        in_specs=[spec] * len(ins),
        out_specs=[spec] * len(outs),
        out_shape=outs,
        scratch_shapes=scratch,
        cost_estimate=pl.CostEstimate(flops=int(flops), bytes_accessed=int(nbytes), transcendentals=0),
        compiler_params=pltpu.CompilerParams(vmem_limit_bytes=VMEM_BYTES),
        name=name,
    )(*ins)


def grams(rows_of, others, store):
    rows = rows_of.shape[0]
    for j, other in enumerate(others):
        store(slice(j * rows, (j + 1) * rows), gram(rows_of[...], other[...]))


def weigh(gap_b, others, put):
    width = others[0].shape[1]
    tile = columns(width)
    for k in range(width // tile):
        at = slice(k * tile, (k + 1) * tile)
        stack = jnp.concatenate([other[:, at] for other in others], axis=0)
        put(at, jnp.dot(gap_b[...], stack, preferred_element_type=jnp.float32))


def own_kernel(scale, s, t, s_mate, t_mate, grad, sums, gap_b):
    rows = s.shape[0]
    for j, (os, ot) in enumerate(((s, t), (s_mate, t_mate))):
        g = (gram(s[...], os[...]) - gram(t[...], ot[...])) * scale
        gap_b[:, j * rows : (j + 1) * rows] = g.astype(jnp.bfloat16)
    wide = gap_b[...].astype(jnp.float32)
    sums[...] = lane_sums(wide * wide)

    def put(at, value):
        grad[:, at] = value

    weigh(gap_b, (s, s_mate), put)


def own_part(s, t, s_mate, t_mate, scale):
    rows, width = s.shape
    return call(
        functools.partial(own_kernel, scale),
        (s, t, s_mate, t_mate),
        [jax.ShapeDtypeStruct((rows, width), jnp.float32), jax.ShapeDtypeStruct((rows, LANES), jnp.float32)],
        [pltpu.VMEM((rows, 2 * rows), jnp.bfloat16)],
        512 * rows * rows * width,
        "own_part",
    )


def student_grams_kernel(s, s_mate, x, x_mate, f, f_mate, mine, out):
    def store_mine(at, value):
        mine[:, at] = value

    def store_out(at, value):
        out[:, at] = value

    grams(s, (x, x_mate, f, f_mate), store_mine)
    grams(f, (s, s_mate, x, x_mate), store_out)


def student_grams(*blocks):
    rows, width = blocks[0].shape
    shape = jax.ShapeDtypeStruct((rows, 4 * rows), jnp.float32)
    return call(student_grams_kernel, blocks, [shape, shape], [], 16 * rows * rows * width, "student_grams")


def send_gap_kernel(f, t, t_mate, x, x_mate, student, factors, out):
    def store(at, value):
        out[:, at] = ((student[:, at] - value) * factors[:, at]).astype(jnp.bfloat16)

    grams(f, (t, t_mate, x, x_mate), store)


def send_gap(f, t, t_mate, x, x_mate, student, factors):
    rows, width = f.shape
    return call(
        send_gap_kernel,
        (f, t, t_mate, x, x_mate, student, factors),
        [jax.ShapeDtypeStruct((rows, 4 * rows), jnp.bfloat16)],
        [],
        512 * rows * rows * width,
        "send_gap",
    )[0]


def near_kernel(scale, t, tx, tx_mate, tf, tf_mate, student, sx, sx_mate, sf, sf_mate, grad_in, sums_in, grad, sums, gap_b):
    def store(at, value):
        gap_b[:, at] = ((student[:, at] - value) * scale).astype(jnp.bfloat16)

    grams(t, (tx, tx_mate, tf, tf_mate), store)
    wide = gap_b[...].astype(jnp.float32)
    sums[...] = sums_in[...] + lane_sums(wide * wide)

    def put(at, value):
        grad[:, at] = grad_in[:, at] + value

    weigh(gap_b, (sx, sx_mate, sf, sf_mate), put)


def near_part(t, tx, tx_mate, tf, tf_mate, student, sx, sx_mate, sf, sf_mate, grad_in, sums_in, scale):
    rows, width = t.shape
    return call(
        functools.partial(near_kernel, scale),
        (t, tx, tx_mate, tf, tf_mate, student, sx, sx_mate, sf, sf_mate, grad_in, sums_in),
        [jax.ShapeDtypeStruct((rows, width), jnp.float32), jax.ShapeDtypeStruct((rows, LANES), jnp.float32)],
        [pltpu.VMEM((rows, 4 * rows), jnp.bfloat16)],
        16 * rows * rows * width,
        "near_part",
    )


def last_kernel(scale, gap_b, a, b, c, d, grad_in, sums_in, grad, sums):
    def put(at, value):
        grad[:, at] = ((grad_in[:, at] + value) * scale).astype(grad.dtype)

    weigh(gap_b, (a, b, c, d), put)
    wide = gap_b[...].astype(jnp.float32)
    sums[...] = sums_in[...] + lane_sums(wide * wide)


def last_part(gap_b, a, b, c, d, grad_in, sums_in, scale):
    rows, width = a.shape
    return call(
        functools.partial(last_kernel, scale),
        (gap_b, a, b, c, d, grad_in, sums_in),
        [jax.ShapeDtypeStruct((rows, width), jnp.bfloat16), jax.ShapeDtypeStruct((rows, LANES), jnp.float32)],
        [],
        8 * rows * rows * width,
        "last_part",
    )


def body(student, teacher):
    rows, width = student.shape
    window = (2 * REACH + 1) * rows
    scale = 1.0 / math.sqrt(width)
    index = lax.axis_index(AXIS)
    inner = (1 - ((index % 2) ^ ((index // 2) % 2))).astype(jnp.float32)
    lane = lax.broadcasted_iota(jnp.int32, (1, 4 * rows), 1)
    factors = jnp.where((lane >= rows) & (lane < 2 * rows), scale * inner, scale)

    s_side = move(student, partner)
    s_far = move(student, heavy)
    s_back = move(student, light)
    s_mate = move(student, swap)
    t_mate = move(teacher, swap)
    t_side = move(after(teacher, s_side), partner)
    t_far = move(after(teacher, s_far), heavy)
    s_diag = move(after(s_side, s_back), light)

    grad, sums = own_part(student, teacher, s_mate, t_mate, scale)
    s_side_mate = move(s_side, swap)
    s_far_mate = move(s_far, swap_to_outer)
    s_back_mate = move(after(s_back, s_side_mate, s_far_mate), swap_to_inner)
    mine, out = student_grams(student, s_mate, s_side, s_side_mate, s_far, s_far_mate)

    t_side_mate = move(after(t_side, out), swap)
    t_far_mate = move(after(t_far, out), swap_to_outer)
    s_diag_mate = move(s_diag, swap)
    out_gap = send_gap(t_far, teacher, t_mate, t_side, t_side_mate, out, factors)
    in_gap = move(out_gap, light)
    grad, sums = near_part(
        teacher, t_side, t_side_mate, t_far, t_far_mate, mine,
        s_side, s_side_mate, s_far, s_far_mate, grad, sums, scale,
    )
    grad, sums = last_part(in_gap, s_back, s_back_mate, s_diag, s_diag_mate, grad, sums, 1.0 / math.sqrt(window))
    return grad, jnp.sum(sums, axis=1) / window


def solution(mesh):
    return jax.shard_map(
        body,
        mesh=mesh,
        in_specs=(P(("parts", "blk"), None), P(("parts", "blk"), None)),
        out_specs=(P(("parts", "blk"), None), P(("parts", "blk"))),
        check_vma=False,
    )
```

time: 120 us -> 103 us (0.86)
  matrix products: 34.8 us -> 0 us
  Pallas kernels: 0 us -> 20 us
  waiting for transfers between devices: 56.7 us -> 50.1 us
  local copies, waits for them, and re-layouts: 0.01 us -> 4.59 us
    dot_general x30 -> x0, matrix products: 34.8 us -> none  [the longest x20 25.5 us: gram(): lax.dot_general(a, b, (((1,), (1,)), ((), ())), preferred_element_type=jn...]
    pallas_call x0 -> x5, Pallas kernels: none -> 20 us  [call(): pl.pallas_call(kernel, in_specs=[spec] * len(ins), out_specs=[spec] * len...]
    ppermute x15, waiting for transfers between devices: 56.7 us -> 50.1 us  [move(): return lax.ppermute(block, AXIS, route)]
    unnamed x4 -> x28, local copies, waits for them, and re-layouts: 0.01 us -> 4.59 us
  transfers between devices with their start and end apart: 15 -> 15, of which waited for: 6 -> 4; matrix products, arithmetic and copies ran while one was open for 29% -> 0% of each run, Pallas kernels for 0% -> 16%
where the time goes in v2:
time: 103 us; the launch traced here: 102 us
  waiting for transfers between devices  50.1 us (49%)
  starting transfers between devices  26.1 us (25%)
  Pallas kernels  20 us (19%)
  local copies, waits for them, and re-layouts  4.59 us (4%)
    ppermute x15, waiting for transfers between devices, move(): return lax.ppermute(block, AXIS, route)  50.1 us
    ppermute x15, starting transfers between devices, move(): return lax.ppermute(block, AXIS, route)  26.1 us
    pallas_call x5, Pallas kernels, call(): pl.pallas_call(kernel, in_specs=[spec] * len(ins), out_specs=[spec] * len...  20 us
    unnamed x28, local copies, waits for them, and re-layouts  4.59 us
  transfers between devices with their start and end apart: 15, of which 4 were waited for; matrix products, arithmetic and copies ran while one was open for 0% of the time, Pallas kernels for 16%

profile of v2, /device:TPU:0, one launch (start us, length us, event | category | flops | bytes accessed | tf_op | source)
XLA Modules:
  0.0 102.4 jit_solution(9962309538912383453)
XLA Ops:
  0.6 3.0 %collective-permute-start.3 = (bf16[192,3584]{1,0:T(8,128)(2,1)}, bf16[192,3584]{1,0:T(8,128)(2,1)S(1)}, u32[]{:S(2)}, u32[]{:S(2)}) collective-permute-start(bf16[192,3584]{1,0:T(8,128)(2,1)} %s.3), channel_id=1, source_target_pairs={{0,2},{1,3},{2,0},{3,1},{4,6},{5,7},{6,4},{7,5},{8,10},{9,11},{10,... | collective-permute-start | bytes 4128776 | tf_op jit(solution)/shard_map/ppermute | solution.py:20
  3.6 1.3 %collective-permute-start = (bf16[192,3584]{1,0:T(8,128)(2,1)}, bf16[192,3584]{1,0:T(8,128)(2,1)S(1)}, u32[]{:S(2)}, u32[]{:S(2)}) collective-permute-start(bf16[192,3584]{1,0:T(8,128)(2,1)} %s.3), channel_id=1, source_target_pairs={{2,6},{3,7},{4,0},{5,1},{6,10},{7,11},{8,4},{9,5},{10,14},{11,15},... | collective-permute-start | bytes 4128776 | tf_op jit(solution)/shard_map/ppermute | solution.py:20
  4.9 4.6 %collective-permute-start.10 = (bf16[192,3584]{1,0:T(8,128)(2,1)}, bf16[192,3584]{1,0:T(8,128)(2,1)S(1)}, u32[]{:S(2)}, u32[]{:S(2)}) collective-permute-start(bf16[192,3584]{1,0:T(8,128)(2,1)} %s.3), channel_id=1, source_target_pairs={{0,4},{1,5},{4,8},{5,9},{6,2},{7,3},{8,12},{9,13},{10,6},{11,7},{1... | collective-permute-start | bytes 4128776 | tf_op jit(solution)/shard_map/ppermute | solution.py:20
  9.6 24.4 %collective-permute-done.3.x.sx = bf16[192,3584]{1,0:T(8,128)(2,1)S(1)} collective-permute-done((bf16[192,3584]{1,0:T(8,128)(2,1)}, bf16[192,3584]{1,0:T(8,128)(2,1)S(1)}, u32[]{:S(2)}, u32[]{:S(2)}) %collective-permute-start.3) | collective-permute-done | bytes 1376288 | tf_op jit(solution)/shard_map/ppermute | solution.py:20
  34.0 3.3 %collective-permute-done.f.sf = bf16[192,3584]{1,0:T(8,128)(2,1)S(1)} collective-permute-done((bf16[192,3584]{1,0:T(8,128)(2,1)}, bf16[192,3584]{1,0:T(8,128)(2,1)S(1)}, u32[]{:S(2)}, u32[]{:S(2)}) %collective-permute-start) | collective-permute-done | bytes 1376288 | tf_op jit(solution)/shard_map/ppermute | solution.py:20
  37.4 1.4 %collective-permute-start.7 = (bf16[192,3584]{1,0:T(8,128)(2,1)S(1)}, bf16[192,3584]{1,0:T(8,128)(2,1)S(1)}, u32[]{:S(2)}, u32[]{:S(2)}) collective-permute-start(bf16[192,3584]{1,0:T(8,128)(2,1)S(1)} %collective-permute-done.f.sf), channel_id=1, source_target_pairs={{0,1},{3,2},{4,5},{7,6},{8,9},{11,10},{12,13},{15,14},{16,17},{19,... | collective-permute-start | bytes 4128776 | tf_op jit(solution)/shard_map/ppermute | solution.py:20
  39.4 1.3 %collective-permute-start.1 = (bf16[192,3584]{1,0:T(8,128)(2,1)}, bf16[192,3584]{1,0:T(8,128)(2,1)}, u32[]{:S(2)}, u32[]{:S(2)}) collective-permute-start(bf16[192,3584]{1,0:T(8,128)(2,1)} %t.5), channel_id=1, source_target_pairs={{2,6},{3,7},{4,0},{5,1},{6,10},{7,11},{8,4},{9,5},{10,14},{11,15},... | collective-permute-start | bytes 4128776 | tf_op jit(solution)/shard_map/ppermute | solution.py:20
  40.7 6.0 %collective-permute-start.12 = (bf16[192,3584]{1,0:T(8,128)(2,1)S(1)}, bf16[192,3584]{1,0:T(8,128)(2,1)}, u32[]{:S(2)}, u32[]{:S(2)}) collective-permute-start(bf16[192,3584]{1,0:T(8,128)(2,1)S(1)} %collective-permute-done.3.x.sx), channel_id=1, source_target_pairs={{0,4},{1,5},{4,8},{5,9},{6,2},{7,3},{8,12},{9,13},{10,6},{11,7},{1... | collective-permute-start | bytes 4128776 | tf_op jit(solution)/shard_map/ppermute | solution.py:20
  46.7 1.3 %copy-done.4 = bf16[192,3584]{1,0:T(8,128)(2,1)S(1)} copy-done((bf16[192,3584]{1,0:T(8,128)(2,1)S(1)}, bf16[192,3584]{1,0:T(8,128)(2,1)}, u32[]{:S(2)}) %copy-start.4) | copy-done | bytes 1376280
  48.1 3.1 %student_grams.1 = (f32[192,768]{1,0:T(8,128)S(1)}, f32[192,768]{1,0:T(8,128)S(1)}) custom-call(bf16[192,3584]{1,0:T(8,128)(2,1)S(1)} %copy-done.4, bf16[192,3584]{1,0:T(8,128)(2,1)S(1)} %collective-permute-done.5.s_mate, bf16[192,3584]{1,0:T(8,128)(2,1)S(1)} %collective-permute-done.3.x.sx, bf16[192,3584]{1,0:T(8,128)(2,1)S(1)} %collective-permute-done.6.x_mate.sx_mate, ...), custom_call_target="tpu_custom_call" | custom-call | flops 2113929216 | bytes 9437184 | tf_op jit(solution)/shard_map/student_grams/pallas_call | solution.py:80
  51.2 0.8 copy-done.12
  52.0 18.3 %collective-permute-done.4.x.tx = bf16[192,3584]{1,0:T(8,128)(2,1)} collective-permute-done((bf16[192,3584]{1,0:T(8,128)(2,1)}, bf16[192,3584]{1,0:T(8,128)(2,1)}, u32[]{:S(2)}, u32[]{:S(2)}) %collective-permute-start.4) | collective-permute-done | bytes 1376288 | tf_op jit(solution)/shard_map/ppermute | solution.py:20
  70.4 4.0 %collective-permute-done.1.f.tf = bf16[192,3584]{1,0:T(8,128)(2,1)} collective-permute-done((bf16[192,3584]{1,0:T(8,128)(2,1)}, bf16[192,3584]{1,0:T(8,128)(2,1)}, u32[]{:S(2)}, u32[]{:S(2)}) %collective-permute-start.1) | collective-permute-done | bytes 1376288 | tf_op jit(solution)/shard_map/ppermute | solution.py:20
  74.4 1.5 %collective-permute-start.14 = (bf16[192,3584]{1,0:T(8,128)(2,1)}, bf16[192,3584]{1,0:T(8,128)(2,1)S(1)}, u32[]{:S(2)}, u32[]{:S(2)}) collective-permute-start(bf16[192,3584]{1,0:T(8,128)(2,1)} %collective-permute-done.1.f.tf), channel_id=1, source_target_pairs={{0,1},{3,2},{4,5},{7,6},{8,9},{11,10},{12,13},{15,14},{16,17},{19,... | collective-permute-start | bytes 4128776 | tf_op jit(solution)/shard_map/ppermute | solution.py:20
  75.8 1.3 %collective-permute-start.11 = (bf16[192,3584]{1,0:T(8,128)(2,1)}, bf16[192,3584]{1,0:T(8,128)(2,1)S(1)}, u32[]{:S(2)}, u32[]{:S(2)}) collective-permute-start(bf16[192,3584]{1,0:T(8,128)(2,1)} %copy-done.6), channel_id=1, source_target_pairs={{1,0},{2,3},{5,4},{6,7},{9,8},{10,11},{13,12},{14,15},{17,16},{18,... | collective-permute-start | bytes 4128776 | tf_op jit(solution)/shard_map/ppermute | solution.py:20
  77.2 1.3 %collective-permute-start.13 = (bf16[192,3584]{1,0:T(8,128)(2,1)}, bf16[192,3584]{1,0:T(8,128)(2,1)S(1)}, u32[]{:S(2)}, u32[]{:S(2)}) collective-permute-start(bf16[192,3584]{1,0:T(8,128)(2,1)} %collective-permute-done.12.c), channel_id=1, source_target_pairs={{0,1},{1,0},{2,3},{3,2},{4,5},{5,4},{6,7},{7,6},{8,9},{9,8},{10,11... | collective-permute-start | bytes 4128776 | tf_op jit(solution)/shard_map/ppermute | solution.py:20
  78.4 1.3 %copy-done.10 = bf16[192,3584]{1,0:T(8,128)(2,1)S(1)} copy-done((bf16[192,3584]{1,0:T(8,128)(2,1)S(1)}, bf16[192,3584]{1,0:T(8,128)(2,1)}, u32[]{:S(2)}) %copy-start.10) | copy-done | bytes 1376280
  79.8 1.1 %copy-done.13 = f32[192,768]{1,0:T(8,128)S(1)} copy-done((f32[192,768]{1,0:T(8,128)S(1)}, f32[192,768]{1,0:T(8,128)}, u32[]{:S(2)}) %copy-start.13) | copy-done | bytes 589848
  80.8 4.4 %send_gap.1 = bf16[192,768]{1,0:T(8,128)(2,1)S(1)} custom-call(bf16[192,3584]{1,0:T(8,128)(2,1)} %collective-permute-done.1.f.tf, bf16[192,3584]{1,0:T(8,128)(2,1)S(1)} %copy-done.10, bf16[192,3584]{1,0:T(8,128)(2,1)} %collective-permute-done.2.t_mate, bf16[192,3584]{1,0:T(8,128)(2,1)} %collective-permute-done.4.x.tx, ...), custom_call_target="tpu_custom_call" | custom-call | flops 67645734912 | bytes 7769088 | tf_op jit(solution)/shard_map/send_gap/pallas_call | solution.py:80
  85.2 3.8 %collective-permute-start.9 = (bf16[192,768]{1,0:T(8,128)(2,1)S(1)}, bf16[192,768]{1,0:T(8,128)(2,1)S(1)}, u32[]{:S(2)}, u32[]{:S(2)}) collective-permute-start(bf16[192,768]{1,0:T(8,128)(2,1)S(1)} %send_gap.1), channel_id=1, source_target_pairs={{0,4},{1,5},{4,8},{5,9},{6,2},{7,3},{8,12},{9,13},{10,6},{11,7},{1... | collective-permute-start | bytes 884744 | tf_op jit(solution)/shard_map/ppermute | solution.py:20
  89.1 3.8 %own_part.1 = (f32[192,3584]{1,0:T(8,128)S(1)}, f32[192,128]{1,0:T(8,128)S(1)}) custom-call(bf16[192,3584]{1,0:T(8,128)(2,1)S(1)} %copy-done.5, bf16[192,3584]{1,0:T(8,128)(2,1)S(1)} %copy-done.11, bf16[192,3584]{1,0:T(8,128)(2,1)S(1)} %copy-done.9, bf16[192,3584]{1,0:T(8,128)(2,1)} %collective-permute-done.2.t_mate), custom_call_target="tpu_custom_call" | custom-call | flops 67645734912 | bytes 8355840 | tf_op jit(solution)/shard_map/own_part/pallas_call | solution.py:80
  92.9 5.0 %near_part.1 = (f32[192,3584]{1,0:T(8,128)S(1)}, f32[192,128]{1,0:T(8,128)S(1)}) custom-call(bf16[192,3584]{1,0:T(8,128)(2,1)S(1)} %copy-done.11, bf16[192,3584]{1,0:T(8,128)(2,1)} %collective-permute-done.4.x.tx, bf16[192,3584]{1,0:T(8,128)(2,1)} %collective-permute-done.8.x_mate.tx_mate, bf16[192,3584]{1,0:T(8,128)(2,1)} %collective-permute-done.1.f.tf, ...), custom_call_target="tpu_custom_call" | custom-call | flops 2113929216 | bytes 18677760 | tf_op jit(solution)/shard_map/near_part/pallas_call | solution.py:80
  98.0 3.7 %last_part.1 = (bf16[192,3584]{1,0:T(8,128)(2,1)}, f32[192,128]{1,0:T(8,128)S(1)}) custom-call(bf16[192,768]{1,0:T(8,128)(2,1)S(1)} %collective-permute-done.9.gap_b, bf16[192,3584]{1,0:T(8,128)(2,1)S(1)} %copy-done.7, bf16[192,3584]{1,0:T(8,128)(2,1)S(1)} %collective-permute-done.11.b, bf16[192,3584]{1,0:T(8,128)(2,1)} %collective-permute-done.12.c, ...), custom_call_target="tpu_custom_call" | custom-call | flops 1056964608 | bytes 10125312 | tf_op jit(solution)/shard_map/last_part/pallas_call | solution.py:80
  101.9 0.6 broadcast_multiply_fusion
  (42 shorter events, 0.9 us)
Async XLA Ops:
  0.6 33.4 %collective-permute-start.3 = (bf16[192,3584]{1,0:T(8,128)(2,1)}, bf16[192,3584]{1,0:T(8,128)(2,1)S(1)}, u32[]{:S(2)}, u32[]{:S(2)}) collective-permute-start(bf16[192,3584]{1,0:T(8,128)(2,1)} %s.3), channel_id=1, source_target_pairs={{0,2},{1,3},{2,0},{3,1},{4,6},{5,7},{6,4},{7,5},{8,10},{9,11},{10,... | collective-permute-start | bytes 4128776 | tf_op jit(solution)/shard_map/ppermute | solution.py:20
  3.6 33.7 %collective-permute-start = (bf16[192,3584]{1,0:T(8,128)(2,1)}, bf16[192,3584]{1,0:T(8,128)(2,1)S(1)}, u32[]{:S(2)}, u32[]{:S(2)}) collective-permute-start(bf16[192,3584]{1,0:T(8,128)(2,1)} %s.3), channel_id=1, source_target_pairs={{2,6},{3,7},{4,0},{5,1},{6,10},{7,11},{8,4},{9,5},{10,14},{11,15},... | collective-permute-start | bytes 4128776 | tf_op jit(solution)/shard_map/ppermute | solution.py:20
  4.9 33.9 %collective-permute-start.10 = (bf16[192,3584]{1,0:T(8,128)(2,1)}, bf16[192,3584]{1,0:T(8,128)(2,1)S(1)}, u32[]{:S(2)}, u32[]{:S(2)}) collective-permute-start(bf16[192,3584]{1,0:T(8,128)(2,1)} %s.3), channel_id=1, source_target_pairs={{0,4},{1,5},{4,8},{5,9},{6,2},{7,3},{8,12},{9,13},{10,6},{11,7},{1... | collective-permute-start | bytes 4128776 | tf_op jit(solution)/shard_map/ppermute | solution.py:20
  9.6 29.8 %collective-permute-start.5 = (bf16[192,3584]{1,0:T(8,128)(2,1)}, bf16[192,3584]{1,0:T(8,128)(2,1)S(1)}, u32[]{:S(2)}, u32[]{:S(2)}) collective-permute-start(bf16[192,3584]{1,0:T(8,128)(2,1)} %s.3), channel_id=1, source_target_pairs={{0,1},{1,0},{2,3},{3,2},{4,5},{5,4},{6,7},{7,6},{8,9},{9,8},{10,11... | collective-permute-start | bytes 4128776 | tf_op jit(solution)/shard_map/ppermute | solution.py:20
  34.0 6.7 %collective-permute-start.6 = (bf16[192,3584]{1,0:T(8,128)(2,1)S(1)}, bf16[192,3584]{1,0:T(8,128)(2,1)S(1)}, u32[]{:S(2)}, u32[]{:S(2)}) collective-permute-start(bf16[192,3584]{1,0:T(8,128)(2,1)S(1)} %collective-permute-done.3.x.sx), channel_id=1, source_target_pairs={{0,1},{1,0},{2,3},{3,2},{4,5},{5,4},{6,7},{7,6},{8,9},{9,8},{10,11... | collective-permute-start | bytes 4128776 | tf_op jit(solution)/shard_map/ppermute | solution.py:20
  37.4 9.3 %collective-permute-start.7 = (bf16[192,3584]{1,0:T(8,128)(2,1)S(1)}, bf16[192,3584]{1,0:T(8,128)(2,1)S(1)}, u32[]{:S(2)}, u32[]{:S(2)}) collective-permute-start(bf16[192,3584]{1,0:T(8,128)(2,1)S(1)} %collective-permute-done.f.sf), channel_id=1, source_target_pairs={{0,1},{3,2},{4,5},{7,6},{8,9},{11,10},{12,13},{15,14},{16,17},{19,... | collective-permute-start | bytes 4128776 | tf_op jit(solution)/shard_map/ppermute | solution.py:20
  38.7 31.6 %collective-permute-start.4 = (bf16[192,3584]{1,0:T(8,128)(2,1)}, bf16[192,3584]{1,0:T(8,128)(2,1)}, u32[]{:S(2)}, u32[]{:S(2)}) collective-permute-start(bf16[192,3584]{1,0:T(8,128)(2,1)} %t.5), channel_id=1, source_target_pairs={{0,2},{1,3},{2,0},{3,1},{4,6},{5,7},{6,4},{7,5},{8,10},{9,11},{10,... | collective-permute-start | bytes 4128776 | tf_op jit(solution)/shard_map/ppermute | solution.py:20
  38.8 7.9 %copy-start.6 = (bf16[192,3584]{1,0:T(8,128)(2,1)}, bf16[192,3584]{1,0:T(8,128)(2,1)S(1)}, u32[]{:S(2)}) copy-start(bf16[192,3584]{1,0:T(8,128)(2,1)S(1)} %collective-permute-done.10.a) | copy-start | bytes 4128772
  38.8 39.6 %collective-permute-start.2 = (bf16[192,3584]{1,0:T(8,128)(2,1)}, bf16[192,3584]{1,0:T(8,128)(2,1)}, u32[]{:S(2)}, u32[]{:S(2)}) collective-permute-start(bf16[192,3584]{1,0:T(8,128)(2,1)} %t.5), channel_id=1, source_target_pairs={{0,1},{1,0},{2,3},{3,2},{4,5},{5,4},{6,7},{7,6},{8,9},{9,8},{10,11... | collective-permute-start | bytes 4128776 | tf_op jit(solution)/shard_map/ppermute | solution.py:20
  39.4 11.8 %copy-start.8 = (bf16[192,3584]{1,0:T(8,128)(2,1)}, bf16[192,3584]{1,0:T(8,128)(2,1)S(1)}, u32[]{:S(2)}) copy-start(bf16[192,3584]{1,0:T(8,128)(2,1)S(1)} %collective-permute-done.5.s_mate) | copy-start | bytes 4128772
  39.4 35.0 %collective-permute-start.1 = (bf16[192,3584]{1,0:T(8,128)(2,1)}, bf16[192,3584]{1,0:T(8,128)(2,1)}, u32[]{:S(2)}, u32[]{:S(2)}) collective-permute-start(bf16[192,3584]{1,0:T(8,128)(2,1)} %t.5), channel_id=1, source_target_pairs={{2,6},{3,7},{4,0},{5,1},{6,10},{7,11},{8,4},{9,5},{10,14},{11,15},... | collective-permute-start | bytes 4128776 | tf_op jit(solution)/shard_map/ppermute | solution.py:20
  40.7 10.5 %copy-start = (bf16[192,3584]{1,0:T(8,128)(2,1)}, bf16[192,3584]{1,0:T(8,128)(2,1)S(1)}, u32[]{:S(2)}) copy-start(bf16[192,3584]{1,0:T(8,128)(2,1)S(1)} %collective-permute-done.6.x_mate.sx_mate) | copy-start | bytes 4128772
  40.7 36.4 %collective-permute-start.12 = (bf16[192,3584]{1,0:T(8,128)(2,1)S(1)}, bf16[192,3584]{1,0:T(8,128)(2,1)}, u32[]{:S(2)}, u32[]{:S(2)}) collective-permute-start(bf16[192,3584]{1,0:T(8,128)(2,1)S(1)} %collective-permute-done.3.x.sx), channel_id=1, source_target_pairs={{0,4},{1,5},{4,8},{5,9},{6,2},{7,3},{8,12},{9,13},{10,6},{11,7},{1... | collective-permute-start | bytes 4128776 | tf_op jit(solution)/shard_map/ppermute | solution.py:20
  70.3 8.1 %collective-permute-start.8 = (bf16[192,3584]{1,0:T(8,128)(2,1)}, bf16[192,3584]{1,0:T(8,128)(2,1)}, u32[]{:S(2)}, u32[]{:S(2)}) collective-permute-start(bf16[192,3584]{1,0:T(8,128)(2,1)} %collective-permute-done.4.x.tx), channel_id=1, source_target_pairs={{0,1},{1,0},{2,3},{3,2},{4,5},{5,4},{6,7},{7,6},{8,9},{9,8},{10,11... | collective-permute-start | bytes 4128776 | tf_op jit(solution)/shard_map/ppermute | solution.py:20
  70.3 18.7 %copy-start.5 = (bf16[192,3584]{1,0:T(8,128)(2,1)S(1)}, bf16[192,3584]{1,0:T(8,128)(2,1)}, u32[]{:S(2)}) copy-start(bf16[192,3584]{1,0:T(8,128)(2,1)} %s.3) | copy-start | bytes 4128772
  70.4 18.7 %copy-start.9 = (bf16[192,3584]{1,0:T(8,128)(2,1)S(1)}, bf16[192,3584]{1,0:T(8,128)(2,1)}, u32[]{:S(2)}) copy-start(bf16[192,3584]{1,0:T(8,128)(2,1)} %copy-done.8) | copy-start | bytes 4128772
  74.4 18.5 %collective-permute-start.14 = (bf16[192,3584]{1,0:T(8,128)(2,1)}, bf16[192,3584]{1,0:T(8,128)(2,1)S(1)}, u32[]{:S(2)}, u32[]{:S(2)}) collective-permute-start(bf16[192,3584]{1,0:T(8,128)(2,1)} %collective-permute-done.1.f.tf), channel_id=1, source_target_pairs={{0,1},{3,2},{4,5},{7,6},{8,9},{11,10},{12,13},{15,14},{16,17},{19,... | collective-permute-start | bytes 4128776 | tf_op jit(solution)/shard_map/ppermute | solution.py:20
  75.8 22.2 %collective-permute-start.11 = (bf16[192,3584]{1,0:T(8,128)(2,1)}, bf16[192,3584]{1,0:T(8,128)(2,1)S(1)}, u32[]{:S(2)}, u32[]{:S(2)}) collective-permute-start(bf16[192,3584]{1,0:T(8,128)(2,1)} %copy-done.6), channel_id=1, source_target_pairs={{1,0},{2,3},{5,4},{6,7},{9,8},{10,11},{13,12},{14,15},{17,16},{18,... | collective-permute-start | bytes 4128776 | tf_op jit(solution)/shard_map/ppermute | solution.py:20
  77.2 20.9 %collective-permute-start.13 = (bf16[192,3584]{1,0:T(8,128)(2,1)}, bf16[192,3584]{1,0:T(8,128)(2,1)S(1)}, u32[]{:S(2)}, u32[]{:S(2)}) collective-permute-start(bf16[192,3584]{1,0:T(8,128)(2,1)} %collective-permute-done.12.c), channel_id=1, source_target_pairs={{0,1},{1,0},{2,3},{3,2},{4,5},{5,4},{6,7},{7,6},{8,9},{9,8},{10,11... | collective-permute-start | bytes 4128776 | tf_op jit(solution)/shard_map/ppermute | solution.py:20
  80.8 8.2 %copy-start.11 = (bf16[192,3584]{1,0:T(8,128)(2,1)S(1)}, bf16[192,3584]{1,0:T(8,128)(2,1)}, u32[]{:S(2)}) copy-start(bf16[192,3584]{1,0:T(8,128)(2,1)} %t.5) | copy-start | bytes 4128772
  85.2 7.7 %copy-start.1 = (bf16[192,3584]{1,0:T(8,128)(2,1)S(1)}, bf16[192,3584]{1,0:T(8,128)(2,1)}, u32[]{:S(2)}) copy-start(bf16[192,3584]{1,0:T(8,128)(2,1)} %copy-done) | copy-start | bytes 4128772
  85.2 7.7 %copy-start.3 = (bf16[192,3584]{1,0:T(8,128)(2,1)S(1)}, bf16[192,3584]{1,0:T(8,128)(2,1)}, u32[]{:S(2)}) copy-start(bf16[192,3584]{1,0:T(8,128)(2,1)} %copy-done.2) | copy-start | bytes 4128772
  85.2 12.8 %collective-permute-start.9 = (bf16[192,768]{1,0:T(8,128)(2,1)S(1)}, bf16[192,768]{1,0:T(8,128)(2,1)S(1)}, u32[]{:S(2)}, u32[]{:S(2)}) collective-permute-start(bf16[192,768]{1,0:T(8,128)(2,1)S(1)} %send_gap.1), channel_id=1, source_target_pairs={{0,4},{1,5},{4,8},{5,9},{6,2},{7,3},{8,12},{9,13},{10,6},{11,7},{1... | collective-permute-start | bytes 884744 | tf_op jit(solution)/shard_map/ppermute | solution.py:20
  92.9 5.1 %copy-start.7 = (bf16[192,3584]{1,0:T(8,128)(2,1)S(1)}, bf16[192,3584]{1,0:T(8,128)(2,1)}, u32[]{:S(2)}) copy-start(bf16[192,3584]{1,0:T(8,128)(2,1)} %copy-done.6) | copy-start | bytes 4128772
  (5 other events, 7.7 us)

commit v3 on v2

--- a/solution.py
+++ b/solution.py
@@ -40,18 +40,6 @@
     return i ^ 1
 
 
-def outer(i):
-    return (i % 2) ^ odd_chip(i)
-
-
-def swap_to_outer(i):
-    return None if outer(i) else i ^ 1
-
-
-def swap_to_inner(i):
-    return i ^ 1 if outer(i) else None
-
-
 def after(block, *others):
     return lax.optimization_barrier((block, *others))[0]
 
@@ -74,7 +62,7 @@
     return width
 
 
-def call(kernel, ins, outs, scratch, flops, name):
+def call(kernel, ins, outs, scratch, flops, name, alias=None):
     nbytes = sum(x.size * x.dtype.itemsize for x in ins) + sum(math.prod(o.shape) * o.dtype.itemsize for o in outs)
     spec = pl.BlockSpec(memory_space=pltpu.VMEM)
     return pl.pallas_call(
@@ -85,6 +73,7 @@
         scratch_shapes=scratch,
         cost_estimate=pl.CostEstimate(flops=int(flops), bytes_accessed=int(nbytes), transcendentals=0),
         compiler_params=pltpu.CompilerParams(vmem_limit_bytes=VMEM_BYTES),
+        input_output_aliases=alias or {},
         name=name,
     )(*ins)
 
@@ -125,52 +114,78 @@
         (s, t, s_mate, t_mate),
         [jax.ShapeDtypeStruct((rows, width), jnp.float32), jax.ShapeDtypeStruct((rows, LANES), jnp.float32)],
         [pltpu.VMEM((rows, 2 * rows), jnp.bfloat16)],
-        512 * rows * rows * width,
+        12 * rows * rows * width,
         "own_part",
     )
 
 
-def student_grams_kernel(s, s_mate, x, x_mate, f, f_mate, mine, out):
+def student_grams_kernel(s, s_mate, x, x_mate, f, mine, out):
     def store_mine(at, value):
         mine[:, at] = value
 
     def store_out(at, value):
         out[:, at] = value
 
-    grams(s, (x, x_mate, f, f_mate), store_mine)
+    grams(s, (x, x_mate, f), store_mine)
     grams(f, (s, s_mate, x, x_mate), store_out)
 
 
 def student_grams(*blocks):
     rows, width = blocks[0].shape
-    shape = jax.ShapeDtypeStruct((rows, 4 * rows), jnp.float32)
-    return call(student_grams_kernel, blocks, [shape, shape], [], 16 * rows * rows * width, "student_grams")
-
-
-def send_gap_kernel(f, t, t_mate, x, x_mate, student, factors, out):
+    shapes = [jax.ShapeDtypeStruct((rows, n * rows), jnp.float32) for n in (3, 4)]
+    return call(student_grams_kernel, blocks, shapes, [], 14 * rows * rows * width, "student_grams")
+
+
+def send_direct_kernel(f, t, t_mate, student, factors, out, cross):
     def store(at, value):
-        out[:, at] = ((student[:, at] - value) * factors[:, at]).astype(jnp.bfloat16)
-
-    grams(f, (t, t_mate, x, x_mate), store)
-
-
-def send_gap(f, t, t_mate, x, x_mate, student, factors):
+        g = ((student[:, at] - value) * factors[:, at]).astype(jnp.bfloat16)
+        out[:, at] = g
+        if at.start:
+            cross[...] = g
+
+    grams(f, (t, t_mate), store)
+
+
+def send_direct(f, t, t_mate, student, factors):
     rows, width = f.shape
     return call(
-        send_gap_kernel,
-        (f, t, t_mate, x, x_mate, student, factors),
+        send_direct_kernel,
+        (f, t, t_mate, student, factors),
+        [jax.ShapeDtypeStruct((rows, 4 * rows), jnp.bfloat16), jax.ShapeDtypeStruct((rows, rows), jnp.bfloat16)],
+        [],
+        4 * rows * rows * width,
+        "send_direct",
+    )
+
+
+def send_diag_kernel(scale, f, x, x_mate, student, direct, out):
+    rows = f.shape[0]
+    out[:, : 2 * rows] = direct[:, : 2 * rows]
+    for j, other in enumerate((x, x_mate)):
+        at = slice((j + 2) * rows, (j + 3) * rows)
+        out[:, at] = ((student[:, at] - gram(f[...], other[...])) * scale).astype(jnp.bfloat16)
+
+
+def send_diag(f, x, x_mate, student, direct, scale):
+    rows, width = f.shape
+    return call(
+        functools.partial(send_diag_kernel, scale),
+        (f, x, x_mate, student, direct),
         [jax.ShapeDtypeStruct((rows, 4 * rows), jnp.bfloat16)],
         [],
-        512 * rows * rows * width,
-        "send_gap",
+        4 * rows * rows * width,
+        "send_diag",
     )[0]
 
 
-def near_kernel(scale, t, tx, tx_mate, tf, tf_mate, student, sx, sx_mate, sf, sf_mate, grad_in, sums_in, grad, sums, gap_b):
+def near_kernel(scale, t, tx, tx_mate, tf, student, cross, sx, sx_mate, sf, sf_mate, grad_in, sums_in, grad, sums, gap_b):
+    rows = t.shape[0]
+
     def store(at, value):
         gap_b[:, at] = ((student[:, at] - value) * scale).astype(jnp.bfloat16)
 
-    grams(t, (tx, tx_mate, tf, tf_mate), store)
+    grams(t, (tx, tx_mate, tf), store)
+    gap_b[:, 3 * rows :] = cross[...].astype(jnp.float32).T.astype(jnp.bfloat16)
     wide = gap_b[...].astype(jnp.float32)
     sums[...] = sums_in[...] + lane_sums(wide * wide)
 
@@ -180,37 +195,51 @@
     weigh(gap_b, (sx, sx_mate, sf, sf_mate), put)
 
 
-def near_part(t, tx, tx_mate, tf, tf_mate, student, sx, sx_mate, sf, sf_mate, grad_in, sums_in, scale):
+def near_part(t, tx, tx_mate, tf, student, cross, sx, sx_mate, sf, sf_mate, grad_in, sums_in, scale):
     rows, width = t.shape
     return call(
         functools.partial(near_kernel, scale),
-        (t, tx, tx_mate, tf, tf_mate, student, sx, sx_mate, sf, sf_mate, grad_in, sums_in),
+        (t, tx, tx_mate, tf, student, cross, sx, sx_mate, sf, sf_mate, grad_in, sums_in),
         [jax.ShapeDtypeStruct((rows, width), jnp.float32), jax.ShapeDtypeStruct((rows, LANES), jnp.float32)],
         [pltpu.VMEM((rows, 4 * rows), jnp.bfloat16)],
-        16 * rows * rows * width,
+        14 * rows * rows * width,
         "near_part",
-    )
-
-
-def last_kernel(scale, gap_b, a, b, c, d, grad_in, sums_in, grad, sums):
-    def put(at, value):
-        grad[:, at] = ((grad_in[:, at] + value) * scale).astype(grad.dtype)
-
-    weigh(gap_b, (a, b, c, d), put)
+        {10: 0, 11: 1},
+    )
+
+
+def last_kernel(scale, weight, gap_b, a, b, c, d, grad_in, sums_in, grad, sums, held, sems):
+    width = a.shape[1]
+    tile = columns(width)
+    copies = []
     wide = gap_b[...].astype(jnp.float32)
-    sums[...] = sums_in[...] + lane_sums(wide * wide)
-
-
-def last_part(gap_b, a, b, c, d, grad_in, sums_in, scale):
+    total = sums_in[...] + lane_sums(wide * wide)
+    sums[...] = jnp.sum(total.T, axis=0, keepdims=True) * weight
+    for k in range(width // tile):
+        at = slice(k * tile, (k + 1) * tile)
+        stack = jnp.concatenate([other[:, at] for other in (a, b, c, d)], axis=0)
+        value = jnp.dot(gap_b[...], stack, preferred_element_type=jnp.float32)
+        held[:, at] = ((grad_in[:, at] + value) * scale).astype(grad.dtype)
+        copy = pltpu.make_async_copy(held.at[:, at], grad.at[:, at], sems.at[k])
+        copy.start()
+        copies.append(copy)
+    for copy in copies:
+        copy.wait()
+
+
+def last_part(gap_b, a, b, c, d, grad_in, sums_in, scale, weight):
     rows, width = a.shape
-    return call(
-        functools.partial(last_kernel, scale),
-        (gap_b, a, b, c, d, grad_in, sums_in),
-        [jax.ShapeDtypeStruct((rows, width), jnp.bfloat16), jax.ShapeDtypeStruct((rows, LANES), jnp.float32)],
-        [],
-        8 * rows * rows * width,
-        "last_part",
-    )
+    spec = pl.BlockSpec(memory_space=pltpu.VMEM)
+    return pl.pallas_call(
+        functools.partial(last_kernel, scale, weight),
+        in_specs=[spec] * 7,
+        out_specs=[pl.BlockSpec(memory_space=pl.ANY), spec],
+        out_shape=[jax.ShapeDtypeStruct((rows, width), jnp.bfloat16), jax.ShapeDtypeStruct((1, rows), jnp.float32)],
+        scratch_shapes=[pltpu.VMEM((rows, width), jnp.bfloat16), pltpu.SemaphoreType.DMA((width // columns(width),))],
+        cost_estimate=pl.CostEstimate(flops=8 * rows * rows * width, bytes_accessed=16 * rows * width, transcendentals=0),
+        compiler_params=pltpu.CompilerParams(vmem_limit_bytes=VMEM_BYTES),
+        name="last_part",
+    )(gap_b, a, b, c, d, grad_in, sums_in)
 
 
 def body(student, teacher):
@@ -232,22 +261,23 @@
     s_diag = move(after(s_side, s_back), light)
 
     grad, sums = own_part(student, teacher, s_mate, t_mate, scale)
-    s_side_mate = move(s_side, swap)
-    s_far_mate = move(s_far, swap_to_outer)
-    s_back_mate = move(after(s_back, s_side_mate, s_far_mate), swap_to_inner)
-    mine, out = student_grams(student, s_mate, s_side, s_side_mate, s_far, s_far_mate)
-
-    t_side_mate = move(after(t_side, out), swap)
-    t_far_mate = move(after(t_far, out), swap_to_outer)
-    s_diag_mate = move(s_diag, swap)
-    out_gap = send_gap(t_far, teacher, t_mate, t_side, t_side_mate, out, factors)
+    s_side_mate = move(after(s_side, sums), swap)
+    mine, out = student_grams(student, s_mate, s_side, s_side_mate, s_far)
+
+    t_side_mate = move(after(t_side, out, t_far), swap)
+    direct, cross = send_direct(t_far, teacher, t_mate, out, factors)
+    out_gap = send_diag(t_far, t_side, t_side_mate, out, after(direct, s_diag), scale)
+    cross_mate = move(cross, swap)
+    s_diag_mate = move(after(s_diag, out_gap), swap)
+    s_back_mate = move(after(s_back, out_gap), swap)
+    s_far_mate = move(after(s_far, out_gap), swap)
     in_gap = move(out_gap, light)
     grad, sums = near_part(
-        teacher, t_side, t_side_mate, t_far, t_far_mate, mine,
+        teacher, t_side, t_side_mate, t_far, mine, cross_mate,
         s_side, s_side_mate, s_far, s_far_mate, grad, sums, scale,
     )
-    grad, sums = last_part(in_gap, s_back, s_back_mate, s_diag, s_diag_mate, grad, sums, 1.0 / math.sqrt(window))
-    return grad, jnp.sum(sums, axis=1) / window
+    grad, sums = last_part(in_gap, s_back, s_back_mate, s_diag, s_diag_mate, grad, sums, 1.0 / math.sqrt(window), 1.0 / window)
+    return grad, sums.reshape(rows)
 
 
 def solution(mesh):

time: 103 us -> 95.4 us (0.926)
  waiting for transfers between devices: 50.1 us -> 44.8 us
  starting transfers between devices: 26.1 us -> 22.7 us
  Pallas kernels: 20 us -> 21.6 us
    ppermute x15, waiting for transfers between devices: 50.1 us -> 44.8 us  [move(): return lax.ppermute(block, AXIS, route)]
    pallas_call x0 -> x1, Pallas kernels: none -> 3.89 us  [last_part(): pl.pallas_call(functools.partial(last_kernel, scale, weight), in_specs=[s...]
    ppermute x15, starting transfers between devices: 26.1 us -> 22.7 us  [move(): return lax.ppermute(block, AXIS, route)]
    pallas_call x5, Pallas kernels: 20 us -> 17.7 us  [call(): pl.pallas_call(kernel, in_specs=[spec] * len(ins), out_specs=[spec] * len...]
    unnamed x28 -> x26, local copies, waits for them, and re-layouts: 4.59 us -> 5 us
  transfers between devices with their start and end apart: 15 -> 15, of which waited for: 4 -> 5; matrix products, arithmetic and copies ran while one was open for 0% -> 0% of each run, Pallas kernels for 16% -> 16%
where the time goes in v3:
time: 95.4 us; the launch traced here: 95 us
  waiting for transfers between devices  44.8 us (47%)
  starting transfers between devices  22.7 us (24%)
  Pallas kernels  21.6 us (23%)
  local copies, waits for them, and re-layouts  5 us (5%)
    ppermute x15, waiting for transfers between devices, move(): return lax.ppermute(block, AXIS, route)  44.8 us
    ppermute x15, starting transfers between devices, move(): return lax.ppermute(block, AXIS, route)  22.7 us
    pallas_call x5, Pallas kernels, call(): pl.pallas_call(kernel, in_specs=[spec] * len(ins), out_specs=[spec] * len...  17.7 us
    unnamed x26, local copies, waits for them, and re-layouts  5 us
    pallas_call x1, Pallas kernels, last_part(): pl.pallas_call(functools.partial(last_kernel, scale, weight), in_specs=[s...  3.89 us
  transfers between devices with their start and end apart: 15, of which 5 were waited for; matrix products, arithmetic and copies ran while one was open for 0% of the time, Pallas kernels for 16%

profile of v3, /device:TPU:0, one launch (start us, length us, event | category | flops | bytes accessed | tf_op | source)
XLA Modules:
  0.0 95.0 jit_solution(8715628879357549210)
XLA Ops:
  0.6 0.5 collective-permute-start.4
  1.2 2.9 %collective-permute-start.2 = (bf16[192,3584]{1,0:T(8,128)(2,1)}, bf16[192,3584]{1,0:T(8,128)(2,1)S(1)}, u32[]{:S(2)}, u32[]{:S(2)}) collective-permute-start(bf16[192,3584]{1,0:T(8,128)(2,1)} %s.3), channel_id=1, source_target_pairs={{0,2},{1,3},{2,0},{3,1},{4,6},{5,7},{6,4},{7,5},{8,10},{9,11},{10,... | collective-permute-start | bytes 4128776 | tf_op jit(solution)/shard_map/ppermute | solution.py:20
  4.1 1.3 %collective-permute-start = (bf16[192,3584]{1,0:T(8,128)(2,1)}, bf16[192,3584]{1,0:T(8,128)(2,1)S(1)}, u32[]{:S(2)}, u32[]{:S(2)}) collective-permute-start(bf16[192,3584]{1,0:T(8,128)(2,1)} %s.3), channel_id=1, source_target_pairs={{2,6},{3,7},{4,0},{5,1},{6,10},{7,11},{8,4},{9,5},{10,14},{11,15},... | collective-permute-start | bytes 4128776 | tf_op jit(solution)/shard_map/ppermute | solution.py:20
  5.4 4.6 %collective-permute-start.8 = (bf16[192,3584]{1,0:T(8,128)(2,1)}, bf16[192,3584]{1,0:T(8,128)(2,1)S(1)}, u32[]{:S(2)}, u32[]{:S(2)}) collective-permute-start(bf16[192,3584]{1,0:T(8,128)(2,1)} %s.3), channel_id=1, source_target_pairs={{0,4},{1,5},{4,8},{5,9},{6,2},{7,3},{8,12},{9,13},{10,6},{11,7},{1... | collective-permute-start | bytes 4128776 | tf_op jit(solution)/shard_map/ppermute | solution.py:20
  10.1 1.3 %copy-done.6 = bf16[192,3584]{1,0:T(8,128)(2,1)S(1)} copy-done((bf16[192,3584]{1,0:T(8,128)(2,1)S(1)}, bf16[192,3584]{1,0:T(8,128)(2,1)}, u32[]{:S(2)}) %copy-start.6) | copy-done | bytes 1376280
  11.4 4.3 %own_part.1 = (f32[192,3584]{1,0:T(8,128)S(1)}, f32[192,128]{1,0:T(8,128)S(1)}) custom-call(bf16[192,3584]{1,0:T(8,128)(2,1)S(1)} %copy-done.6, bf16[192,3584]{1,0:T(8,128)(2,1)} %t.5, bf16[192,3584]{1,0:T(8,128)(2,1)S(1)} %collective-permute-done.4.s_mate, bf16[192,3584]{1,0:T(8,128)(2,1)S(1)} %collective-permute-done.5.t_mate), custom_call_target="tpu_custom_call" | custom-call | flops 1585446912 | bytes 8355840 | tf_op jit(solution)/shard_map/own_part/pallas_call | solution.py:68
  15.8 1.5 %copy-done = f32[192,3584]{1,0:T(8,128)} copy-done((f32[192,3584]{1,0:T(8,128)}, f32[192,3584]{1,0:T(8,128)S(1)}, u32[]{:S(2)}) %copy-start) | copy-done | bytes 2752536
  17.3 17.5 %collective-permute-done.2.x.sx = bf16[192,3584]{1,0:T(8,128)(2,1)S(1)} collective-permute-done((bf16[192,3584]{1,0:T(8,128)(2,1)}, bf16[192,3584]{1,0:T(8,128)(2,1)S(1)}, u32[]{:S(2)}, u32[]{:S(2)}) %collective-permute-start.2) | collective-permute-done | bytes 1376288 | tf_op jit(solution)/shard_map/ppermute | solution.py:20
  34.8 3.3 %collective-permute-done.f.sf = bf16[192,3584]{1,0:T(8,128)(2,1)S(1)} collective-permute-done((bf16[192,3584]{1,0:T(8,128)(2,1)}, bf16[192,3584]{1,0:T(8,128)(2,1)S(1)}, u32[]{:S(2)}, u32[]{:S(2)}) %collective-permute-start) | collective-permute-done | bytes 1376288 | tf_op jit(solution)/shard_map/ppermute | solution.py:20
  38.1 1.3 %collective-permute-start.1 = (bf16[192,3584]{1,0:T(8,128)(2,1)}, bf16[192,3584]{1,0:T(8,128)(2,1)S(1)}, u32[]{:S(2)}, u32[]{:S(2)}) collective-permute-start(bf16[192,3584]{1,0:T(8,128)(2,1)} %t.5), channel_id=1, source_target_pairs={{2,6},{3,7},{4,0},{5,1},{6,10},{7,11},{8,4},{9,5},{10,14},{11,15},... | collective-permute-start | bytes 4128776 | tf_op jit(solution)/shard_map/ppermute | solution.py:20
  39.4 2.9 %collective-permute-start.3 = (bf16[192,3584]{1,0:T(8,128)(2,1)}, bf16[192,3584]{1,0:T(8,128)(2,1)}, u32[]{:S(2)}, u32[]{:S(2)}) collective-permute-start(bf16[192,3584]{1,0:T(8,128)(2,1)} %t.5), channel_id=1, source_target_pairs={{0,2},{1,3},{2,0},{3,1},{4,6},{5,7},{6,4},{7,5},{8,10},{9,11},{10,... | collective-permute-start | bytes 4128776 | tf_op jit(solution)/shard_map/ppermute | solution.py:20
  42.3 4.5 %collective-permute-start.9 = (bf16[192,3584]{1,0:T(8,128)(2,1)S(1)}, bf16[192,3584]{1,0:T(8,128)(2,1)}, u32[]{:S(2)}, u32[]{:S(2)}) collective-permute-start(bf16[192,3584]{1,0:T(8,128)(2,1)S(1)} %collective-permute-done.2.x.sx), channel_id=1, source_target_pairs={{0,4},{1,5},{4,8},{5,9},{6,2},{7,3},{8,12},{9,13},{10,6},{11,7},{1... | collective-permute-start | bytes 4128776 | tf_op jit(solution)/shard_map/ppermute | solution.py:20
  46.8 2.7 %student_grams.1 = (f32[192,576]{1,0:T(8,128)S(1)}, f32[192,768]{1,0:T(8,128)S(1)}) custom-call(bf16[192,3584]{1,0:T(8,128)(2,1)S(1)} %copy-done.6, bf16[192,3584]{1,0:T(8,128)(2,1)S(1)} %collective-permute-done.4.s_mate, bf16[192,3584]{1,0:T(8,128)(2,1)S(1)} %collective-permute-done.2.x.sx, bf16[192,3584]{1,0:T(8,128)(2,1)S(1)} %collective-permute-done.6.x_mate.sx_mate, ...), custom_call_target="tpu_custom_call" | custom-call | flops 1849688064 | bytes 7913472 | tf_op jit(solution)/shard_map/student_grams/pallas_call | solution.py:68
  49.6 0.8 copy-done.11
  50.4 20.9 %collective-permute-done.1.f.tf = bf16[192,3584]{1,0:T(8,128)(2,1)S(1)} collective-permute-done((bf16[192,3584]{1,0:T(8,128)(2,1)}, bf16[192,3584]{1,0:T(8,128)(2,1)S(1)}, u32[]{:S(2)}, u32[]{:S(2)}) %collective-permute-start.1) | collective-permute-done | bytes 1376288 | tf_op jit(solution)/shard_map/ppermute | solution.py:20
  71.6 1.3 %copy-done.8 = bf16[192,3584]{1,0:T(8,128)(2,1)S(1)} copy-done((bf16[192,3584]{1,0:T(8,128)(2,1)S(1)}, bf16[192,3584]{1,0:T(8,128)(2,1)}, u32[]{:S(2)}) %copy-start.8) | copy-done | bytes 1376280
  73.0 2.5 %send_direct.1 = (bf16[192,768]{1,0:T(8,128)(2,1)S(1)}, bf16[192,192]{1,0:T(8,128)(2,1)S(1)}) custom-call(bf16[192,3584]{1,0:T(8,128)(2,1)S(1)} %collective-permute-done.1.f.tf, bf16[192,3584]{1,0:T(8,128)(2,1)} %t.5, bf16[192,3584]{1,0:T(8,128)(2,1)S(1)} %copy-done.8, f32[192,768]{1,0:T(8,128)S(1)} %get-tuple-element.25.student, ...), custom_call_target="tpu_custom_call" | custom-call | flops 528482304 | bytes 5090304 | tf_op jit(solution)/shard_map/send_direct/pallas_call | solution.py:68
  75.5 2.9 %send_diag.1 = bf16[192,768]{1,0:T(8,128)(2,1)S(1)} custom-call(bf16[192,3584]{1,0:T(8,128)(2,1)S(1)} %collective-permute-done.1.f.tf, bf16[192,3584]{1,0:T(8,128)(2,1)} %collective-permute-done.3.x.tx, bf16[192,3584]{1,0:T(8,128)(2,1)} %collective-permute-done.7.x_mate.tx_mate, f32[192,768]{1,0:T(8,128)S(1)} %get-tuple-element.25.student, ...), custom_call_target="tpu_custom_call" | custom-call | flops 528482304 | bytes 5308416 | tf_op jit(solution)/shard_map/send_diag/pallas_call | solution.py:68
  78.4 0.6 collective-permute-start.14
  79.1 0.4 collective-permute-start.11
  79.5 3.5 %collective-permute-start.10 = (bf16[192,768]{1,0:T(8,128)(2,1)S(1)}, bf16[192,768]{1,0:T(8,128)(2,1)S(1)}, u32[]{:S(2)}, u32[]{:S(2)}) collective-permute-start(bf16[192,768]{1,0:T(8,128)(2,1)S(1)} %send_diag.1), channel_id=1, source_target_pairs={{0,4},{1,5},{4,8},{5,9},{6,2},{7,3},{8,12},{9,13},{10,6},{11,7},{1... | collective-permute-start | bytes 884744 | tf_op jit(solution)/shard_map/ppermute | solution.py:20
  83.1 2.8 %collective-permute-done.13.cross = bf16[192,192]{1,0:T(8,128)(2,1)S(1)} collective-permute-done((bf16[192,192]{1,0:T(8,128)(2,1)S(1)}, bf16[192,192]{1,0:T(8,128)(2,1)S(1)}, u32[]{:S(2)}, u32[]{:S(2)}) %collective-permute-start.13) | collective-permute-done | bytes 73760 | tf_op jit(solution)/shard_map/ppermute | solution.py:20
  85.8 5.3 %near_part.1 = (f32[192,3584]{1,0:T(8,128)S(1)}, f32[192,128]{1,0:T(8,128)S(1)}) custom-call(bf16[192,3584]{1,0:T(8,128)(2,1)} %t.5, bf16[192,3584]{1,0:T(8,128)(2,1)} %collective-permute-done.3.x.tx, bf16[192,3584]{1,0:T(8,128)(2,1)} %collective-permute-done.7.x_mate.tx_mate, ...), custom_call_target="tpu_custom_call", output_to_operand_aliasing={{0}: (10, {}), {1}: (11, {})} | custom-call | flops 1849688064 | bytes 17227776 | tf_op jit(solution)/shard_map/near_part/pallas_call | solution.py:68
  91.2 3.9 %last_part.1 = (bf16[192,3584]{1,0:T(8,128)(2,1)}, f32[1,192]{1,0:T(1,128)}) custom-call(bf16[192,768]{1,0:T(8,128)(2,1)S(1)} %collective-permute-done.10.gap_b, bf16[192,3584]{1,0:T(8,128)(2,1)S(1)} %copy-done.10, bf16[192,3584]{1,0:T(8,128)(2,1)S(1)} %collective-permute-done.11.b, bf16[192,3584]{1,0:T(8,128)(2,1)} %collective-permute-done.9.c, ...), custom_call_target="tpu_custom_call" | custom-call | flops 1056964608 | bytes 11010048 | tf_op jit(solution)/shard_map/last_part/pallas_call | solution.py:233
  (39 shorter events, 0.7 us)
Async XLA Ops:
  0.6 9.4 %collective-permute-start.4 = (bf16[192,3584]{1,0:T(8,128)(2,1)}, bf16[192,3584]{1,0:T(8,128)(2,1)S(1)}, u32[]{:S(2)}, u32[]{:S(2)}) collective-permute-start(bf16[192,3584]{1,0:T(8,128)(2,1)} %s.3), channel_id=1, source_target_pairs={{0,1},{1,0},{2,3},{3,2},{4,5},{5,4},{6,7},{7,6},{8,9},{9,8},{10,11... | collective-permute-start | bytes 4128776 | tf_op jit(solution)/shard_map/ppermute | solution.py:20
  1.1 8.9 %collective-permute-start.5 = (bf16[192,3584]{1,0:T(8,128)(2,1)}, bf16[192,3584]{1,0:T(8,128)(2,1)S(1)}, u32[]{:S(2)}, u32[]{:S(2)}) collective-permute-start(bf16[192,3584]{1,0:T(8,128)(2,1)} %t.5), channel_id=1, source_target_pairs={{0,1},{1,0},{2,3},{3,2},{4,5},{5,4},{6,7},{7,6},{8,9},{9,8},{10,11... | collective-permute-start | bytes 4128776 | tf_op jit(solution)/shard_map/ppermute | solution.py:20
  1.2 33.5 %collective-permute-start.2 = (bf16[192,3584]{1,0:T(8,128)(2,1)}, bf16[192,3584]{1,0:T(8,128)(2,1)S(1)}, u32[]{:S(2)}, u32[]{:S(2)}) collective-permute-start(bf16[192,3584]{1,0:T(8,128)(2,1)} %s.3), channel_id=1, source_target_pairs={{0,2},{1,3},{2,0},{3,1},{4,6},{5,7},{6,4},{7,5},{8,10},{9,11},{10,... | collective-permute-start | bytes 4128776 | tf_op jit(solution)/shard_map/ppermute | solution.py:20
  4.1 34.0 %collective-permute-start = (bf16[192,3584]{1,0:T(8,128)(2,1)}, bf16[192,3584]{1,0:T(8,128)(2,1)S(1)}, u32[]{:S(2)}, u32[]{:S(2)}) collective-permute-start(bf16[192,3584]{1,0:T(8,128)(2,1)} %s.3), channel_id=1, source_target_pairs={{2,6},{3,7},{4,0},{5,1},{6,10},{7,11},{8,4},{9,5},{10,14},{11,15},... | collective-permute-start | bytes 4128776 | tf_op jit(solution)/shard_map/ppermute | solution.py:20
  5.4 36.9 %collective-permute-start.8 = (bf16[192,3584]{1,0:T(8,128)(2,1)}, bf16[192,3584]{1,0:T(8,128)(2,1)S(1)}, u32[]{:S(2)}, u32[]{:S(2)}) collective-permute-start(bf16[192,3584]{1,0:T(8,128)(2,1)} %s.3), channel_id=1, source_target_pairs={{0,4},{1,5},{4,8},{5,9},{6,2},{7,3},{8,12},{9,13},{10,6},{11,7},{1... | collective-permute-start | bytes 4128776 | tf_op jit(solution)/shard_map/ppermute | solution.py:20
  11.4 4.3 %copy-start.7 = (bf16[192,3584]{1,0:T(8,128)(2,1)}, bf16[192,3584]{1,0:T(8,128)(2,1)S(1)}, u32[]{:S(2)}) copy-start(bf16[192,3584]{1,0:T(8,128)(2,1)S(1)} %collective-permute-done.5.t_mate) | copy-start | bytes 4128772
  34.8 12.0 %collective-permute-start.6 = (bf16[192,3584]{1,0:T(8,128)(2,1)S(1)}, bf16[192,3584]{1,0:T(8,128)(2,1)S(1)}, u32[]{:S(2)}, u32[]{:S(2)}) collective-permute-start(bf16[192,3584]{1,0:T(8,128)(2,1)S(1)} %collective-permute-done.2.x.sx), channel_id=1, source_target_pairs={{0,1},{1,0},{2,3},{3,2},{4,5},{5,4},{6,7},{7,6},{8,9},{9,8},{10,11... | collective-permute-start | bytes 4128776 | tf_op jit(solution)/shard_map/ppermute | solution.py:20
  38.1 11.4 %copy-start.2 = (bf16[192,3584]{1,0:T(8,128)(2,1)}, bf16[192,3584]{1,0:T(8,128)(2,1)S(1)}, u32[]{:S(2)}) copy-start(bf16[192,3584]{1,0:T(8,128)(2,1)S(1)} %collective-permute-done.f.sf) | copy-start | bytes 4128772
  38.1 33.1 %collective-permute-start.1 = (bf16[192,3584]{1,0:T(8,128)(2,1)}, bf16[192,3584]{1,0:T(8,128)(2,1)S(1)}, u32[]{:S(2)}, u32[]{:S(2)}) collective-permute-start(bf16[192,3584]{1,0:T(8,128)(2,1)} %t.5), channel_id=1, source_target_pairs={{2,6},{3,7},{4,0},{5,1},{6,10},{7,11},{8,4},{9,5},{10,14},{11,15},... | collective-permute-start | bytes 4128776 | tf_op jit(solution)/shard_map/ppermute | solution.py:20
  39.4 32.2 %collective-permute-start.3 = (bf16[192,3584]{1,0:T(8,128)(2,1)}, bf16[192,3584]{1,0:T(8,128)(2,1)}, u32[]{:S(2)}, u32[]{:S(2)}) collective-permute-start(bf16[192,3584]{1,0:T(8,128)(2,1)} %t.5), channel_id=1, source_target_pairs={{0,2},{1,3},{2,0},{3,1},{4,6},{5,7},{6,4},{7,5},{8,10},{9,11},{10,... | collective-permute-start | bytes 4128776 | tf_op jit(solution)/shard_map/ppermute | solution.py:20
  42.3 7.3 %copy-start.9 = (bf16[192,3584]{1,0:T(8,128)(2,1)}, bf16[192,3584]{1,0:T(8,128)(2,1)S(1)}, u32[]{:S(2)}) copy-start(bf16[192,3584]{1,0:T(8,128)(2,1)S(1)} %collective-permute-done.8.a) | copy-start | bytes 4128772
  42.3 33.2 %collective-permute-start.9 = (bf16[192,3584]{1,0:T(8,128)(2,1)S(1)}, bf16[192,3584]{1,0:T(8,128)(2,1)}, u32[]{:S(2)}, u32[]{:S(2)}) collective-permute-start(bf16[192,3584]{1,0:T(8,128)(2,1)S(1)} %collective-permute-done.2.x.sx), channel_id=1, source_target_pairs={{0,4},{1,5},{4,8},{5,9},{6,2},{7,3},{8,12},{9,13},{10,6},{11,7},{1... | collective-permute-start | bytes 4128776 | tf_op jit(solution)/shard_map/ppermute | solution.py:20
  46.8 2.8 %copy-start.4 = (bf16[192,3584]{1,0:T(8,128)(2,1)}, bf16[192,3584]{1,0:T(8,128)(2,1)S(1)}, u32[]{:S(2)}) copy-start(bf16[192,3584]{1,0:T(8,128)(2,1)S(1)} %collective-permute-done.6.x_mate.sx_mate) | copy-start | bytes 4128772
  71.6 3.9 %collective-permute-start.7 = (bf16[192,3584]{1,0:T(8,128)(2,1)}, bf16[192,3584]{1,0:T(8,128)(2,1)}, u32[]{:S(2)}, u32[]{:S(2)}) collective-permute-start(bf16[192,3584]{1,0:T(8,128)(2,1)} %collective-permute-done.3.x.tx), channel_id=1, source_target_pairs={{0,1},{1,0},{2,3},{3,2},{4,5},{5,4},{6,7},{7,6},{8,9},{9,8},{10,11... | collective-permute-start | bytes 4128776 | tf_op jit(solution)/shard_map/ppermute | solution.py:20
  72.9 6.1 %copy-start.10 = (bf16[192,3584]{1,0:T(8,128)(2,1)S(1)}, bf16[192,3584]{1,0:T(8,128)(2,1)}, u32[]{:S(2)}) copy-start(bf16[192,3584]{1,0:T(8,128)(2,1)} %copy-done.9) | copy-start | bytes 4128772
  73.0 12.9 %copy-start.5 = (bf16[192,3584]{1,0:T(8,128)(2,1)S(1)}, bf16[192,3584]{1,0:T(8,128)(2,1)}, u32[]{:S(2)}) copy-start(bf16[192,3584]{1,0:T(8,128)(2,1)} %copy-done.4) | copy-start | bytes 4128772
  75.5 2.9 %copy-start.3 = (bf16[192,3584]{1,0:T(8,128)(2,1)S(1)}, bf16[192,3584]{1,0:T(8,128)(2,1)}, u32[]{:S(2)}) copy-start(bf16[192,3584]{1,0:T(8,128)(2,1)} %copy-done.2) | copy-start | bytes 4128772
  75.5 10.3 %copy-start.1 = (f32[192,3584]{1,0:T(8,128)S(1)}, f32[192,3584]{1,0:T(8,128)}, u32[]{:S(2)}) copy-start(f32[192,3584]{1,0:T(8,128)} %copy-done) | copy-start | bytes 8257540
  75.5 10.3 %copy-start.12 = (f32[192,576]{1,0:T(8,128)S(1)}, f32[192,576]{1,0:T(8,128)}, u32[]{:S(2)}) copy-start(f32[192,576]{1,0:T(8,128)} %copy-done.11) | copy-start | bytes 1327108
  78.4 7.4 %collective-permute-start.14 = (bf16[192,3584]{1,0:T(8,128)(2,1)S(1)}, bf16[192,3584]{1,0:T(8,128)(2,1)S(1)}, u32[]{:S(2)}, u32[]{:S(2)}) collective-permute-start(bf16[192,3584]{1,0:T(8,128)(2,1)S(1)} %copy-done.3), channel_id=1, source_target_pairs={{0,1},{1,0},{2,3},{3,2},{4,5},{5,4},{6,7},{7,6},{8,9},{9,8},{10,11... | collective-permute-start | bytes 4128776 | tf_op jit(solution)/shard_map/ppermute | solution.py:20
  79.0 12.2 %collective-permute-start.12 = (bf16[192,3584]{1,0:T(8,128)(2,1)}, bf16[192,3584]{1,0:T(8,128)(2,1)S(1)}, u32[]{:S(2)}, u32[]{:S(2)}) collective-permute-start(bf16[192,3584]{1,0:T(8,128)(2,1)} %collective-permute-done.9.c), channel_id=1, source_target_pairs={{0,1},{1,0},{2,3},{3,2},{4,5},{5,4},{6,7},{7,6},{8,9},{9,8},{10,11... | collective-permute-start | bytes 4128776 | tf_op jit(solution)/shard_map/ppermute | solution.py:20
  79.1 12.1 %collective-permute-start.11 = (bf16[192,3584]{1,0:T(8,128)(2,1)S(1)}, bf16[192,3584]{1,0:T(8,128)(2,1)S(1)}, u32[]{:S(2)}, u32[]{:S(2)}) collective-permute-start(bf16[192,3584]{1,0:T(8,128)(2,1)S(1)} %copy-done.10), channel_id=1, source_target_pairs={{0,1},{1,0},{2,3},{3,2},{4,5},{5,4},{6,7},{7,6},{8,9},{9,8},{10,11... | collective-permute-start | bytes 4128776 | tf_op jit(solution)/shard_map/ppermute | solution.py:20
  79.5 11.6 %collective-permute-start.10 = (bf16[192,768]{1,0:T(8,128)(2,1)S(1)}, bf16[192,768]{1,0:T(8,128)(2,1)S(1)}, u32[]{:S(2)}, u32[]{:S(2)}) collective-permute-start(bf16[192,768]{1,0:T(8,128)(2,1)S(1)} %send_diag.1), channel_id=1, source_target_pairs={{0,4},{1,5},{4,8},{5,9},{6,2},{7,3},{8,12},{9,13},{10,6},{11,7},{1... | collective-permute-start | bytes 884744 | tf_op jit(solution)/shard_map/ppermute | solution.py:20
  83.0 2.8 %collective-permute-start.13 = (bf16[192,192]{1,0:T(8,128)(2,1)S(1)}, bf16[192,192]{1,0:T(8,128)(2,1)S(1)}, u32[]{:S(2)}, u32[]{:S(2)}) collective-permute-start(bf16[192,192]{1,0:T(8,128)(2,1)S(1)} %get-tuple-element.33), channel_id=1, source_target_pairs={{0,1},{1,0},{2,3},{3,2},{4,5},{5,4},{6,7},{7,6},{8,9},{9,8},{10,11... | collective-permute-start | bytes 221192 | tf_op jit(solution)/shard_map/ppermute | solution.py:20
  (4 other events, 5.0 us)

commit v4 on v3

v4 whole, which is shorter than its diff:
```python
import functools
import math

import jax
import jax.numpy as jnp
from jax import lax
from jax.experimental import pallas as pl
from jax.experimental.pallas import tpu as pltpu
from jax.sharding import PartitionSpec as P

REACH = 4
AXIS = "blk"
LANES = 128
VMEM_BYTES = 9 * 1024 * 1024


def move(block, target):
    devices = range(lax.axis_size(AXIS))
    route = [(i, target(i)) for i in devices if target(i) is not None and target(i) in devices]
    return lax.ppermute(block, AXIS, route)


def odd_chip(i):
    return (i // 2) % 2


def partner(i):
    return i ^ 2


def heavy(i):
    return i + 4 if odd_chip(i) else i - 4


def light(i):
    return i - 4 if odd_chip(i) else i + 4


def swap(i):
    return i ^ 1


def after(block, *others):
    return lax.optimization_barrier((block, *others))[0]


def gram(a, b):
    return lax.dot_general(a, b, (((1,), (1,)), ((), ())), preferred_element_type=jnp.float32)


def lane_sums(x):
    total = x[:, :LANES]
    for k in range(1, x.shape[1] // LANES):
        total = total + x[:, k * LANES : (k + 1) * LANES]
    return total


def columns(width):
    for tile in (512, 384, 256, 128):
        if width % tile == 0:
            return tile
    return width


def call(kernel, ins, outs, scratch, flops, name, alias=None, streamed=()):
    nbytes = sum(x.size * x.dtype.itemsize for x in ins) + sum(math.prod(o.shape) * o.dtype.itemsize for o in outs)
    spec = pl.BlockSpec(memory_space=pltpu.VMEM)
    far = pl.BlockSpec(memory_space=pltpu.HBM)
    return pl.pallas_call(
        kernel,
        in_specs=[far if j in streamed else spec for j in range(len(ins))],
        out_specs=[spec] * len(outs),
        out_shape=outs,
        scratch_shapes=scratch,
        cost_estimate=pl.CostEstimate(flops=int(flops), bytes_accessed=int(nbytes), transcendentals=0),
        compiler_params=pltpu.CompilerParams(vmem_limit_bytes=VMEM_BYTES),
        input_output_aliases=alias or {},
        name=name,
    )(*ins)


def fetch(source, target, sems, tile):
    copies = []
    for k in range(source.shape[1] // tile):
        at = slice(k * tile, (k + 1) * tile)
        copies.append(pltpu.make_async_copy(source.at[:, at], target.at[:, at], sems.at[k]))
        copies[-1].start()
    return copies


def grams(rows_of, others, store):
    rows = rows_of.shape[0]
    for j, other in enumerate(others):
        store(slice(j * rows, (j + 1) * rows), gram(rows_of[...], other[...]))


def weigh(gap_b, others, put):
    width = others[0].shape[1]
    tile = columns(width)
    for k in range(width // tile):
        at = slice(k * tile, (k + 1) * tile)
        stack = jnp.concatenate([other[:, at] for other in others], axis=0)
        put(at, jnp.dot(gap_b[...], stack, preferred_element_type=jnp.float32))


def own_kernel(scale, s, t, s_mate, t_mate, grad, sums, gap_b):
    rows = s.shape[0]
    for j, (os, ot) in enumerate(((s, t), (s_mate, t_mate))):
        g = (gram(s[...], os[...]) - gram(t[...], ot[...])) * scale
        gap_b[:, j * rows : (j + 1) * rows] = g.astype(jnp.bfloat16)
    wide = gap_b[...].astype(jnp.float32)
    sums[...] = lane_sums(wide * wide)

    def put(at, value):
        grad[:, at] = value

    weigh(gap_b, (s, s_mate), put)


def own_part(s, t, s_mate, t_mate, scale):
    rows, width = s.shape
    return call(
        functools.partial(own_kernel, scale),
        (s, t, s_mate, t_mate),
        [jax.ShapeDtypeStruct((rows, width), jnp.float32), jax.ShapeDtypeStruct((rows, LANES), jnp.float32)],
        [pltpu.VMEM((rows, 2 * rows), jnp.bfloat16)],
        12 * rows * rows * width,
        "own_part",
    )


def student_grams_kernel(s, s_mate, x, f, mine, out):
    def store_mine(at, value):
        mine[:, at] = value

    def store_out(at, value):
        out[:, at] = value

    grams(s, (x, f), store_mine)
    grams(f, (s, s_mate, x), store_out)


def student_grams(*blocks):
    rows, width = blocks[0].shape
    shapes = [jax.ShapeDtypeStruct((rows, n * rows), jnp.float32) for n in (2, 3)]
    return call(student_grams_kernel, blocks, shapes, [], 10 * rows * rows * width, "student_grams")


def stage_kernel(*refs):
    *blocks, out, sems = refs
    rows = blocks[0].shape[0]
    copies = [
        pltpu.make_async_copy(block, out.at[j * rows : (j + 1) * rows], sems.at[j]) for j, block in enumerate(blocks)
    ]
    for copy in copies:
        copy.start()
    for copy in copies:
        copy.wait()


def stage(*blocks):
    rows, width = blocks[0].shape
    count = len(blocks)
    return call(
        stage_kernel, blocks, [jax.ShapeDtypeStruct((count * rows, width), jnp.bfloat16)],
        [pltpu.SemaphoreType.DMA((count,))], 0, "stage", streamed=tuple(range(count)),
    )[0]


def send_direct_kernel(f, three, student, factors, out, cross):
    rows = f.shape[0]
    g = ((student[...] - gram(f[...], three[...])) * factors[...]).astype(jnp.bfloat16)
    out[:, : 3 * rows] = g
    cross[...] = g[:, rows : 2 * rows]


def send_direct(f, three, student, factors):
    rows, width = f.shape
    return call(
        send_direct_kernel,
        (f, three, student, factors),
        [jax.ShapeDtypeStruct((rows, 4 * rows), jnp.bfloat16), jax.ShapeDtypeStruct((rows, rows), jnp.bfloat16)],
        [],
        6 * rows * rows * width,
        "send_direct",
    )


def send_diag_kernel(scale, f, tf, x_mate, tx_mate, direct, out):
    rows = f.shape[0]
    out[:, : 3 * rows] = direct[:, : 3 * rows]
    g = gram(f[...], x_mate[...]) - gram(tf[...], tx_mate[...])
    out[:, 3 * rows :] = (g * scale).astype(jnp.bfloat16)


def send_diag(f, tf, x_mate, tx_mate, direct, scale):
    rows, width = f.shape
    return call(
        functools.partial(send_diag_kernel, scale),
        (f, tf, x_mate, tx_mate, direct),
        [jax.ShapeDtypeStruct((rows, 4 * rows), jnp.bfloat16)],
        [],
        4 * rows * rows * width,
        "send_diag",
    )[0]


def near_kernel(
    scale, s, three, tx_mate, tf, student, cross, sx, sx_mate, sf, sf_mate, grad_in, sums_in, far,
    grad, sums, near, gap_b, sem
):
    rows = s.shape[0]
    copy = pltpu.make_async_copy(far, near, sem)
    copy.start()
    t, tx = three.at[:rows], three.at[2 * rows :]
    blocks = (
        student[:, :rows] - gram(t[...], tx[...]),
        gram(s[...], sx_mate[...]) - gram(t[...], tx_mate[...]),
        student[:, rows:] - gram(t[...], tf[...]),
    )
    for j, block in enumerate(blocks):
        gap_b[:, j * rows : (j + 1) * rows] = (block * scale).astype(jnp.bfloat16)
    gap_b[:, 3 * rows :] = cross[...].astype(jnp.float32).T.astype(jnp.bfloat16)
    wide = gap_b[...].astype(jnp.float32)
    sums[...] = sums_in[...] + lane_sums(wide * wide)

    def put(at, value):
        grad[:, at] = grad_in[:, at] + value

    weigh(gap_b, (sx, sx_mate, sf, sf_mate), put)
    copy.wait()


def near_part(s, three, tx_mate, tf, student, cross, sx, sx_mate, sf, sf_mate, grad_in, sums_in, far, scale):
    rows, width = s.shape
    return call(
        functools.partial(near_kernel, scale),
        (s, three, tx_mate, tf, student, cross, sx, sx_mate, sf, sf_mate, grad_in, sums_in, far),
        [
            jax.ShapeDtypeStruct((rows, width), jnp.float32),
            jax.ShapeDtypeStruct((rows, LANES), jnp.float32),
            jax.ShapeDtypeStruct((rows, width), jnp.bfloat16),
        ],
        [pltpu.VMEM((rows, 4 * rows), jnp.bfloat16), pltpu.SemaphoreType.DMA],
        16 * rows * rows * width,
        "near_part",
        {10: 0, 11: 1},
        streamed=(12,),
    )


def last_kernel(scale, weight, gap_b, a, b, c, d, grad_in, sums_in, grad, sums):
    def put(at, value):
        grad[:, at] = ((grad_in[:, at] + value) * scale).astype(grad.dtype)

    weigh(gap_b, (a, b, c, d), put)
    wide = gap_b[...].astype(jnp.float32)
    total = sums_in[...] + lane_sums(wide * wide)
    sums[...] = jnp.sum(total.T, axis=0, keepdims=True) * weight


def last_part(gap_b, a, b, c, d, grad_in, sums_in, scale, weight):
    rows, width = a.shape
    return call(
        functools.partial(last_kernel, scale, weight),
        (gap_b, a, b, c, d, grad_in, sums_in),
        [jax.ShapeDtypeStruct((rows, width), jnp.bfloat16), jax.ShapeDtypeStruct((1, rows), jnp.float32)],
        [],
        8 * rows * rows * width,
        "last_part",
    )


def body(student, teacher):
    rows, width = student.shape
    window = (2 * REACH + 1) * rows
    scale = 1.0 / math.sqrt(width)
    index = lax.axis_index(AXIS)
    inner = (1 - ((index % 2) ^ ((index // 2) % 2))).astype(jnp.float32)
    lane = lax.broadcasted_iota(jnp.int32, (1, 3 * rows), 1)
    factors = jnp.where((lane >= rows) & (lane < 2 * rows), scale * inner, scale)

    s_side = move(student, partner)
    s_far = move(student, heavy)
    s_back = move(student, light)
    s_mate = move(student, swap)
    t_mate = move(teacher, swap)
    grad, sums = own_part(student, teacher, s_mate, t_mate, scale)
    t_next = after(teacher, sums)
    t_side = move(t_next, partner)
    t_far = move(t_next, heavy)
    s_diag = move(after(s_side, s_back), light)
    mine, out = student_grams(student, s_mate, s_side, s_far)

    s_side_mate = move(after(s_side, out, t_side), swap)
    t_side_mate = move(after(t_side, out), swap)
    three = stage(teacher, t_mate, t_side)
    direct, cross = send_direct(t_far, three, out, factors)
    cross_mate = move(cross, swap)
    out_gap = send_diag(s_far, t_far, s_side_mate, t_side_mate, after(direct, cross_mate, s_diag), scale)
    s_far_mate = move(after(s_far, out_gap), swap)
    s_diag_mate = move(after(s_diag, out_gap), swap)
    s_back_mate = move(after(s_back, out_gap), swap)
    in_gap = move(out_gap, light)
    grad, sums, s_diag = near_part(
        student, three, t_side_mate, t_far, mine, cross_mate, s_side, s_side_mate, s_far, s_far_mate, grad, sums,
        s_diag, scale,
    )
    grad, sums = last_part(in_gap, s_back, s_back_mate, s_diag, s_diag_mate, grad, sums, 1.0 / math.sqrt(window), 1.0 / window)
    return grad, sums.reshape(rows)


def solution(mesh):
    return jax.shard_map(
        body,
        mesh=mesh,
        in_specs=(P(("parts", "blk"), None), P(("parts", "blk"), None)),
        out_specs=(P(("parts", "blk"), None), P(("parts", "blk"))),
        check_vma=False,
    )
```

time: 95.4 us -> 91.1 us (0.955)
  waiting for transfers between devices: 44.8 us -> 41 us
    ppermute x15, waiting for transfers between devices: 44.8 us -> 41 us  [move(): return lax.ppermute(block, AXIS, route)]
    pallas_call x6 -> x7, Pallas kernels: 21.6 us -> 21.8 us  [call(): pl.pallas_call(kernel, in_specs=[far if j in streamed else spec for j in...]
    unnamed x26 -> x22, local copies, waits for them, and re-layouts: 5 us -> 4.93 us
  transfers between devices with their start and end apart: 15 -> 15, of which waited for: 5 -> 6; matrix products, arithmetic and copies ran while one was open for 0% -> 0% of each run, Pallas kernels for 16% -> 18%
where the time goes in v4:
time: 91.1 us; the launch traced here: 90.6 us
  waiting for transfers between devices  41 us (45%)
  starting transfers between devices  22 us (24%)
  Pallas kernels  21.8 us (24%)
  local copies, waits for them, and re-layouts  4.93 us (5%)
    ppermute x15, waiting for transfers between devices, move(): return lax.ppermute(block, AXIS, route)  41 us
    ppermute x15, starting transfers between devices, move(): return lax.ppermute(block, AXIS, route)  22 us
    pallas_call x7, Pallas kernels, call(): pl.pallas_call(kernel, in_specs=[far if j in streamed else spec for j in...  21.8 us
    unnamed x22, local copies, waits for them, and re-layouts  4.93 us
  transfers between devices with their start and end apart: 15, of which 6 were waited for; matrix products, arithmetic and copies ran while one was open for 0% of the time, Pallas kernels for 18%

profile of v4, /device:TPU:0, one launch (start us, length us, event | category | flops | bytes accessed | tf_op | source)
XLA Modules:
  0.0 90.6 jit_solution(10361323871253962409)
XLA Ops:
  0.6 0.5 collective-permute-start.1
  1.2 1.3 %collective-permute-start = (bf16[192,3584]{1,0:T(8,128)(2,1)}, bf16[192,3584]{1,0:T(8,128)(2,1)S(1)}, u32[]{:S(2)}, u32[]{:S(2)}) collective-permute-start(bf16[192,3584]{1,0:T(8,128)(2,1)} %s.5), channel_id=1, source_target_pairs={{2,6},{3,7},{4,0},{5,1},{6,10},{7,11},{8,4},{9,5},{10,14},{11,15},... | collective-permute-start | bytes 4128776 | tf_op jit(solution)/shard_map/ppermute | solution.py:20
  2.5 5.3 %collective-permute-start.4 = (bf16[192,3584]{1,0:T(8,128)(2,1)}, bf16[192,3584]{1,0:T(8,128)(2,1)}, u32[]{:S(2)}, u32[]{:S(2)}) collective-permute-start(bf16[192,3584]{1,0:T(8,128)(2,1)} %s.5), channel_id=1, source_target_pairs={{0,2},{1,3},{2,0},{3,1},{4,6},{5,7},{6,4},{7,5},{8,10},{9,11},{10,... | collective-permute-start | bytes 4128776 | tf_op jit(solution)/shard_map/ppermute | solution.py:20
  7.8 3.5 %collective-permute-start.9 = (bf16[192,3584]{1,0:T(8,128)(2,1)}, bf16[192,3584]{1,0:T(8,128)(2,1)S(1)}, u32[]{:S(2)}, u32[]{:S(2)}) collective-permute-start(bf16[192,3584]{1,0:T(8,128)(2,1)} %s.5), channel_id=1, source_target_pairs={{0,4},{1,5},{4,8},{5,9},{6,2},{7,3},{8,12},{9,13},{10,6},{11,7},{1... | collective-permute-start | bytes 4128776 | tf_op jit(solution)/shard_map/ppermute | solution.py:20
  11.3 1.3 %copy-done.2 = bf16[192,3584]{1,0:T(8,128)(2,1)S(1)} copy-done((bf16[192,3584]{1,0:T(8,128)(2,1)S(1)}, bf16[192,3584]{1,0:T(8,128)(2,1)}, u32[]{:S(2)}) %copy-start.2) | copy-done | bytes 1376280
  12.6 4.4 %own_part.1 = (f32[192,3584]{1,0:T(8,128)S(1)}, f32[192,128]{1,0:T(8,128)S(1)}) custom-call(bf16[192,3584]{1,0:T(8,128)(2,1)S(1)} %copy-done.2, bf16[192,3584]{1,0:T(8,128)(2,1)} %refs_0_.1, bf16[192,3584]{1,0:T(8,128)(2,1)S(1)} %collective-permute-done.1.s_mate, bf16[192,3584]{1,0:T(8,128)(2,1)S(1)} %collective-permute-done.2.t_mate.refs_1_), custom_call_target="tpu_custom_call" | custom-call | flops 1585446912 | bytes 8355840 | tf_op jit(solution)/shard_map/own_part/pallas_call | solution.py:69
  17.0 1.5 %copy-done = f32[192,3584]{1,0:T(8,128)} copy-done((f32[192,3584]{1,0:T(8,128)}, f32[192,3584]{1,0:T(8,128)S(1)}, u32[]{:S(2)}) %copy-start) | copy-done | bytes 2752536
  18.5 1.3 %collective-permute-start.3 = (bf16[192,3584]{1,0:T(8,128)(2,1)}, bf16[192,3584]{1,0:T(8,128)(2,1)S(1)}, u32[]{:S(2)}, u32[]{:S(2)}) collective-permute-start(bf16[192,3584]{1,0:T(8,128)(2,1)} %refs_0_.1), channel_id=1, source_target_pairs={{2,6},{3,7},{4,0},{5,1},{6,10},{7,11},{8,4},{9,5},{10,14},{11,15},... | collective-permute-start | bytes 4128776 | tf_op jit(solution)/shard_map/ppermute | solution.py:20
  19.8 19.3 %collective-permute-done.4.x.sx = bf16[192,3584]{1,0:T(8,128)(2,1)} collective-permute-done((bf16[192,3584]{1,0:T(8,128)(2,1)}, bf16[192,3584]{1,0:T(8,128)(2,1)}, u32[]{:S(2)}, u32[]{:S(2)}) %collective-permute-start.4) | collective-permute-done | bytes 1376288 | tf_op jit(solution)/shard_map/ppermute | solution.py:20
  39.1 1.5 %collective-permute-done.9.a = bf16[192,3584]{1,0:T(8,128)(2,1)S(1)} collective-permute-done((bf16[192,3584]{1,0:T(8,128)(2,1)}, bf16[192,3584]{1,0:T(8,128)(2,1)S(1)}, u32[]{:S(2)}, u32[]{:S(2)}) %collective-permute-start.9) | collective-permute-done | bytes 1376288 | tf_op jit(solution)/shard_map/ppermute | solution.py:20
  40.6 5.4 %collective-permute-start.10 = (bf16[192,3584]{1,0:T(8,128)(2,1)}, bf16[192,3584]{1,0:T(8,128)(2,1)}, u32[]{:S(2)}, u32[]{:S(2)}) collective-permute-start(bf16[192,3584]{1,0:T(8,128)(2,1)} %collective-permute-done.4.x.sx), channel_id=1, source_target_pairs={{0,4},{1,5},{4,8},{5,9},{6,2},{7,3},{8,12},{9,13},{10,6},{11,7},{1... | collective-permute-start | bytes 4128776 | tf_op jit(solution)/shard_map/ppermute | solution.py:20
  46.0 3.4 %student_grams.1 = (f32[192,384]{1,0:T(8,128)S(1)}, f32[192,576]{1,0:T(8,128)S(1)}) custom-call(bf16[192,3584]{1,0:T(8,128)(2,1)S(1)} %copy-done.3, bf16[192,3584]{1,0:T(8,128)(2,1)S(1)} %collective-permute-done.1.s_mate, bf16[192,3584]{1,0:T(8,128)(2,1)} %collective-permute-done.4.x.sx, bf16[192,3584]{1,0:T(8,128)(2,1)S(1)} %collective-permute-done.f.sf), custom_call_target="tpu_custom_call" | custom-call | flops 1321205760 | bytes 6242304 | tf_op jit(solution)/shard_map/student_grams/pallas_call | solution.py:69
  49.4 0.7 copy-done.9
  50.1 17.6 %collective-permute-done.5.refs_2_ = bf16[192,3584]{1,0:T(8,128)(2,1)} collective-permute-done((bf16[192,3584]{1,0:T(8,128)(2,1)}, bf16[192,3584]{1,0:T(8,128)(2,1)}, u32[]{:S(2)}, u32[]{:S(2)}) %collective-permute-start.5) | collective-permute-done | bytes 1376288 | tf_op jit(solution)/shard_map/ppermute | solution.py:20
  67.7 0.5 collective-permute-start.7
  68.3 1.3 %copy-done.8 = bf16[192,3584]{1,0:T(8,128)(2,1)S(1)} copy-done((bf16[192,3584]{1,0:T(8,128)(2,1)S(1)}, bf16[192,3584]{1,0:T(8,128)(2,1)}, u32[]{:S(2)}) %copy-start.8) | copy-done | bytes 1376280
  69.6 1.8 %stage.1.three = bf16[576,3584]{1,0:T(8,128)(2,1)S(1)} custom-call(bf16[192,3584]{1,0:T(8,128)(2,1)} %refs_0_.1, bf16[192,3584]{1,0:T(8,128)(2,1)S(1)} %copy-done.8, bf16[192,3584]{1,0:T(8,128)(2,1)} %collective-permute-done.5.refs_2_), custom_call_target="tpu_custom_call" | custom-call | bytes 8257536 | tf_op jit(solution)/shard_map/stage/pallas_call | solution.py:69
  71.4 1.7 %send_direct.1 = (bf16[192,768]{1,0:T(8,128)(2,1)S(1)}, bf16[192,192]{1,0:T(8,128)(2,1)S(1)}) custom-call(bf16[192,3584]{1,0:T(8,128)(2,1)S(1)} %collective-permute-done.3.f.tf, bf16[576,3584]{1,0:T(8,128)(2,1)S(1)} %stage.1.three, f32[192,576]{1,0:T(8,128)S(1)} %get-tuple-element.23.student, f32[1,576]{1,0:T(1,128)S(1)} %and_select_fusion.factors), custom_call_target="tpu_custom_call" | custom-call | flops 792723456 | bytes 6318336 | tf_op jit(solution)/shard_map/send_direct/pallas_call | solution.py:69
  73.5 1.0 %collective-permute-done.8.cross = bf16[192,192]{1,0:T(8,128)(2,1)S(1)} collective-permute-done((bf16[192,192]{1,0:T(8,128)(2,1)S(1)}, bf16[192,192]{1,0:T(8,128)(2,1)S(1)}, u32[]{:S(2)}, u32[]{:S(2)}) %collective-permute-start.8) | collective-permute-done | bytes 73760 | tf_op jit(solution)/shard_map/ppermute | solution.py:20
  74.5 2.9 %send_diag.1 = bf16[192,768]{1,0:T(8,128)(2,1)S(1)} custom-call(bf16[192,3584]{1,0:T(8,128)(2,1)S(1)} %collective-permute-done.f.sf, bf16[192,3584]{1,0:T(8,128)(2,1)S(1)} %collective-permute-done.3.f.tf, bf16[192,3584]{1,0:T(8,128)(2,1)} %collective-permute-done.6.x_mate.sx_mate, bf16[192,3584]{1,0:T(8,128)(2,1)} %collective-permute-done.7.tx_mate, ...), custom_call_target="tpu_custom_call" | custom-call | flops 528482304 | bytes 6094848 | tf_op jit(solution)/shard_map/send_diag/pallas_call | solution.py:69
  78.1 3.4 %collective-permute-start.11 = (bf16[192,768]{1,0:T(8,128)(2,1)S(1)}, bf16[192,768]{1,0:T(8,128)(2,1)S(1)}, u32[]{:S(2)}, u32[]{:S(2)}) collective-permute-start(bf16[192,768]{1,0:T(8,128)(2,1)S(1)} %send_diag.1), channel_id=1, source_target_pairs={{0,4},{1,5},{4,8},{5,9},{6,2},{7,3},{8,12},{9,13},{10,6},{11,7},{1... | collective-permute-start | bytes 884744 | tf_op jit(solution)/shard_map/ppermute | solution.py:20
  81.6 5.4 %near_part.1 = (f32[192,3584]{1,0:T(8,128)S(1)}, f32[192,128]{1,0:T(8,128)S(1)}, bf16[192,3584]{1,0:T(8,128)(2,1)S(1)}) custom-call(bf16[192,3584]{1,0:T(8,128)(2,1)S(1)} %copy-done.4, bf16[576,3584]{1,0:T(8,128)(2,1)S(1)} %stage.1.three, bf16[192,3584]{1,0:T(8,128)(2,1)} %collective-permute-done.7.tx_mate, ...), custom_call_target="tpu_custom_call", output_to_operand_aliasing={{0}: (10, {}), {1}: (11, {})} | custom-call | flops 2113929216 | bytes 22585344 | tf_op jit(solution)/shard_map/near_part/pallas_call | solution.py:69
  87.0 1.3 %collective-permute-done.11.gap_b = bf16[192,768]{1,0:T(8,128)(2,1)S(1)} collective-permute-done((bf16[192,768]{1,0:T(8,128)(2,1)S(1)}, bf16[192,768]{1,0:T(8,128)(2,1)S(1)}, u32[]{:S(2)}, u32[]{:S(2)}) %collective-permute-start.11) | collective-permute-done | bytes 294944 | tf_op jit(solution)/shard_map/ppermute | solution.py:20
  88.3 2.3 %last_part.1 = (bf16[192,3584]{1,0:T(8,128)(2,1)}, f32[1,192]{1,0:T(1,128)}) custom-call(bf16[192,768]{1,0:T(8,128)(2,1)S(1)} %collective-permute-done.11.gap_b, bf16[192,3584]{1,0:T(8,128)(2,1)S(1)} %copy-done.6, bf16[192,3584]{1,0:T(8,128)(2,1)S(1)} %collective-permute-done.12.b, bf16[192,3584]{1,0:T(8,128)(2,1)S(1)} %get-tuple-element.34.c, ...), custom_call_target="tpu_custom_call" | custom-call | flops 1056964608 | bytes 10027776 | tf_op jit(solution)/shard_map/last_part/pallas_call | solution.py:69
  (36 shorter events, 1.2 us)
Async XLA Ops:
  0.6 10.6 %collective-permute-start.1 = (bf16[192,3584]{1,0:T(8,128)(2,1)}, bf16[192,3584]{1,0:T(8,128)(2,1)S(1)}, u32[]{:S(2)}, u32[]{:S(2)}) collective-permute-start(bf16[192,3584]{1,0:T(8,128)(2,1)} %s.5), channel_id=1, source_target_pairs={{0,1},{1,0},{2,3},{3,2},{4,5},{5,4},{6,7},{7,6},{8,9},{9,8},{10,11... | collective-permute-start | bytes 4128776 | tf_op jit(solution)/shard_map/ppermute | solution.py:20
  1.1 10.1 %collective-permute-start.2 = (bf16[192,3584]{1,0:T(8,128)(2,1)}, bf16[192,3584]{1,0:T(8,128)(2,1)S(1)}, u32[]{:S(2)}, u32[]{:S(2)}) collective-permute-start(bf16[192,3584]{1,0:T(8,128)(2,1)} %refs_0_.1), channel_id=1, source_target_pairs={{0,1},{1,0},{2,3},{3,2},{4,5},{5,4},{6,7},{7,6},{8,9},{9,8},{10,11... | collective-permute-start | bytes 4128776 | tf_op jit(solution)/shard_map/ppermute | solution.py:20
  1.2 44.8 %collective-permute-start = (bf16[192,3584]{1,0:T(8,128)(2,1)}, bf16[192,3584]{1,0:T(8,128)(2,1)S(1)}, u32[]{:S(2)}, u32[]{:S(2)}) collective-permute-start(bf16[192,3584]{1,0:T(8,128)(2,1)} %s.5), channel_id=1, source_target_pairs={{2,6},{3,7},{4,0},{5,1},{6,10},{7,11},{8,4},{9,5},{10,14},{11,15},... | collective-permute-start | bytes 4128776 | tf_op jit(solution)/shard_map/ppermute | solution.py:20
  2.5 36.6 %collective-permute-start.4 = (bf16[192,3584]{1,0:T(8,128)(2,1)}, bf16[192,3584]{1,0:T(8,128)(2,1)}, u32[]{:S(2)}, u32[]{:S(2)}) collective-permute-start(bf16[192,3584]{1,0:T(8,128)(2,1)} %s.5), channel_id=1, source_target_pairs={{0,2},{1,3},{2,0},{3,1},{4,6},{5,7},{6,4},{7,5},{8,10},{9,11},{10,... | collective-permute-start | bytes 4128776 | tf_op jit(solution)/shard_map/ppermute | solution.py:20
  7.8 32.8 %collective-permute-start.9 = (bf16[192,3584]{1,0:T(8,128)(2,1)}, bf16[192,3584]{1,0:T(8,128)(2,1)S(1)}, u32[]{:S(2)}, u32[]{:S(2)}) collective-permute-start(bf16[192,3584]{1,0:T(8,128)(2,1)} %s.5), channel_id=1, source_target_pairs={{0,4},{1,5},{4,8},{5,9},{6,2},{7,3},{8,12},{9,13},{10,6},{11,7},{1... | collective-permute-start | bytes 4128776 | tf_op jit(solution)/shard_map/ppermute | solution.py:20
  11.3 1.3 %copy-start.2 = (bf16[192,3584]{1,0:T(8,128)(2,1)S(1)}, bf16[192,3584]{1,0:T(8,128)(2,1)}, u32[]{:S(2)}) copy-start(bf16[192,3584]{1,0:T(8,128)(2,1)} %s.5) | copy-start | bytes 4128772
  12.6 4.4 %copy-start.7 = (bf16[192,3584]{1,0:T(8,128)(2,1)}, bf16[192,3584]{1,0:T(8,128)(2,1)S(1)}, u32[]{:S(2)}) copy-start(bf16[192,3584]{1,0:T(8,128)(2,1)S(1)} %collective-permute-done.2.t_mate.refs_1_) | copy-start | bytes 4128772
  12.6 33.4 %copy-start.3 = (bf16[192,3584]{1,0:T(8,128)(2,1)S(1)}, bf16[192,3584]{1,0:T(8,128)(2,1)}, u32[]{:S(2)}) copy-start(bf16[192,3584]{1,0:T(8,128)(2,1)} %s.5) | copy-start | bytes 4128772
  17.0 1.5 %copy-start = (f32[192,3584]{1,0:T(8,128)}, f32[192,3584]{1,0:T(8,128)S(1)}, u32[]{:S(2)}) copy-start(f32[192,3584]{1,0:T(8,128)S(1)} %get-tuple-element.33.grad_in) | copy-start | bytes 8257540
  18.5 49.2 %collective-permute-start.5 = (bf16[192,3584]{1,0:T(8,128)(2,1)}, bf16[192,3584]{1,0:T(8,128)(2,1)}, u32[]{:S(2)}, u32[]{:S(2)}) collective-permute-start(bf16[192,3584]{1,0:T(8,128)(2,1)} %refs_0_.1), channel_id=1, source_target_pairs={{0,2},{1,3},{2,0},{3,1},{4,6},{5,7},{6,4},{7,5},{8,10},{9,11},{10,... | collective-permute-start | bytes 4128776 | tf_op jit(solution)/shard_map/ppermute | solution.py:20
  18.5 52.9 %collective-permute-start.3 = (bf16[192,3584]{1,0:T(8,128)(2,1)}, bf16[192,3584]{1,0:T(8,128)(2,1)S(1)}, u32[]{:S(2)}, u32[]{:S(2)}) collective-permute-start(bf16[192,3584]{1,0:T(8,128)(2,1)} %refs_0_.1), channel_id=1, source_target_pairs={{2,6},{3,7},{4,0},{5,1},{6,10},{7,11},{8,4},{9,5},{10,14},{11,15},... | collective-permute-start | bytes 4128776 | tf_op jit(solution)/shard_map/ppermute | solution.py:20
  40.6 8.8 %copy-start.5 = (bf16[192,3584]{1,0:T(8,128)(2,1)}, bf16[192,3584]{1,0:T(8,128)(2,1)S(1)}, u32[]{:S(2)}) copy-start(bf16[192,3584]{1,0:T(8,128)(2,1)S(1)} %collective-permute-done.9.a) | copy-start | bytes 4128772
  40.6 32.9 %collective-permute-start.10 = (bf16[192,3584]{1,0:T(8,128)(2,1)}, bf16[192,3584]{1,0:T(8,128)(2,1)}, u32[]{:S(2)}, u32[]{:S(2)}) collective-permute-start(bf16[192,3584]{1,0:T(8,128)(2,1)} %collective-permute-done.4.x.sx), channel_id=1, source_target_pairs={{0,4},{1,5},{4,8},{5,9},{6,2},{7,3},{8,12},{9,13},{10,6},{11,7},{1... | collective-permute-start | bytes 4128776 | tf_op jit(solution)/shard_map/ppermute | solution.py:20
  67.7 6.8 %collective-permute-start.6 = (bf16[192,3584]{1,0:T(8,128)(2,1)}, bf16[192,3584]{1,0:T(8,128)(2,1)}, u32[]{:S(2)}, u32[]{:S(2)}) collective-permute-start(bf16[192,3584]{1,0:T(8,128)(2,1)} %collective-permute-done.4.x.sx), channel_id=1, source_target_pairs={{0,1},{1,0},{2,3},{3,2},{4,5},{5,4},{6,7},{7,6},{8,9},{9,8},{10,11... | collective-permute-start | bytes 4128776 | tf_op jit(solution)/shard_map/ppermute | solution.py:20
  67.7 6.8 %collective-permute-start.7 = (bf16[192,3584]{1,0:T(8,128)(2,1)}, bf16[192,3584]{1,0:T(8,128)(2,1)}, u32[]{:S(2)}, u32[]{:S(2)}) collective-permute-start(bf16[192,3584]{1,0:T(8,128)(2,1)} %collective-permute-done.5.refs_2_), channel_id=1, source_target_pairs={{0,1},{1,0},{2,3},{3,2},{4,5},{5,4},{6,7},{7,6},{8,9},{9,8},{10,11... | collective-permute-start | bytes 4128776 | tf_op jit(solution)/shard_map/ppermute | solution.py:20
  73.1 1.4 %collective-permute-start.8 = (bf16[192,192]{1,0:T(8,128)(2,1)S(1)}, bf16[192,192]{1,0:T(8,128)(2,1)S(1)}, u32[]{:S(2)}, u32[]{:S(2)}) collective-permute-start(bf16[192,192]{1,0:T(8,128)(2,1)S(1)} %get-tuple-element.27), channel_id=1, source_target_pairs={{0,1},{1,0},{2,3},{3,2},{4,5},{5,4},{6,7},{7,6},{8,9},{9,8},{10,11... | collective-permute-start | bytes 221192 | tf_op jit(solution)/shard_map/ppermute | solution.py:20
  74.5 3.5 %copy-start.6 = (bf16[192,3584]{1,0:T(8,128)(2,1)S(1)}, bf16[192,3584]{1,0:T(8,128)(2,1)}, u32[]{:S(2)}) copy-start(bf16[192,3584]{1,0:T(8,128)(2,1)} %copy-done.5) | copy-start | bytes 4128772
  74.5 7.1 %copy-start.4 = (bf16[192,3584]{1,0:T(8,128)(2,1)S(1)}, bf16[192,3584]{1,0:T(8,128)(2,1)}, u32[]{:S(2)}) copy-start(bf16[192,3584]{1,0:T(8,128)(2,1)} %s.5) | copy-start | bytes 4128772
  74.5 7.1 %copy-start.10 = (f32[192,384]{1,0:T(8,128)S(1)}, f32[192,384]{1,0:T(8,128)}, u32[]{:S(2)}) copy-start(f32[192,384]{1,0:T(8,128)} %copy-done.9) | copy-start | bytes 884740
  74.5 7.1 %copy-start.1 = (f32[192,3584]{1,0:T(8,128)S(1)}, f32[192,3584]{1,0:T(8,128)}, u32[]{:S(2)}) copy-start(f32[192,3584]{1,0:T(8,128)} %copy-done) | copy-start | bytes 8257540
  77.4 4.2 %collective-permute-start.13 = (bf16[192,3584]{1,0:T(8,128)(2,1)S(1)}, bf16[192,3584]{1,0:T(8,128)(2,1)S(1)}, u32[]{:S(2)}, u32[]{:S(2)}) collective-permute-start(bf16[192,3584]{1,0:T(8,128)(2,1)S(1)} %collective-permute-done.f.sf), channel_id=1, source_target_pairs={{0,1},{1,0},{2,3},{3,2},{4,5},{5,4},{6,7},{7,6},{8,9},{9,8},{10,11... | collective-permute-start | bytes 4128776 | tf_op jit(solution)/shard_map/ppermute | solution.py:20
  77.6 10.7 %collective-permute-start.14 = (bf16[192,3584]{1,0:T(8,128)(2,1)}, bf16[192,3584]{1,0:T(8,128)(2,1)S(1)}, u32[]{:S(2)}, u32[]{:S(2)}) collective-permute-start(bf16[192,3584]{1,0:T(8,128)(2,1)} %collective-permute-done.10.far), channel_id=1, source_target_pairs={{0,1},{1,0},{2,3},{3,2},{4,5},{5,4},{6,7},{7,6},{8,9},{9,8},{10,11... | collective-permute-start | bytes 4128776 | tf_op jit(solution)/shard_map/ppermute | solution.py:20
  78.0 10.3 %collective-permute-start.12 = (bf16[192,3584]{1,0:T(8,128)(2,1)S(1)}, bf16[192,3584]{1,0:T(8,128)(2,1)S(1)}, u32[]{:S(2)}, u32[]{:S(2)}) collective-permute-start(bf16[192,3584]{1,0:T(8,128)(2,1)S(1)} %copy-done.6), channel_id=1, source_target_pairs={{0,1},{1,0},{2,3},{3,2},{4,5},{5,4},{6,7},{7,6},{8,9},{9,8},{10,11... | collective-permute-start | bytes 4128776 | tf_op jit(solution)/shard_map/ppermute | solution.py:20
  78.1 10.2 %collective-permute-start.11 = (bf16[192,768]{1,0:T(8,128)(2,1)S(1)}, bf16[192,768]{1,0:T(8,128)(2,1)S(1)}, u32[]{:S(2)}, u32[]{:S(2)}) collective-permute-start(bf16[192,768]{1,0:T(8,128)(2,1)S(1)} %send_diag.1), channel_id=1, source_target_pairs={{0,4},{1,5},{4,8},{5,9},{6,2},{7,3},{8,12},{9,13},{10,6},{11,7},{1... | collective-permute-start | bytes 884744 | tf_op jit(solution)/shard_map/ppermute | solution.py:20
  (2 other events, 2.1 us)

commit v5 on v4

--- a/solution.py
+++ b/solution.py
@@ -62,7 +62,7 @@
     return width
 
 
-def call(kernel, ins, outs, scratch, flops, name, alias=None, streamed=()):
+def call(kernel, ins, outs, scratch, flops, name, alias=None, streamed=(), free=False):
     nbytes = sum(x.size * x.dtype.itemsize for x in ins) + sum(math.prod(o.shape) * o.dtype.itemsize for o in outs)
     spec = pl.BlockSpec(memory_space=pltpu.VMEM)
     far = pl.BlockSpec(memory_space=pltpu.HBM)
@@ -72,7 +72,7 @@
         out_specs=[spec] * len(outs),
         out_shape=outs,
         scratch_shapes=scratch,
-        cost_estimate=pl.CostEstimate(flops=int(flops), bytes_accessed=int(nbytes), transcendentals=0),
+        cost_estimate=pl.CostEstimate(flops=int(flops), bytes_accessed=0 if free else int(nbytes), transcendentals=0),
         compiler_params=pltpu.CompilerParams(vmem_limit_bytes=VMEM_BYTES),
         input_output_aliases=alias or {},
         name=name,
@@ -163,7 +163,7 @@
     count = len(blocks)
     return call(
         stage_kernel, blocks, [jax.ShapeDtypeStruct((count * rows, width), jnp.bfloat16)],
-        [pltpu.SemaphoreType.DMA((count,))], 0, "stage", streamed=tuple(range(count)),
+        [pltpu.SemaphoreType.DMA((count,))], 0, "stage", streamed=tuple(range(count)), free=True,
     )[0]
 
 
@@ -186,18 +186,19 @@
     )
 
 
-def send_diag_kernel(scale, f, tf, x_mate, tx_mate, direct, out):
+def send_diag_kernel(scale, direct, mates, f, tf, out):
     rows = f.shape[0]
+    x_mate, tx_mate = mates.at[:rows], mates.at[rows:]
     out[:, : 3 * rows] = direct[:, : 3 * rows]
     g = gram(f[...], x_mate[...]) - gram(tf[...], tx_mate[...])
     out[:, 3 * rows :] = (g * scale).astype(jnp.bfloat16)
 
 
-def send_diag(f, tf, x_mate, tx_mate, direct, scale):
+def send_diag(direct, mates, f, tf, scale):
     rows, width = f.shape
     return call(
         functools.partial(send_diag_kernel, scale),
-        (f, tf, x_mate, tx_mate, direct),
+        (direct, mates, f, tf),
         [jax.ShapeDtypeStruct((rows, 4 * rows), jnp.bfloat16)],
         [],
         4 * rows * rows * width,
@@ -206,13 +207,14 @@
 
 
 def near_kernel(
-    scale, s, three, tx_mate, tf, student, cross, sx, sx_mate, sf, sf_mate, grad_in, sums_in, far,
+    scale, s, three, mates, tf, student, cross, sx, sf, sf_mate, grad_in, sums_in, far,
     grad, sums, near, gap_b, sem
 ):
     rows = s.shape[0]
     copy = pltpu.make_async_copy(far, near, sem)
     copy.start()
     t, tx = three.at[:rows], three.at[2 * rows :]
+    sx_mate, tx_mate = mates.at[:rows], mates.at[rows:]
     blocks = (
         student[:, :rows] - gram(t[...], tx[...]),
         gram(s[...], sx_mate[...]) - gram(t[...], tx_mate[...]),
@@ -231,11 +233,11 @@
     copy.wait()
 
 
-def near_part(s, three, tx_mate, tf, student, cross, sx, sx_mate, sf, sf_mate, grad_in, sums_in, far, scale):
+def near_part(s, three, mates, tf, student, cross, sx, sf, sf_mate, grad_in, sums_in, far, scale):
     rows, width = s.shape
     return call(
         functools.partial(near_kernel, scale),
-        (s, three, tx_mate, tf, student, cross, sx, sx_mate, sf, sf_mate, grad_in, sums_in, far),
+        (s, three, mates, tf, student, cross, sx, sf, sf_mate, grad_in, sums_in, far),
         [
             jax.ShapeDtypeStruct((rows, width), jnp.float32),
             jax.ShapeDtypeStruct((rows, LANES), jnp.float32),
@@ -244,8 +246,8 @@
         [pltpu.VMEM((rows, 4 * rows), jnp.bfloat16), pltpu.SemaphoreType.DMA],
         16 * rows * rows * width,
         "near_part",
-        {10: 0, 11: 1},
-        streamed=(12,),
+        {9: 0, 10: 1},
+        streamed=(11,),
     )
 
 
@@ -297,13 +299,15 @@
     three = stage(teacher, t_mate, t_side)
     direct, cross = send_direct(t_far, three, out, factors)
     cross_mate = move(cross, swap)
-    out_gap = send_diag(s_far, t_far, s_side_mate, t_side_mate, after(direct, cross_mate, s_diag), scale)
+    mates = stage(s_side_mate, t_side_mate)
+    _, direct, cross_mate = lax.optimization_barrier((s_diag, direct, cross_mate))
+    out_gap = send_diag(direct, mates, s_far, t_far, scale)
     s_far_mate = move(after(s_far, out_gap), swap)
     s_diag_mate = move(after(s_diag, out_gap), swap)
     s_back_mate = move(after(s_back, out_gap), swap)
     in_gap = move(out_gap, light)
     grad, sums, s_diag = near_part(
-        student, three, t_side_mate, t_far, mine, cross_mate, s_side, s_side_mate, s_far, s_far_mate, grad, sums,
+        student, three, mates, t_far, mine, cross_mate, s_side, s_far, s_far_mate, grad, sums,
         s_diag, scale,
     )
     grad, sums = last_part(in_gap, s_back, s_back_mate, s_diag, s_diag_mate, grad, sums, 1.0 / math.sqrt(window), 1.0 / window)

time: 91.1 us -> 89.8 us (0.986)
  Pallas kernels: 21.8 us -> 20.7 us
    pallas_call x7 -> x8, Pallas kernels: 21.8 us -> 20.7 us  [call(): pl.pallas_call(kernel, in_specs=[far if j in streamed else spec for j in...]
  transfers between devices with their start and end apart: 15 -> 15, of which waited for: 6 -> 5; matrix products, arithmetic and copies ran while one was open for 0% -> 0% of each run, Pallas kernels for 18% -> 18%
where the time goes in v5:
time: 89.8 us; the launch traced here: 89.3 us
  waiting for transfers between devices  40.9 us (46%)
  starting transfers between devices  21.9 us (24%)
  Pallas kernels  20.7 us (23%)
  local copies, waits for them, and re-layouts  4.94 us (6%)
    ppermute x15, waiting for transfers between devices, move(): return lax.ppermute(block, AXIS, route)  40.9 us
    ppermute x15, starting transfers between devices, move(): return lax.ppermute(block, AXIS, route)  21.9 us
    pallas_call x8, Pallas kernels, call(): pl.pallas_call(kernel, in_specs=[far if j in streamed else spec for j in...  20.7 us
    unnamed x22, local copies, waits for them, and re-layouts  4.94 us
  transfers between devices with their start and end apart: 15, of which 5 were waited for; matrix products, arithmetic and copies ran while one was open for 0% of the time, Pallas kernels for 18%

profile of v5, /device:TPU:0, one launch (start us, length us, event | category | flops | bytes accessed | tf_op | source)
XLA Modules:
  0.0 89.3 jit_solution(4038281476394118482)
XLA Ops:
  0.6 0.5 collective-permute-start.3
  1.2 2.9 %collective-permute-start = (bf16[192,3584]{1,0:T(8,128)(2,1)}, bf16[192,3584]{1,0:T(8,128)(2,1)}, u32[]{:S(2)}, u32[]{:S(2)}) collective-permute-start(bf16[192,3584]{1,0:T(8,128)(2,1)} %s.5), channel_id=1, source_target_pairs={{0,2},{1,3},{2,0},{3,1},{4,6},{5,7},{6,4},{7,5},{8,10},{9,11},{10,... | collective-permute-start | bytes 4128776 | tf_op jit(solution)/shard_map/ppermute | solution.py:20
  4.1 1.3 %collective-permute-start.7 = (bf16[192,3584]{1,0:T(8,128)(2,1)}, bf16[192,3584]{1,0:T(8,128)(2,1)S(1)}, u32[]{:S(2)}, u32[]{:S(2)}) collective-permute-start(bf16[192,3584]{1,0:T(8,128)(2,1)} %s.5), channel_id=1, source_target_pairs={{2,6},{3,7},{4,0},{5,1},{6,10},{7,11},{8,4},{9,5},{10,14},{11,15},... | collective-permute-start | bytes 4128776 | tf_op jit(solution)/shard_map/ppermute | solution.py:20
  5.4 4.6 %collective-permute-start.1 = (bf16[192,3584]{1,0:T(8,128)(2,1)}, bf16[192,3584]{1,0:T(8,128)(2,1)S(1)}, u32[]{:S(2)}, u32[]{:S(2)}) collective-permute-start(bf16[192,3584]{1,0:T(8,128)(2,1)} %s.5), channel_id=1, source_target_pairs={{0,4},{1,5},{4,8},{5,9},{6,2},{7,3},{8,12},{9,13},{10,6},{11,7},{1... | collective-permute-start | bytes 4128776 | tf_op jit(solution)/shard_map/ppermute | solution.py:20
  10.1 1.3 %copy-done.2 = bf16[192,3584]{1,0:T(8,128)(2,1)S(1)} copy-done((bf16[192,3584]{1,0:T(8,128)(2,1)S(1)}, bf16[192,3584]{1,0:T(8,128)(2,1)}, u32[]{:S(2)}) %copy-start.2) | copy-done | bytes 1376280
  11.4 4.4 %own_part.1 = (f32[192,3584]{1,0:T(8,128)S(1)}, f32[192,128]{1,0:T(8,128)S(1)}) custom-call(bf16[192,3584]{1,0:T(8,128)(2,1)S(1)} %copy-done.2, bf16[192,3584]{1,0:T(8,128)(2,1)} %refs_0_.1, bf16[192,3584]{1,0:T(8,128)(2,1)S(1)} %collective-permute-done.3.s_mate, bf16[192,3584]{1,0:T(8,128)(2,1)S(1)} %collective-permute-done.4.t_mate.refs_1_), custom_call_target="tpu_custom_call" | custom-call | flops 1585446912 | bytes 8355840 | tf_op jit(solution)/shard_map/own_part/pallas_call | solution.py:69
  15.8 1.5 %copy-done = f32[192,3584]{1,0:T(8,128)} copy-done((f32[192,3584]{1,0:T(8,128)}, f32[192,3584]{1,0:T(8,128)S(1)}, u32[]{:S(2)}) %copy-start) | copy-done | bytes 2752536
  17.4 1.3 %collective-permute-start.5 = (bf16[192,3584]{1,0:T(8,128)(2,1)}, bf16[192,3584]{1,0:T(8,128)(2,1)S(1)}, u32[]{:S(2)}, u32[]{:S(2)}) collective-permute-start(bf16[192,3584]{1,0:T(8,128)(2,1)} %refs_0_.1), channel_id=1, source_target_pairs={{2,6},{3,7},{4,0},{5,1},{6,10},{7,11},{8,4},{9,5},{10,14},{11,15},... | collective-permute-start | bytes 4128776 | tf_op jit(solution)/shard_map/ppermute | solution.py:20
  18.6 16.8 %collective-permute-done.x.sx = bf16[192,3584]{1,0:T(8,128)(2,1)} collective-permute-done((bf16[192,3584]{1,0:T(8,128)(2,1)}, bf16[192,3584]{1,0:T(8,128)(2,1)}, u32[]{:S(2)}, u32[]{:S(2)}) %collective-permute-start) | collective-permute-done | bytes 1376288 | tf_op jit(solution)/shard_map/ppermute | solution.py:20
  35.4 4.0 %collective-permute-done.1.a = bf16[192,3584]{1,0:T(8,128)(2,1)S(1)} collective-permute-done((bf16[192,3584]{1,0:T(8,128)(2,1)}, bf16[192,3584]{1,0:T(8,128)(2,1)S(1)}, u32[]{:S(2)}, u32[]{:S(2)}) %collective-permute-start.1) | collective-permute-done | bytes 1376288 | tf_op jit(solution)/shard_map/ppermute | solution.py:20
  39.4 5.4 %collective-permute-start.2 = (bf16[192,3584]{1,0:T(8,128)(2,1)}, bf16[192,3584]{1,0:T(8,128)(2,1)}, u32[]{:S(2)}, u32[]{:S(2)}) collective-permute-start(bf16[192,3584]{1,0:T(8,128)(2,1)} %collective-permute-done.x.sx), channel_id=1, source_target_pairs={{0,4},{1,5},{4,8},{5,9},{6,2},{7,3},{8,12},{9,13},{10,6},{11,7},{1... | collective-permute-start | bytes 4128776 | tf_op jit(solution)/shard_map/ppermute | solution.py:20
  44.8 3.4 %student_grams.1 = (f32[192,384]{1,0:T(8,128)S(1)}, f32[192,576]{1,0:T(8,128)S(1)}) custom-call(bf16[192,3584]{1,0:T(8,128)(2,1)S(1)} %copy-done.3, bf16[192,3584]{1,0:T(8,128)(2,1)S(1)} %collective-permute-done.3.s_mate, bf16[192,3584]{1,0:T(8,128)(2,1)} %collective-permute-done.x.sx, bf16[192,3584]{1,0:T(8,128)(2,1)S(1)} %collective-permute-done.7.f.sf), custom_call_target="tpu_custom_call" | custom-call | flops 1321205760 | bytes 6242304 | tf_op jit(solution)/shard_map/student_grams/pallas_call | solution.py:69
  48.2 0.7 copy-done.9
  48.9 15.5 %collective-permute-done.6.refs_2_ = bf16[192,3584]{1,0:T(8,128)(2,1)} collective-permute-done((bf16[192,3584]{1,0:T(8,128)(2,1)}, bf16[192,3584]{1,0:T(8,128)(2,1)}, u32[]{:S(2)}, u32[]{:S(2)}) %collective-permute-start.6) | collective-permute-done | bytes 1376288 | tf_op jit(solution)/shard_map/ppermute | solution.py:20
  64.9 1.3 %copy-done.8 = bf16[192,3584]{1,0:T(8,128)(2,1)S(1)} copy-done((bf16[192,3584]{1,0:T(8,128)(2,1)S(1)}, bf16[192,3584]{1,0:T(8,128)(2,1)}, u32[]{:S(2)}) %copy-start.8) | copy-done | bytes 1376280
  66.2 1.8 %stage.2.three = bf16[576,3584]{1,0:T(8,128)(2,1)S(1)} custom-call(bf16[192,3584]{1,0:T(8,128)(2,1)} %refs_0_.1, bf16[192,3584]{1,0:T(8,128)(2,1)S(1)} %copy-done.8, bf16[192,3584]{1,0:T(8,128)(2,1)} %collective-permute-done.6.refs_2_), custom_call_target="tpu_custom_call" | custom-call | tf_op jit(solution)/shard_map/stage/pallas_call | solution.py:69
  68.1 1.7 %send_direct.1 = (bf16[192,768]{1,0:T(8,128)(2,1)S(1)}, bf16[192,192]{1,0:T(8,128)(2,1)S(1)}) custom-call(bf16[192,3584]{1,0:T(8,128)(2,1)S(1)} %collective-permute-done.5.f.tf, bf16[576,3584]{1,0:T(8,128)(2,1)S(1)} %stage.2.three, f32[192,576]{1,0:T(8,128)S(1)} %get-tuple-element.25.student, f32[1,576]{1,0:T(1,128)S(1)} %and_select_fusion.factors), custom_call_target="tpu_custom_call" | custom-call | flops 792723456 | bytes 6318336 | tf_op jit(solution)/shard_map/send_direct/pallas_call | solution.py:69
  69.8 2.5 %collective-permute-done.2.far = bf16[192,3584]{1,0:T(8,128)(2,1)} collective-permute-done((bf16[192,3584]{1,0:T(8,128)(2,1)}, bf16[192,3584]{1,0:T(8,128)(2,1)}, u32[]{:S(2)}, u32[]{:S(2)}) %collective-permute-start.2) | collective-permute-done | bytes 1376288 | tf_op jit(solution)/shard_map/ppermute | solution.py:20
  72.3 1.8 %stage.3.mates = bf16[384,3584]{1,0:T(8,128)(2,1)S(1)} custom-call(bf16[192,3584]{1,0:T(8,128)(2,1)} %collective-permute-done.9.refs_0_, bf16[192,3584]{1,0:T(8,128)(2,1)} %collective-permute-done.10.refs_1_), custom_call_target="tpu_custom_call" | custom-call | tf_op jit(solution)/shard_map/stage/pallas_call | solution.py:69
  74.1 1.0 %send_diag.1 = bf16[192,768]{1,0:T(8,128)(2,1)S(1)} custom-call(bf16[192,768]{1,0:T(8,128)(2,1)S(1)} %get-tuple-element.28.direct, bf16[384,3584]{1,0:T(8,128)(2,1)S(1)} %stage.3.mates, bf16[192,3584]{1,0:T(8,128)(2,1)S(1)} %collective-permute-done.7.f.sf, bf16[192,3584]{1,0:T(8,128)(2,1)S(1)} %collective-permute-done.5.f.tf), custom_call_target="tpu_custom_call" | custom-call | flops 528482304 | bytes 6094848 | tf_op jit(solution)/shard_map/send_diag/pallas_call | solution.py:69
  75.8 4.5 %collective-permute-start.11 = (bf16[192,768]{1,0:T(8,128)(2,1)S(1)}, bf16[192,768]{1,0:T(8,128)(2,1)S(1)}, u32[]{:S(2)}, u32[]{:S(2)}) collective-permute-start(bf16[192,768]{1,0:T(8,128)(2,1)S(1)} %send_diag.1), channel_id=1, source_target_pairs={{0,4},{1,5},{4,8},{5,9},{6,2},{7,3},{8,12},{9,13},{10,6},{11,7},{1... | collective-permute-start | bytes 884744 | tf_op jit(solution)/shard_map/ppermute | solution.py:20
  80.3 4.4 %near_part.1 = (f32[192,3584]{1,0:T(8,128)S(1)}, f32[192,128]{1,0:T(8,128)S(1)}, bf16[192,3584]{1,0:T(8,128)(2,1)S(1)}) custom-call(bf16[192,3584]{1,0:T(8,128)(2,1)S(1)} %copy-done.4, bf16[576,3584]{1,0:T(8,128)(2,1)S(1)} %stage.2.three, bf16[384,3584]{1,0:T(8,128)(2,1)S(1)} %stage.3.mates, ...), custom_call_target="tpu_custom_call", output_to_operand_aliasing={{0}: (9, {}), {1}: (10, {})} | custom-call | flops 2113929216 | bytes 22585344 | tf_op jit(solution)/shard_map/near_part/pallas_call | solution.py:69
  84.8 2.2 %collective-permute-done.11.gap_b = bf16[192,768]{1,0:T(8,128)(2,1)S(1)} collective-permute-done((bf16[192,768]{1,0:T(8,128)(2,1)S(1)}, bf16[192,768]{1,0:T(8,128)(2,1)S(1)}, u32[]{:S(2)}, u32[]{:S(2)}) %collective-permute-start.11) | collective-permute-done | bytes 294944 | tf_op jit(solution)/shard_map/ppermute | solution.py:20
  87.0 2.3 %last_part.1 = (bf16[192,3584]{1,0:T(8,128)(2,1)}, f32[1,192]{1,0:T(1,128)}) custom-call(bf16[192,768]{1,0:T(8,128)(2,1)S(1)} %collective-permute-done.11.gap_b, bf16[192,3584]{1,0:T(8,128)(2,1)S(1)} %copy-done.6, bf16[192,3584]{1,0:T(8,128)(2,1)S(1)} %collective-permute-done.12.b, bf16[192,3584]{1,0:T(8,128)(2,1)S(1)} %get-tuple-element.36.c, ...), custom_call_target="tpu_custom_call" | custom-call | flops 1056964608 | bytes 10027776 | tf_op jit(solution)/shard_map/last_part/pallas_call | solution.py:69
  (37 shorter events, 1.4 us)
Async XLA Ops:
  0.6 9.5 %collective-permute-start.3 = (bf16[192,3584]{1,0:T(8,128)(2,1)}, bf16[192,3584]{1,0:T(8,128)(2,1)S(1)}, u32[]{:S(2)}, u32[]{:S(2)}) collective-permute-start(bf16[192,3584]{1,0:T(8,128)(2,1)} %s.5), channel_id=1, source_target_pairs={{0,1},{1,0},{2,3},{3,2},{4,5},{5,4},{6,7},{7,6},{8,9},{9,8},{10,11... | collective-permute-start | bytes 4128776 | tf_op jit(solution)/shard_map/ppermute | solution.py:20
  1.1 8.9 %collective-permute-start.4 = (bf16[192,3584]{1,0:T(8,128)(2,1)}, bf16[192,3584]{1,0:T(8,128)(2,1)S(1)}, u32[]{:S(2)}, u32[]{:S(2)}) collective-permute-start(bf16[192,3584]{1,0:T(8,128)(2,1)} %refs_0_.1), channel_id=1, source_target_pairs={{0,1},{1,0},{2,3},{3,2},{4,5},{5,4},{6,7},{7,6},{8,9},{9,8},{10,11... | collective-permute-start | bytes 4128776 | tf_op jit(solution)/shard_map/ppermute | solution.py:20
  1.2 34.2 %collective-permute-start = (bf16[192,3584]{1,0:T(8,128)(2,1)}, bf16[192,3584]{1,0:T(8,128)(2,1)}, u32[]{:S(2)}, u32[]{:S(2)}) collective-permute-start(bf16[192,3584]{1,0:T(8,128)(2,1)} %s.5), channel_id=1, source_target_pairs={{0,2},{1,3},{2,0},{3,1},{4,6},{5,7},{6,4},{7,5},{8,10},{9,11},{10,... | collective-permute-start | bytes 4128776 | tf_op jit(solution)/shard_map/ppermute | solution.py:20
  4.1 40.7 %collective-permute-start.7 = (bf16[192,3584]{1,0:T(8,128)(2,1)}, bf16[192,3584]{1,0:T(8,128)(2,1)S(1)}, u32[]{:S(2)}, u32[]{:S(2)}) collective-permute-start(bf16[192,3584]{1,0:T(8,128)(2,1)} %s.5), channel_id=1, source_target_pairs={{2,6},{3,7},{4,0},{5,1},{6,10},{7,11},{8,4},{9,5},{10,14},{11,15},... | collective-permute-start | bytes 4128776 | tf_op jit(solution)/shard_map/ppermute | solution.py:20
  5.4 34.0 %collective-permute-start.1 = (bf16[192,3584]{1,0:T(8,128)(2,1)}, bf16[192,3584]{1,0:T(8,128)(2,1)S(1)}, u32[]{:S(2)}, u32[]{:S(2)}) collective-permute-start(bf16[192,3584]{1,0:T(8,128)(2,1)} %s.5), channel_id=1, source_target_pairs={{0,4},{1,5},{4,8},{5,9},{6,2},{7,3},{8,12},{9,13},{10,6},{11,7},{1... | collective-permute-start | bytes 4128776 | tf_op jit(solution)/shard_map/ppermute | solution.py:20
  10.1 1.3 %copy-start.2 = (bf16[192,3584]{1,0:T(8,128)(2,1)S(1)}, bf16[192,3584]{1,0:T(8,128)(2,1)}, u32[]{:S(2)}) copy-start(bf16[192,3584]{1,0:T(8,128)(2,1)} %s.5) | copy-start | bytes 4128772
  11.4 4.4 %copy-start.7 = (bf16[192,3584]{1,0:T(8,128)(2,1)}, bf16[192,3584]{1,0:T(8,128)(2,1)S(1)}, u32[]{:S(2)}) copy-start(bf16[192,3584]{1,0:T(8,128)(2,1)S(1)} %collective-permute-done.4.t_mate.refs_1_) | copy-start | bytes 4128772
  11.4 33.4 %copy-start.3 = (bf16[192,3584]{1,0:T(8,128)(2,1)S(1)}, bf16[192,3584]{1,0:T(8,128)(2,1)}, u32[]{:S(2)}) copy-start(bf16[192,3584]{1,0:T(8,128)(2,1)} %s.5) | copy-start | bytes 4128772
  15.8 1.5 %copy-start = (f32[192,3584]{1,0:T(8,128)}, f32[192,3584]{1,0:T(8,128)S(1)}, u32[]{:S(2)}) copy-start(f32[192,3584]{1,0:T(8,128)S(1)} %get-tuple-element.35.grad_in) | copy-start | bytes 8257540
  17.4 47.0 %collective-permute-start.6 = (bf16[192,3584]{1,0:T(8,128)(2,1)}, bf16[192,3584]{1,0:T(8,128)(2,1)}, u32[]{:S(2)}, u32[]{:S(2)}) collective-permute-start(bf16[192,3584]{1,0:T(8,128)(2,1)} %refs_0_.1), channel_id=1, source_target_pairs={{0,2},{1,3},{2,0},{3,1},{4,6},{5,7},{6,4},{7,5},{8,10},{9,11},{10,... | collective-permute-start | bytes 4128776 | tf_op jit(solution)/shard_map/ppermute | solution.py:20
  17.4 50.7 %collective-permute-start.5 = (bf16[192,3584]{1,0:T(8,128)(2,1)}, bf16[192,3584]{1,0:T(8,128)(2,1)S(1)}, u32[]{:S(2)}, u32[]{:S(2)}) collective-permute-start(bf16[192,3584]{1,0:T(8,128)(2,1)} %refs_0_.1), channel_id=1, source_target_pairs={{2,6},{3,7},{4,0},{5,1},{6,10},{7,11},{8,4},{9,5},{10,14},{11,15},... | collective-permute-start | bytes 4128776 | tf_op jit(solution)/shard_map/ppermute | solution.py:20
  39.4 8.8 %copy-start.5 = (bf16[192,3584]{1,0:T(8,128)(2,1)}, bf16[192,3584]{1,0:T(8,128)(2,1)S(1)}, u32[]{:S(2)}) copy-start(bf16[192,3584]{1,0:T(8,128)(2,1)S(1)} %collective-permute-done.1.a) | copy-start | bytes 4128772
  39.4 32.9 %collective-permute-start.2 = (bf16[192,3584]{1,0:T(8,128)(2,1)}, bf16[192,3584]{1,0:T(8,128)(2,1)}, u32[]{:S(2)}, u32[]{:S(2)}) collective-permute-start(bf16[192,3584]{1,0:T(8,128)(2,1)} %collective-permute-done.x.sx), channel_id=1, source_target_pairs={{0,4},{1,5},{4,8},{5,9},{6,2},{7,3},{8,12},{9,13},{10,6},{11,7},{1... | collective-permute-start | bytes 4128776 | tf_op jit(solution)/shard_map/ppermute | solution.py:20
  64.4 7.9 %collective-permute-start.9 = (bf16[192,3584]{1,0:T(8,128)(2,1)}, bf16[192,3584]{1,0:T(8,128)(2,1)}, u32[]{:S(2)}, u32[]{:S(2)}) collective-permute-start(bf16[192,3584]{1,0:T(8,128)(2,1)} %collective-permute-done.x.sx), channel_id=1, source_target_pairs={{0,1},{1,0},{2,3},{3,2},{4,5},{5,4},{6,7},{7,6},{8,9},{9,8},{10,11... | collective-permute-start | bytes 4128776 | tf_op jit(solution)/shard_map/ppermute | solution.py:20
  64.4 7.9 %collective-permute-start.10 = (bf16[192,3584]{1,0:T(8,128)(2,1)}, bf16[192,3584]{1,0:T(8,128)(2,1)}, u32[]{:S(2)}, u32[]{:S(2)}) collective-permute-start(bf16[192,3584]{1,0:T(8,128)(2,1)} %collective-permute-done.6.refs_2_), channel_id=1, source_target_pairs={{0,1},{1,0},{2,3},{3,2},{4,5},{5,4},{6,7},{7,6},{8,9},{9,8},{10,11... | collective-permute-start | bytes 4128776 | tf_op jit(solution)/shard_map/ppermute | solution.py:20
  69.8 2.5 %collective-permute-start.8 = (bf16[192,192]{1,0:T(8,128)(2,1)S(1)}, bf16[192,192]{1,0:T(8,128)(2,1)S(1)}, u32[]{:S(2)}, u32[]{:S(2)}) collective-permute-start(bf16[192,192]{1,0:T(8,128)(2,1)S(1)} %get-tuple-element.27), channel_id=1, source_target_pairs={{0,1},{1,0},{2,3},{3,2},{4,5},{5,4},{6,7},{7,6},{8,9},{9,8},{10,11... | collective-permute-start | bytes 221192 | tf_op jit(solution)/shard_map/ppermute | solution.py:20
  74.1 1.6 %copy-start.6 = (bf16[192,3584]{1,0:T(8,128)(2,1)S(1)}, bf16[192,3584]{1,0:T(8,128)(2,1)}, u32[]{:S(2)}) copy-start(bf16[192,3584]{1,0:T(8,128)(2,1)} %copy-done.5) | copy-start | bytes 4128772
  74.1 6.2 %copy-start.1 = (f32[192,3584]{1,0:T(8,128)S(1)}, f32[192,3584]{1,0:T(8,128)}, u32[]{:S(2)}) copy-start(f32[192,3584]{1,0:T(8,128)} %copy-done) | copy-start | bytes 8257540
  74.1 6.2 %copy-start.4 = (bf16[192,3584]{1,0:T(8,128)(2,1)S(1)}, bf16[192,3584]{1,0:T(8,128)(2,1)}, u32[]{:S(2)}) copy-start(bf16[192,3584]{1,0:T(8,128)(2,1)} %s.5) | copy-start | bytes 4128772
  74.1 6.2 %copy-start.10 = (f32[192,384]{1,0:T(8,128)S(1)}, f32[192,384]{1,0:T(8,128)}, u32[]{:S(2)}) copy-start(f32[192,384]{1,0:T(8,128)} %copy-done.9) | copy-start | bytes 884740
  75.1 5.2 %collective-permute-start.13 = (bf16[192,3584]{1,0:T(8,128)(2,1)S(1)}, bf16[192,3584]{1,0:T(8,128)(2,1)S(1)}, u32[]{:S(2)}, u32[]{:S(2)}) collective-permute-start(bf16[192,3584]{1,0:T(8,128)(2,1)S(1)} %collective-permute-done.7.f.sf), channel_id=1, source_target_pairs={{0,1},{1,0},{2,3},{3,2},{4,5},{5,4},{6,7},{7,6},{8,9},{9,8},{10,11... | collective-permute-start | bytes 4128776 | tf_op jit(solution)/shard_map/ppermute | solution.py:20
  75.2 11.8 %collective-permute-start.14 = (bf16[192,3584]{1,0:T(8,128)(2,1)}, bf16[192,3584]{1,0:T(8,128)(2,1)S(1)}, u32[]{:S(2)}, u32[]{:S(2)}) collective-permute-start(bf16[192,3584]{1,0:T(8,128)(2,1)} %collective-permute-done.2.far), channel_id=1, source_target_pairs={{0,1},{1,0},{2,3},{3,2},{4,5},{5,4},{6,7},{7,6},{8,9},{9,8},{10,11... | collective-permute-start | bytes 4128776 | tf_op jit(solution)/shard_map/ppermute | solution.py:20
  75.7 11.3 %collective-permute-start.12 = (bf16[192,3584]{1,0:T(8,128)(2,1)S(1)}, bf16[192,3584]{1,0:T(8,128)(2,1)S(1)}, u32[]{:S(2)}, u32[]{:S(2)}) collective-permute-start(bf16[192,3584]{1,0:T(8,128)(2,1)S(1)} %copy-done.6), channel_id=1, source_target_pairs={{0,1},{1,0},{2,3},{3,2},{4,5},{5,4},{6,7},{7,6},{8,9},{9,8},{10,11... | collective-permute-start | bytes 4128776 | tf_op jit(solution)/shard_map/ppermute | solution.py:20
  75.8 11.2 %collective-permute-start.11 = (bf16[192,768]{1,0:T(8,128)(2,1)S(1)}, bf16[192,768]{1,0:T(8,128)(2,1)S(1)}, u32[]{:S(2)}, u32[]{:S(2)}) collective-permute-start(bf16[192,768]{1,0:T(8,128)(2,1)S(1)} %send_diag.1), channel_id=1, source_target_pairs={{0,4},{1,5},{4,8},{5,9},{6,2},{7,3},{8,12},{9,13},{10,6},{11,7},{1... | collective-permute-start | bytes 884744 | tf_op jit(solution)/shard_map/ppermute | solution.py:20
  (2 other events, 2.1 us)

commit v6 on v5

--- a/solution.py
+++ b/solution.py
@@ -167,8 +167,9 @@
     )[0]
 
 
-def send_direct_kernel(f, three, student, factors, out, cross):
+def send_direct_kernel(f, three, student, factors, out, cross, near):
     rows = f.shape[0]
+    near[...] = f[...]
     g = ((student[...] - gram(f[...], three[...])) * factors[...]).astype(jnp.bfloat16)
     out[:, : 3 * rows] = g
     cross[...] = g[:, rows : 2 * rows]
@@ -179,26 +180,26 @@
     return call(
         send_direct_kernel,
         (f, three, student, factors),
-        [jax.ShapeDtypeStruct((rows, 4 * rows), jnp.bfloat16), jax.ShapeDtypeStruct((rows, rows), jnp.bfloat16)],
+        [jax.ShapeDtypeStruct((rows, n), jnp.bfloat16) for n in (4 * rows, rows, width)],
         [],
         6 * rows * rows * width,
         "send_direct",
     )
 
 
-def send_diag_kernel(scale, direct, mates, f, tf, out):
-    rows = f.shape[0]
-    x_mate, tx_mate = mates.at[:rows], mates.at[rows:]
+def send_diag_kernel(scale, direct, mates, tf, out):
+    rows = tf.shape[0]
+    x_mate, tx_mate, f = mates.at[:rows], mates.at[rows : 2 * rows], mates.at[2 * rows :]
     out[:, : 3 * rows] = direct[:, : 3 * rows]
     g = gram(f[...], x_mate[...]) - gram(tf[...], tx_mate[...])
     out[:, 3 * rows :] = (g * scale).astype(jnp.bfloat16)
 
 
-def send_diag(direct, mates, f, tf, scale):
-    rows, width = f.shape
+def send_diag(direct, mates, tf, scale):
+    rows, width = tf.shape
     return call(
         functools.partial(send_diag_kernel, scale),
-        (direct, mates, f, tf),
+        (direct, mates, tf),
         [jax.ShapeDtypeStruct((rows, 4 * rows), jnp.bfloat16)],
         [],
         4 * rows * rows * width,
@@ -207,14 +208,14 @@
 
 
 def near_kernel(
-    scale, s, three, mates, tf, student, cross, sx, sf, sf_mate, grad_in, sums_in, far,
+    scale, s, three, mates, tf, student, cross, sx, sf_mate, grad_in, sums_in, far,
     grad, sums, near, gap_b, sem
 ):
     rows = s.shape[0]
-    copy = pltpu.make_async_copy(far, near, sem)
+    copy = pltpu.make_async_copy(far.at[:, : s.shape[1]], near, sem)
     copy.start()
     t, tx = three.at[:rows], three.at[2 * rows :]
-    sx_mate, tx_mate = mates.at[:rows], mates.at[rows:]
+    sx_mate, tx_mate, sf = mates.at[:rows], mates.at[rows : 2 * rows], mates.at[2 * rows :]
     blocks = (
         student[:, :rows] - gram(t[...], tx[...]),
         gram(s[...], sx_mate[...]) - gram(t[...], tx_mate[...]),
@@ -233,11 +234,11 @@
     copy.wait()
 
 
-def near_part(s, three, mates, tf, student, cross, sx, sf, sf_mate, grad_in, sums_in, far, scale):
+def near_part(s, three, mates, tf, student, cross, sx, sf_mate, grad_in, sums_in, far, scale):
     rows, width = s.shape
     return call(
         functools.partial(near_kernel, scale),
-        (s, three, mates, tf, student, cross, sx, sf, sf_mate, grad_in, sums_in, far),
+        (s, three, mates, tf, student, cross, sx, sf_mate, grad_in, sums_in, far),
         [
             jax.ShapeDtypeStruct((rows, width), jnp.float32),
             jax.ShapeDtypeStruct((rows, LANES), jnp.float32),
@@ -246,8 +247,8 @@
         [pltpu.VMEM((rows, 4 * rows), jnp.bfloat16), pltpu.SemaphoreType.DMA],
         16 * rows * rows * width,
         "near_part",
-        {9: 0, 10: 1},
-        streamed=(11,),
+        {8: 0, 9: 1},
+        streamed=(10,),
     )
 
 
@@ -291,23 +292,23 @@
     t_next = after(teacher, sums)
     t_side = move(t_next, partner)
     t_far = move(t_next, heavy)
-    s_diag = move(after(s_side, s_back), light)
+    s_diag = move(after(jnp.pad(s_side, ((0, 0), (0, LANES))), s_back), light)
     mine, out = student_grams(student, s_mate, s_side, s_far)
 
     s_side_mate = move(after(s_side, out, t_side), swap)
     t_side_mate = move(after(t_side, out), swap)
     three = stage(teacher, t_mate, t_side)
-    direct, cross = send_direct(t_far, three, out, factors)
+    direct, cross, t_far = send_direct(t_far, three, out, factors)
     cross_mate = move(cross, swap)
-    mates = stage(s_side_mate, t_side_mate)
-    _, direct, cross_mate = lax.optimization_barrier((s_diag, direct, cross_mate))
-    out_gap = send_diag(direct, mates, s_far, t_far, scale)
+    mates = stage(s_side_mate, t_side_mate, s_far)
+    _, mates, cross_mate = lax.optimization_barrier((s_diag, mates, cross_mate))
+    out_gap = send_diag(direct, mates, t_far, scale)
     s_far_mate = move(after(s_far, out_gap), swap)
     s_diag_mate = move(after(s_diag, out_gap), swap)
     s_back_mate = move(after(s_back, out_gap), swap)
     in_gap = move(out_gap, light)
     grad, sums, s_diag = near_part(
-        student, three, mates, t_far, mine, cross_mate, s_side, s_far, s_far_mate, grad, sums,
+        student, three, mates, t_far, mine, cross_mate, s_side, s_far_mate, grad, sums,
         s_diag, scale,
     )
     grad, sums = last_part(in_gap, s_back, s_back_mate, s_diag, s_diag_mate, grad, sums, 1.0 / math.sqrt(window), 1.0 / window)

time: 89.8 us -> 89 us (level)
  waiting for transfers between devices: 40.9 us -> 39 us
  local copies, waits for them, and re-layouts: 4.94 us -> 6.18 us
    ppermute x15, waiting for transfers between devices: 40.9 us -> 39 us  [move(): return lax.ppermute(block, AXIS, route)]
    pad x0 -> x1, local copies, waits for them, and re-layouts: none -> 1.25 us  [body(): s_diag = move(after(jnp.pad(s_side, ((0, 0), (0, LANES))), s_back), light)]
  transfers between devices with their start and end apart: 15 -> 15, of which waited for: 5 -> 5; matrix products, arithmetic and copies ran while one was open for 0% -> 1% of each run, Pallas kernels for 18% -> 19%
where the time goes in v6:
time: 89 us; the launch traced here: 88.6 us
  waiting for transfers between devices  39 us (44%)
  starting transfers between devices  22 us (25%)
  Pallas kernels  20.5 us (23%)
  local copies, waits for them, and re-layouts  6.18 us (7%)
    ppermute x15, waiting for transfers between devices, move(): return lax.ppermute(block, AXIS, route)  39 us
    ppermute x15, starting transfers between devices, move(): return lax.ppermute(block, AXIS, route)  22 us
    pallas_call x8, Pallas kernels, call(): pl.pallas_call(kernel, in_specs=[far if j in streamed else spec for j in...  20.5 us
    unnamed x22, local copies, waits for them, and re-layouts  4.93 us
  transfers between devices with their start and end apart: 15, of which 5 were waited for; matrix products, arithmetic and copies ran while one was open for 1% of the time, Pallas kernels for 19%

profile of v6, /device:TPU:0, one launch (start us, length us, event | category | flops | bytes accessed | tf_op | source)
XLA Modules:
  0.0 88.6 jit_solution(15772706729098220968)
XLA Ops:
  0.6 0.5 collective-permute-start
  1.2 2.9 %collective-permute-start.4 = (bf16[192,3584]{1,0:T(8,128)(2,1)}, bf16[192,3584]{1,0:T(8,128)(2,1)S(1)}, u32[]{:S(2)}, u32[]{:S(2)}) collective-permute-start(bf16[192,3584]{1,0:T(8,128)(2,1)} %s.5), channel_id=1, source_target_pairs={{0,2},{1,3},{2,0},{3,1},{4,6},{5,7},{6,4},{7,5},{8,10},{9,11},{10,... | collective-permute-start | bytes 4128776 | tf_op jit(solution)/shard_map/ppermute | solution.py:20
  4.1 1.3 %collective-permute-start.5 = (bf16[192,3584]{1,0:T(8,128)(2,1)}, bf16[192,3584]{1,0:T(8,128)(2,1)S(1)}, u32[]{:S(2)}, u32[]{:S(2)}) collective-permute-start(bf16[192,3584]{1,0:T(8,128)(2,1)} %s.5), channel_id=1, source_target_pairs={{2,6},{3,7},{4,0},{5,1},{6,10},{7,11},{8,4},{9,5},{10,14},{11,15},... | collective-permute-start | bytes 4128776 | tf_op jit(solution)/shard_map/ppermute | solution.py:20
  5.4 4.6 %collective-permute-start.6 = (bf16[192,3584]{1,0:T(8,128)(2,1)}, bf16[192,3584]{1,0:T(8,128)(2,1)S(1)}, u32[]{:S(2)}, u32[]{:S(2)}) collective-permute-start(bf16[192,3584]{1,0:T(8,128)(2,1)} %s.5), channel_id=1, source_target_pairs={{0,4},{1,5},{4,8},{5,9},{6,2},{7,3},{8,12},{9,13},{10,6},{11,7},{1... | collective-permute-start | bytes 4128776 | tf_op jit(solution)/shard_map/ppermute | solution.py:20
  10.1 1.3 %copy-done.2 = bf16[192,3584]{1,0:T(8,128)(2,1)S(1)} copy-done((bf16[192,3584]{1,0:T(8,128)(2,1)S(1)}, bf16[192,3584]{1,0:T(8,128)(2,1)}, u32[]{:S(2)}) %copy-start.2) | copy-done | bytes 1376280
  11.4 4.3 %own_part.1 = (f32[192,3584]{1,0:T(8,128)S(1)}, f32[192,128]{1,0:T(8,128)S(1)}) custom-call(bf16[192,3584]{1,0:T(8,128)(2,1)S(1)} %copy-done.2, bf16[192,3584]{1,0:T(8,128)(2,1)} %refs_0_.1, bf16[192,3584]{1,0:T(8,128)(2,1)S(1)} %collective-permute-done.s_mate, bf16[192,3584]{1,0:T(8,128)(2,1)S(1)} %collective-permute-done.1.t_mate.refs_1_), custom_call_target="tpu_custom_call" | custom-call | flops 1585446912 | bytes 8355840 | tf_op jit(solution)/shard_map/own_part/pallas_call | solution.py:69
  15.8 1.5 %copy-done = f32[192,3584]{1,0:T(8,128)} copy-done((f32[192,3584]{1,0:T(8,128)}, f32[192,3584]{1,0:T(8,128)S(1)}, u32[]{:S(2)}) %copy-start) | copy-done | bytes 2752536
  17.3 1.4 %collective-permute-start.2 = (bf16[192,3584]{1,0:T(8,128)(2,1)}, bf16[192,3584]{1,0:T(8,128)(2,1)}, u32[]{:S(2)}, u32[]{:S(2)}) collective-permute-start(bf16[192,3584]{1,0:T(8,128)(2,1)} %refs_0_.1), channel_id=1, source_target_pairs={{2,6},{3,7},{4,0},{5,1},{6,10},{7,11},{8,4},{9,5},{10,14},{11,15},... | collective-permute-start | bytes 4128776 | tf_op jit(solution)/shard_map/ppermute | solution.py:20
  18.8 16.6 %collective-permute-done.4.x.sx = bf16[192,3584]{1,0:T(8,128)(2,1)S(1)} collective-permute-done((bf16[192,3584]{1,0:T(8,128)(2,1)}, bf16[192,3584]{1,0:T(8,128)(2,1)S(1)}, u32[]{:S(2)}, u32[]{:S(2)}) %collective-permute-start.4) | collective-permute-done | bytes 1376288 | tf_op jit(solution)/shard_map/ppermute | solution.py:20
  35.3 1.3 %pad.4 = bf16[192,3712]{1,0:T(8,128)(2,1)} pad(bf16[192,3584]{1,0:T(8,128)(2,1)S(1)} %collective-permute-done.4.x.sx, bf16[]{:T(256)} %constant.41.clone.1), padding=0_0x0_128 | pad | bytes 2801666 | tf_op jit(solution)/shard_map/jit(_pad)/pad | solution.py:295
  36.6 2.8 %collective-permute-done.6.a = bf16[192,3584]{1,0:T(8,128)(2,1)S(1)} collective-permute-done((bf16[192,3584]{1,0:T(8,128)(2,1)}, bf16[192,3584]{1,0:T(8,128)(2,1)S(1)}, u32[]{:S(2)}, u32[]{:S(2)}) %collective-permute-start.6) | collective-permute-done | bytes 1376288 | tf_op jit(solution)/shard_map/ppermute | solution.py:20
  39.4 5.4 %collective-permute-start.7 = (bf16[192,3712]{1,0:T(8,128)(2,1)}, bf16[192,3712]{1,0:T(8,128)(2,1)}, u32[]{:S(2)}, u32[]{:S(2)}) collective-permute-start(bf16[192,3712]{1,0:T(8,128)(2,1)} %pad.4), channel_id=1, source_target_pairs={{0,4},{1,5},{4,8},{5,9},{6,2},{7,3},{8,12},{9,13},{10,6},{11,7},{1... | collective-permute-start | bytes 4276232 | tf_op jit(solution)/shard_map/ppermute | solution.py:20
  44.8 2.0 %student_grams.1 = (f32[192,384]{1,0:T(8,128)S(1)}, f32[192,576]{1,0:T(8,128)S(1)}) custom-call(bf16[192,3584]{1,0:T(8,128)(2,1)S(1)} %copy-done.3, bf16[192,3584]{1,0:T(8,128)(2,1)S(1)} %collective-permute-done.s_mate, bf16[192,3584]{1,0:T(8,128)(2,1)S(1)} %collective-permute-done.4.x.sx, bf16[192,3584]{1,0:T(8,128)(2,1)S(1)} %collective-permute-done.5.f.refs_2_), custom_call_target="tpu_custom_call" | custom-call | flops 1321205760 | bytes 6242304 | tf_op jit(solution)/shard_map/student_grams/pallas_call | solution.py:69
  46.9 0.7 copy-done.9
  47.6 16.8 %collective-permute-done.3.refs_2_ = bf16[192,3584]{1,0:T(8,128)(2,1)} collective-permute-done((bf16[192,3584]{1,0:T(8,128)(2,1)}, bf16[192,3584]{1,0:T(8,128)(2,1)}, u32[]{:S(2)}, u32[]{:S(2)}) %collective-permute-start.3) | collective-permute-done | bytes 1376288 | tf_op jit(solution)/shard_map/ppermute | solution.py:20
  64.9 1.3 %copy-done.8 = bf16[192,3584]{1,0:T(8,128)(2,1)S(1)} copy-done((bf16[192,3584]{1,0:T(8,128)(2,1)S(1)}, bf16[192,3584]{1,0:T(8,128)(2,1)}, u32[]{:S(2)}) %copy-start.8) | copy-done | bytes 1376280
  66.2 1.8 %stage.2.three = bf16[576,3584]{1,0:T(8,128)(2,1)S(1)} custom-call(bf16[192,3584]{1,0:T(8,128)(2,1)} %refs_0_.1, bf16[192,3584]{1,0:T(8,128)(2,1)S(1)} %copy-done.8, bf16[192,3584]{1,0:T(8,128)(2,1)} %collective-permute-done.3.refs_2_), custom_call_target="tpu_custom_call" | custom-call | tf_op jit(solution)/shard_map/stage/pallas_call | solution.py:69
  68.1 3.1 %send_direct.1 = (bf16[192,768]{1,0:T(8,128)(2,1)S(1)}, bf16[192,192]{1,0:T(8,128)(2,1)S(1)}, bf16[192,3584]{1,0:T(8,128)(2,1)S(1)}) custom-call(bf16[192,3584]{1,0:T(8,128)(2,1)} %collective-permute-done.2.f, bf16[576,3584]{1,0:T(8,128)(2,1)S(1)} %stage.2.three, f32[192,576]{1,0:T(8,128)S(1)} %get-tuple-element.25.student, f32[1,576]{1,0:T(1,128)S(1)} %and_select_fusion.factors), custom_call_target="tpu_custom_call" | custom-call | flops 792723456 | bytes 7694592 | tf_op jit(solution)/shard_map/send_direct/pallas_call | solution.py:69
  71.3 1.8 %stage.3.mates = bf16[576,3584]{1,0:T(8,128)(2,1)S(1)} custom-call(bf16[192,3584]{1,0:T(8,128)(2,1)} %collective-permute-done.8.refs_0_, bf16[192,3584]{1,0:T(8,128)(2,1)} %collective-permute-done.9.refs_1_, bf16[192,3584]{1,0:T(8,128)(2,1)S(1)} %collective-permute-done.5.f.refs_2_), custom_call_target="tpu_custom_call" | custom-call | tf_op jit(solution)/shard_map/stage/pallas_call | solution.py:69
  73.4 1.0 %send_diag.1 = bf16[192,768]{1,0:T(8,128)(2,1)S(1)} custom-call(bf16[192,768]{1,0:T(8,128)(2,1)S(1)} %get-tuple-element.26.direct, bf16[576,3584]{1,0:T(8,128)(2,1)S(1)} %stage.3.mates, bf16[192,3584]{1,0:T(8,128)(2,1)S(1)} %get-tuple-element.32.tf), custom_call_target="tpu_custom_call" | custom-call | flops 528482304 | bytes 6094848 | tf_op jit(solution)/shard_map/send_diag/pallas_call | solution.py:69
  75.2 4.4 %collective-permute-start.11 = (bf16[192,768]{1,0:T(8,128)(2,1)S(1)}, bf16[192,768]{1,0:T(8,128)(2,1)S(1)}, u32[]{:S(2)}, u32[]{:S(2)}) collective-permute-start(bf16[192,768]{1,0:T(8,128)(2,1)S(1)} %send_diag.1), channel_id=1, source_target_pairs={{0,4},{1,5},{4,8},{5,9},{6,2},{7,3},{8,12},{9,13},{10,6},{11,7},{1... | collective-permute-start | bytes 884744 | tf_op jit(solution)/shard_map/ppermute | solution.py:20
  79.6 4.2 %near_part.1 = (f32[192,3584]{1,0:T(8,128)S(1)}, f32[192,128]{1,0:T(8,128)S(1)}, bf16[192,3584]{1,0:T(8,128)(2,1)S(1)}) custom-call(bf16[192,3584]{1,0:T(8,128)(2,1)S(1)} %copy-done.4, bf16[576,3584]{1,0:T(8,128)(2,1)S(1)} %stage.2.three, bf16[576,3584]{1,0:T(8,128)(2,1)S(1)} %stage.3.mates, ...), custom_call_target="tpu_custom_call", output_to_operand_aliasing={{0}: (8, {}), {1}: (9, {})} | custom-call | flops 2113929216 | bytes 22634496 | tf_op jit(solution)/shard_map/near_part/pallas_call | solution.py:69
  83.8 2.5 %collective-permute-done.11.gap_b = bf16[192,768]{1,0:T(8,128)(2,1)S(1)} collective-permute-done((bf16[192,768]{1,0:T(8,128)(2,1)S(1)}, bf16[192,768]{1,0:T(8,128)(2,1)S(1)}, u32[]{:S(2)}, u32[]{:S(2)}) %collective-permute-start.11) | collective-permute-done | bytes 294944 | tf_op jit(solution)/shard_map/ppermute | solution.py:20
  86.2 2.3 %last_part.1 = (bf16[192,3584]{1,0:T(8,128)(2,1)}, f32[1,192]{1,0:T(1,128)}) custom-call(bf16[192,768]{1,0:T(8,128)(2,1)S(1)} %collective-permute-done.11.gap_b, bf16[192,3584]{1,0:T(8,128)(2,1)S(1)} %copy-done.6, bf16[192,3584]{1,0:T(8,128)(2,1)S(1)} %collective-permute-done.12.b, bf16[192,3584]{1,0:T(8,128)(2,1)S(1)} %get-tuple-element.38.c, ...), custom_call_target="tpu_custom_call" | custom-call | flops 1056964608 | bytes 10076928 | tf_op jit(solution)/shard_map/last_part/pallas_call | solution.py:69
  (38 shorter events, 1.8 us)
Async XLA Ops:
  0.6 9.5 %collective-permute-start = (bf16[192,3584]{1,0:T(8,128)(2,1)}, bf16[192,3584]{1,0:T(8,128)(2,1)S(1)}, u32[]{:S(2)}, u32[]{:S(2)}) collective-permute-start(bf16[192,3584]{1,0:T(8,128)(2,1)} %s.5), channel_id=1, source_target_pairs={{0,1},{1,0},{2,3},{3,2},{4,5},{5,4},{6,7},{7,6},{8,9},{9,8},{10,11... | collective-permute-start | bytes 4128776 | tf_op jit(solution)/shard_map/ppermute | solution.py:20
  1.1 8.9 %collective-permute-start.1 = (bf16[192,3584]{1,0:T(8,128)(2,1)}, bf16[192,3584]{1,0:T(8,128)(2,1)S(1)}, u32[]{:S(2)}, u32[]{:S(2)}) collective-permute-start(bf16[192,3584]{1,0:T(8,128)(2,1)} %refs_0_.1), channel_id=1, source_target_pairs={{0,1},{1,0},{2,3},{3,2},{4,5},{5,4},{6,7},{7,6},{8,9},{9,8},{10,11... | collective-permute-start | bytes 4128776 | tf_op jit(solution)/shard_map/ppermute | solution.py:20
  1.2 34.1 %collective-permute-start.4 = (bf16[192,3584]{1,0:T(8,128)(2,1)}, bf16[192,3584]{1,0:T(8,128)(2,1)S(1)}, u32[]{:S(2)}, u32[]{:S(2)}) collective-permute-start(bf16[192,3584]{1,0:T(8,128)(2,1)} %s.5), channel_id=1, source_target_pairs={{0,2},{1,3},{2,0},{3,1},{4,6},{5,7},{6,4},{7,5},{8,10},{9,11},{10,... | collective-permute-start | bytes 4128776 | tf_op jit(solution)/shard_map/ppermute | solution.py:20
  4.1 40.7 %collective-permute-start.5 = (bf16[192,3584]{1,0:T(8,128)(2,1)}, bf16[192,3584]{1,0:T(8,128)(2,1)S(1)}, u32[]{:S(2)}, u32[]{:S(2)}) collective-permute-start(bf16[192,3584]{1,0:T(8,128)(2,1)} %s.5), channel_id=1, source_target_pairs={{2,6},{3,7},{4,0},{5,1},{6,10},{7,11},{8,4},{9,5},{10,14},{11,15},... | collective-permute-start | bytes 4128776 | tf_op jit(solution)/shard_map/ppermute | solution.py:20
  5.4 34.0 %collective-permute-start.6 = (bf16[192,3584]{1,0:T(8,128)(2,1)}, bf16[192,3584]{1,0:T(8,128)(2,1)S(1)}, u32[]{:S(2)}, u32[]{:S(2)}) collective-permute-start(bf16[192,3584]{1,0:T(8,128)(2,1)} %s.5), channel_id=1, source_target_pairs={{0,4},{1,5},{4,8},{5,9},{6,2},{7,3},{8,12},{9,13},{10,6},{11,7},{1... | collective-permute-start | bytes 4128776 | tf_op jit(solution)/shard_map/ppermute | solution.py:20
  10.1 1.3 %copy-start.2 = (bf16[192,3584]{1,0:T(8,128)(2,1)S(1)}, bf16[192,3584]{1,0:T(8,128)(2,1)}, u32[]{:S(2)}) copy-start(bf16[192,3584]{1,0:T(8,128)(2,1)} %s.5) | copy-start | bytes 4128772
  11.4 4.3 %copy-start.7 = (bf16[192,3584]{1,0:T(8,128)(2,1)}, bf16[192,3584]{1,0:T(8,128)(2,1)S(1)}, u32[]{:S(2)}) copy-start(bf16[192,3584]{1,0:T(8,128)(2,1)S(1)} %collective-permute-done.1.t_mate.refs_1_) | copy-start | bytes 4128772
  15.8 1.5 %copy-start = (f32[192,3584]{1,0:T(8,128)}, f32[192,3584]{1,0:T(8,128)S(1)}, u32[]{:S(2)}) copy-start(f32[192,3584]{1,0:T(8,128)S(1)} %get-tuple-element.37.grad_in) | copy-start | bytes 8257540
  17.3 27.5 %copy-start.3 = (bf16[192,3584]{1,0:T(8,128)(2,1)S(1)}, bf16[192,3584]{1,0:T(8,128)(2,1)}, u32[]{:S(2)}) copy-start(bf16[192,3584]{1,0:T(8,128)(2,1)} %s.5) | copy-start | bytes 4128772
  17.3 47.0 %collective-permute-start.3 = (bf16[192,3584]{1,0:T(8,128)(2,1)}, bf16[192,3584]{1,0:T(8,128)(2,1)}, u32[]{:S(2)}, u32[]{:S(2)}) collective-permute-start(bf16[192,3584]{1,0:T(8,128)(2,1)} %refs_0_.1), channel_id=1, source_target_pairs={{0,2},{1,3},{2,0},{3,1},{4,6},{5,7},{6,4},{7,5},{8,10},{9,11},{10,... | collective-permute-start | bytes 4128776 | tf_op jit(solution)/shard_map/ppermute | solution.py:20
  17.3 50.7 %collective-permute-start.2 = (bf16[192,3584]{1,0:T(8,128)(2,1)}, bf16[192,3584]{1,0:T(8,128)(2,1)}, u32[]{:S(2)}, u32[]{:S(2)}) collective-permute-start(bf16[192,3584]{1,0:T(8,128)(2,1)} %refs_0_.1), channel_id=1, source_target_pairs={{2,6},{3,7},{4,0},{5,1},{6,10},{7,11},{8,4},{9,5},{10,14},{11,15},... | collective-permute-start | bytes 4128776 | tf_op jit(solution)/shard_map/ppermute | solution.py:20
  39.4 7.4 %copy-start.5 = (bf16[192,3584]{1,0:T(8,128)(2,1)}, bf16[192,3584]{1,0:T(8,128)(2,1)S(1)}, u32[]{:S(2)}) copy-start(bf16[192,3584]{1,0:T(8,128)(2,1)S(1)} %collective-permute-done.6.a) | copy-start | bytes 4128772
  39.4 33.9 %collective-permute-start.7 = (bf16[192,3712]{1,0:T(8,128)(2,1)}, bf16[192,3712]{1,0:T(8,128)(2,1)}, u32[]{:S(2)}, u32[]{:S(2)}) collective-permute-start(bf16[192,3712]{1,0:T(8,128)(2,1)} %pad.4), channel_id=1, source_target_pairs={{0,4},{1,5},{4,8},{5,9},{6,2},{7,3},{8,12},{9,13},{10,6},{11,7},{1... | collective-permute-start | bytes 4276232 | tf_op jit(solution)/shard_map/ppermute | solution.py:20
  64.4 6.9 %collective-permute-start.8 = (bf16[192,3584]{1,0:T(8,128)(2,1)S(1)}, bf16[192,3584]{1,0:T(8,128)(2,1)}, u32[]{:S(2)}, u32[]{:S(2)}) collective-permute-start(bf16[192,3584]{1,0:T(8,128)(2,1)S(1)} %collective-permute-done.4.x.sx), channel_id=1, source_target_pairs={{0,1},{1,0},{2,3},{3,2},{4,5},{5,4},{6,7},{7,6},{8,9},{9,8},{10,11... | collective-permute-start | bytes 4128776 | tf_op jit(solution)/shard_map/ppermute | solution.py:20
  64.4 6.9 %collective-permute-start.9 = (bf16[192,3584]{1,0:T(8,128)(2,1)}, bf16[192,3584]{1,0:T(8,128)(2,1)}, u32[]{:S(2)}, u32[]{:S(2)}) collective-permute-start(bf16[192,3584]{1,0:T(8,128)(2,1)} %collective-permute-done.3.refs_2_), channel_id=1, source_target_pairs={{0,1},{1,0},{2,3},{3,2},{4,5},{5,4},{6,7},{7,6},{8,9},{9,8},{10,11... | collective-permute-start | bytes 4128776 | tf_op jit(solution)/shard_map/ppermute | solution.py:20
  71.2 2.2 %collective-permute-start.10 = (bf16[192,192]{1,0:T(8,128)(2,1)S(1)}, bf16[192,192]{1,0:T(8,128)(2,1)S(1)}, u32[]{:S(2)}, u32[]{:S(2)}) collective-permute-start(bf16[192,192]{1,0:T(8,128)(2,1)S(1)} %get-tuple-element.30), channel_id=1, source_target_pairs={{0,1},{1,0},{2,3},{3,2},{4,5},{5,4},{6,7},{7,6},{8,9},{9,8},{10,11... | collective-permute-start | bytes 221192 | tf_op jit(solution)/shard_map/ppermute | solution.py:20
  73.4 1.6 %copy-start.6 = (bf16[192,3584]{1,0:T(8,128)(2,1)S(1)}, bf16[192,3584]{1,0:T(8,128)(2,1)}, u32[]{:S(2)}) copy-start(bf16[192,3584]{1,0:T(8,128)(2,1)} %copy-done.5) | copy-start | bytes 4128772
  73.4 6.2 %copy-start.1 = (f32[192,3584]{1,0:T(8,128)S(1)}, f32[192,3584]{1,0:T(8,128)}, u32[]{:S(2)}) copy-start(f32[192,3584]{1,0:T(8,128)} %copy-done) | copy-start | bytes 8257540
  73.4 6.2 %copy-start.4 = (bf16[192,3584]{1,0:T(8,128)(2,1)S(1)}, bf16[192,3584]{1,0:T(8,128)(2,1)}, u32[]{:S(2)}) copy-start(bf16[192,3584]{1,0:T(8,128)(2,1)} %s.5) | copy-start | bytes 4128772
  73.4 6.2 %copy-start.10 = (f32[192,384]{1,0:T(8,128)S(1)}, f32[192,384]{1,0:T(8,128)}, u32[]{:S(2)}) copy-start(f32[192,384]{1,0:T(8,128)} %copy-done.9) | copy-start | bytes 884740
  74.3 5.2 %collective-permute-start.13 = (bf16[192,3584]{1,0:T(8,128)(2,1)S(1)}, bf16[192,3584]{1,0:T(8,128)(2,1)S(1)}, u32[]{:S(2)}, u32[]{:S(2)}) collective-permute-start(bf16[192,3584]{1,0:T(8,128)(2,1)S(1)} %collective-permute-done.5.f.refs_2_), channel_id=1, source_target_pairs={{0,1},{1,0},{2,3},{3,2},{4,5},{5,4},{6,7},{7,6},{8,9},{9,8},{10,11... | collective-permute-start | bytes 4128776 | tf_op jit(solution)/shard_map/ppermute | solution.py:20
  74.7 11.6 %collective-permute-start.14 = (bf16[192,3712]{1,0:T(8,128)(2,1)}, bf16[192,3712]{1,0:T(8,128)(2,1)S(1)}, u32[]{:S(2)}, u32[]{:S(2)}) collective-permute-start(bf16[192,3712]{1,0:T(8,128)(2,1)} %collective-permute-done.7.far), channel_id=1, source_target_pairs={{0,1},{1,0},{2,3},{3,2},{4,5},{5,4},{6,7},{7,6},{8,9},{9,8},{10,11... | collective-permute-start | bytes 4276232 | tf_op jit(solution)/shard_map/ppermute | solution.py:20
  74.9 11.3 %collective-permute-start.12 = (bf16[192,3584]{1,0:T(8,128)(2,1)S(1)}, bf16[192,3584]{1,0:T(8,128)(2,1)S(1)}, u32[]{:S(2)}, u32[]{:S(2)}) collective-permute-start(bf16[192,3584]{1,0:T(8,128)(2,1)S(1)} %copy-done.6), channel_id=1, source_target_pairs={{0,1},{1,0},{2,3},{3,2},{4,5},{5,4},{6,7},{7,6},{8,9},{9,8},{10,11... | collective-permute-start | bytes 4128776 | tf_op jit(solution)/shard_map/ppermute | solution.py:20
  75.2 11.1 %collective-permute-start.11 = (bf16[192,768]{1,0:T(8,128)(2,1)S(1)}, bf16[192,768]{1,0:T(8,128)(2,1)S(1)}, u32[]{:S(2)}, u32[]{:S(2)}) collective-permute-start(bf16[192,768]{1,0:T(8,128)(2,1)S(1)} %send_diag.1), channel_id=1, source_target_pairs={{0,4},{1,5},{4,8},{5,9},{6,2},{7,3},{8,12},{9,13},{10,6},{11,7},{1... | collective-permute-start | bytes 884744 | tf_op jit(solution)/shard_map/ppermute | solution.py:20
  (2 other events, 2.1 us)
